TPU v7x, 32 devices: a whole 2x2x4 slice. The times are simulated.
32 devices in a mesh: sx: 8 (over z, core), sy: 4 (over y, x).
Axes of the slice: x: 2, y: 2, z: 4, core: 2. Of those that a mesh axis runs over, the one named last changes fastest.
Arguments:
- right_sides: float32 [256, 32, 128], P(('sx', 'sy')), may hold values from -16 to 16
- tiles: bfloat16 [256, 7, 128, 128], P(('sx', 'sy')), may hold values from -1 to 1
- tile_cols: int32 [256, 6], P(('sx', 'sy')), may hold values from 0 to 15
- send_rows: int32 [128, 2], P(('sx', 'sy')), may hold values from 0 to 7
- block_inverse: bfloat16 [256, 128, 128], P(('sx', 'sy')), may hold values from -1 to 1
- coarse_basis: bfloat16 [256, 32, 128], P(('sx', 'sy')), may hold values from -0.1875 to 0.1875
- coarse_inverse: float32 [1024, 1024], P(('sx', 'sy')), may hold values from -4 to 4, as said below
Outputs:
- solution: float32 [256, 32, 128], P(('sx', 'sy'))
- residual: float32 [256, 32, 128], P(('sx', 'sy'))
Inputs may be any that keep to these rules, and one draw needn't show every extreme that they name: coarse_inverse is symmetric: entry (i, j) equals entry (j, i).
All inputs are finite; a program needn't handle non-finite values.
Results may differ from a plain program's by a relative error of at most 0.012.
Values may be sent and summed in bfloat16 or wider, within the bound.
No kernel may reach another device: no remote copies, remote signals or barrier semaphores. Data moves between devices by JAX's collectives and lax.ppermute only.
A program may use at most 64 MiB of HBM per device.

v0:
```python
import jax
import jax.numpy as jnp
from jax import lax
from jax.sharding import PartitionSpec as P


def shifted(value, axis, steps):
    count = lax.axis_size(axis)
    initial, last = (max(0, -steps), min(count, count - steps))
    return lax.ppermute(value, axis, [(source, source + steps) for source in range(initial, last)])


def apply_operator(packed, tiles, tile_cols, send_rows):
    outgoing = packed[send_rows]
    from_below = shifted(outgoing[0], "sx", 1)
    from_above = shifted(outgoing[1], "sx", -1)
    from_left = shifted(outgoing[2], "sy", 1)
    from_right = shifted(outgoing[3], "sy", -1)
    extended = jnp.concatenate([packed, from_below, from_above, from_left, from_right], axis=0)
    picked = extended[tile_cols]
    stacked = jnp.concatenate([packed[:, None], picked], axis=1)
    return jnp.einsum("btik,btrk->bri", tiles, stacked, preferred_element_type=jnp.float32)


def restrict(vector, coarse_basis):
    return jnp.einsum(
        "bki,bri->kr", coarse_basis.astype(jnp.float32), vector, precision=lax.Precision.HIGHEST
    )


def coarse_solve(restricted, coarse_inverse):
    width = restricted.shape[0]
    count_rhs = restricted.shape[1]
    flat = restricted.reshape(1, width * count_rhs)
    piece = lax.all_gather(flat, ("sx", "sy"), axis=0, tiled=True)
    count = piece.shape[0]
    return jnp.dot(
        coarse_inverse, piece.reshape(count * width, count_rhs), precision=lax.Precision.HIGHEST
    )


def precondition(vector, coarse, block_inverse, coarse_basis):
    local = jnp.einsum(
        "bik,brk->bri",
        block_inverse,
        vector.astype(jnp.bfloat16),
        preferred_element_type=jnp.float32,
    )
    spread = jnp.einsum(
        "bki,kr->bri", coarse_basis, coarse.astype(jnp.bfloat16), preferred_element_type=jnp.float32
    )
    return local + spread


def step_weight(residual, image):
    upper, lower = lax.psum(
        (jnp.sum(residual * image, axis=(0, 2)), jnp.sum(image * image, axis=(0, 2))), ("sx", "sy")
    )
    return upper / (lower + 1e-06)


def body(right_sides, tiles, tile_cols, send_rows, block_inverse, coarse_basis, coarse_inverse):
    residual = right_sides
    coarse_now = coarse_solve(restrict(residual, coarse_basis), coarse_inverse)
    update = precondition(residual, coarse_now, block_inverse, coarse_basis)
    image = apply_operator(update.astype(jnp.bfloat16), tiles, tile_cols, send_rows)
    weight = step_weight(residual, image)
    solution = weight[None, :, None] * update
    residual = residual - weight[None, :, None] * image
    coarse_next = coarse_solve(restrict(residual, coarse_basis), coarse_inverse)
    update = precondition(residual, coarse_next, block_inverse, coarse_basis)
    image = apply_operator(update.astype(jnp.bfloat16), tiles, tile_cols, send_rows)
    weight = step_weight(residual, image)
    solution = solution + weight[None, :, None] * update
    residual = residual - weight[None, :, None] * image
    return (solution, residual)


def solution(mesh):
    placed = (
        P(("sx", "sy"), None, None),
        P(("sx", "sy"), None, None, None),
        P(("sx", "sy"), None),
        P(("sx", "sy"), None),
        P(("sx", "sy"), None, None),
        P(("sx", "sy"), None, None),
        P(("sx", "sy"), None),
    )
    return jax.shard_map(
        body,
        mesh=mesh,
        in_specs=placed,
        out_specs=(P(("sx", "sy"), None, None), P(("sx", "sy"), None, None)),
        check_vma=False,
    )
```

profile of v0, /device:TPU:0, one launch (start us, length us, event | category | flops | bytes accessed | tf_op | source)
XLA Modules:
  0.0 248.0 jit_solution(15811371420190779251)
XLA Ops:
  0.7 0.8 compare_select_fusion.1
  1.7 1.1 convolution_bitcast_fusion.5
  2.9 70.5 %all-gather = f32[32,1,1024]{2,1,0:T(1,128)S(1)} all-gather(f32[1,1,1024]{2,1,0:T(1,128)S(1)} %reshape.78), channel_id=1, replica_groups=mesh['sx'=8,'sy'=4] {'sx','sy'}, dimensions={0}, use_global_device_ids=true | all-gather | bytes 135168 | tf_op jit(solution)/shard_map/all_gather | solution.py:35
  73.4 0.3 reduce
  73.7 0.2 reshape.19
  73.9 1.9 fusion
  75.9 0.2 constant_dynamic-update-slice_fusion.4
  76.2 0.6 gather_fusion
  76.8 1.3 collective-permute-start.3
  78.1 4.5 %collective-permute-start.2 = (bf16[2,32,128]{2,1,0:T(8,128)(2,1)S(1)}, bf16[2,32,128]{2,1,0:T(8,128)(2,1)S(1)}, u32[]{:S(2)}, u32[]{:S(2)}) collective-permute-start(bf16[2,32,128]{2,1,0:T(8,128)(2,1)S(1)} %get-tuple-element.19), channel_id=1, source_target_pairs={{0,1},{1,2},{2,3},{4,5},{5,6},{6,7},{8,9},{9,10},{10,11},{12,13},{... | collective-permute-start | bytes 49160 | tf_op jit(solution)/shard_map/ppermute | solution.py:10
  82.6 1.3 collective-permute-start.1
  83.9 3.0 %collective-permute-start = (bf16[2,32,128]{2,1,0:T(8,128)(2,1)S(1)}, bf16[2,32,128]{2,1,0:T(8,128)(2,1)S(1)}, u32[]{:S(2)}, u32[]{:S(2)}) collective-permute-start(bf16[2,32,128]{2,1,0:T(8,128)(2,1)S(1)} %get-tuple-element.21), channel_id=1, source_target_pairs={{0,4},{4,8},{8,12},{12,16},{16,20},{20,24},{24,28},{1,5},{5,9},{9,... | collective-permute-start | bytes 49160 | tf_op jit(solution)/shard_map/ppermute | solution.py:10
  87.1 0.7 collective-permute-done
  87.8 0.6 gather_fusion.1
  88.5 0.8 multiply_reduce_fusion.2
  89.3 40.0 %all-reduce.1 = (f32[32]{0:T(128)S(1)}, f32[32]{0:T(128)S(1)}) all-reduce(f32[32]{0:T(128)S(1)} %get-tuple-element.5, f32[32]{0:T(128)S(1)} %get-tuple-element.4), channel_id=1, replica_groups=mesh['sx'=8,'sy'=4] {'sx','sy'}, use_global_device_ids=true, to_apply=%region_1.0 | all-reduce | flops 64 | bytes 512 | tf_op jit(solution)/shard_map/psum | solution.py:56
  129.4 0.2 convolution_bitcast_fusion.4
  129.7 66.4 %all-gather.1 = f32[32,1,1024]{2,1,0:T(1,128)S(1)} all-gather(f32[1,1,1024]{2,1,0:T(1,128)S(1)} %reshape.80), channel_id=1, replica_groups=mesh['sx'=8,'sy'=4] {'sx','sy'}, dimensions={0}, use_global_device_ids=true | all-gather | bytes 135168 | tf_op jit(solution)/shard_map/all_gather | solution.py:35
  196.1 0.3 reduce.1
  196.4 0.2 reshape.21
  196.6 1.0 fusion.1
  197.7 0.3 constant_dynamic-update-slice_fusion.9
  198.0 0.6 gather_fusion.2
  198.6 1.3 collective-permute-start.4
  199.9 1.3 collective-permute-start.7
  201.2 4.5 %collective-permute-start.6 = (bf16[2,32,128]{2,1,0:T(8,128)(2,1)S(1)}, bf16[2,32,128]{2,1,0:T(8,128)(2,1)S(1)}, u32[]{:S(2)}, u32[]{:S(2)}) collective-permute-start(bf16[2,32,128]{2,1,0:T(8,128)(2,1)S(1)} %get-tuple-element.15), channel_id=1, source_target_pairs={{0,1},{1,2},{2,3},{4,5},{5,6},{6,7},{8,9},{9,10},{10,11},{12,13},{... | collective-permute-start | bytes 49160 | tf_op jit(solution)/shard_map/ppermute | solution.py:10
  205.7 1.3 collective-permute-start.5
  207.1 1.8 collective-permute-done.5
  208.8 0.6 gather_fusion.3
  209.5 0.8 multiply_reduce_fusion
  210.3 36.9 %all-reduce = (f32[32]{0:T(128)S(1)}, f32[32]{0:T(128)S(1)}) all-reduce(f32[32]{0:T(128)S(1)} %get-tuple-element.3, f32[32]{0:T(128)S(1)} %get-tuple-element.2), channel_id=1, replica_groups=mesh['sx'=8,'sy'=4] {'sx','sy'}, use_global_device_ids=true, to_apply=%region_5.0 | all-reduce | flops 64 | bytes 512 | tf_op jit(solution)/shard_map/psum | solution.py:56
  247.2 0.8 multiply_subtract_fusion
  (42 shorter events, 1.0 us)
Async XLA Ops:
  0.6 87.8 %copy-start = (bf16[8,7,128,128]{3,2,1,0:T(8,128)(2,1)S(1)}, bf16[8,7,128,128]{3,2,1,0:T(8,128)(2,1)}, u32[]{:S(2)}) copy-start(bf16[8,7,128,128]{3,2,1,0:T(8,128)(2,1)} %param.8) | copy-start | bytes 5505028
  0.6 75.1 %copy-start.3 = (bf16[8,32,128]{2,1,0:T(8,128)(2,1)S(1)}, bf16[8,32,128]{2,1,0:T(8,128)(2,1)}, u32[]{:S(2)}) copy-start(bf16[8,32,128]{2,1,0:T(8,128)(2,1)} %param.12) | copy-start | bytes 196612
  0.7 75.2 %copy-start.1 = (f32[8,32,128]{2,1,0:T(8,128)S(1)}, f32[8,32,128]{2,1,0:T(8,128)}, u32[]{:S(2)}) copy-start(f32[8,32,128]{2,1,0:T(8,128)} %param.7) | copy-start | bytes 393220
  0.7 75.2 %copy-start.2 = (bf16[8,128,128]{2,1,0:T(8,128)(2,1)S(1)}, bf16[8,128,128]{2,1,0:T(8,128)(2,1)}, u32[]{:S(2)}) copy-start(bf16[8,128,128]{2,1,0:T(8,128)(2,1)} %param.11) | copy-start | bytes 786436
  0.7 86.3 %copy-start.5 = (s32[8,6]{1,0:T(8,128)S(1)}, s32[8,6]{1,0:T(8,128)}, u32[]{:S(2)}) copy-start(s32[8,6]{1,0:T(8,128)} %param.9) | copy-start | bytes 580
  76.8 11.1 %collective-permute-start.3 = (bf16[2,32,128]{2,1,0:T(8,128)(2,1)S(1)}, bf16[2,32,128]{2,1,0:T(8,128)(2,1)S(1)}, u32[]{:S(2)}, u32[]{:S(2)}) collective-permute-start(bf16[2,32,128]{2,1,0:T(8,128)(2,1)S(1)} %get-tuple-element.18), channel_id=1, source_target_pairs={{1,0},{2,1},{3,2},{5,4},{6,5},{7,6},{9,8},{10,9},{11,10},{13,12},{... | collective-permute-start | bytes 49160 | tf_op jit(solution)/shard_map/ppermute | solution.py:10
  78.1 9.7 %collective-permute-start.2 = (bf16[2,32,128]{2,1,0:T(8,128)(2,1)S(1)}, bf16[2,32,128]{2,1,0:T(8,128)(2,1)S(1)}, u32[]{:S(2)}, u32[]{:S(2)}) collective-permute-start(bf16[2,32,128]{2,1,0:T(8,128)(2,1)S(1)} %get-tuple-element.19), channel_id=1, source_target_pairs={{0,1},{1,2},{2,3},{4,5},{5,6},{6,7},{8,9},{9,10},{10,11},{12,13},{... | collective-permute-start | bytes 49160 | tf_op jit(solution)/shard_map/ppermute | solution.py:10
  82.6 5.2 %collective-permute-start.1 = (bf16[2,32,128]{2,1,0:T(8,128)(2,1)S(1)}, bf16[2,32,128]{2,1,0:T(8,128)(2,1)S(1)}, u32[]{:S(2)}, u32[]{:S(2)}) collective-permute-start(bf16[2,32,128]{2,1,0:T(8,128)(2,1)S(1)} %get-tuple-element.20), channel_id=1, source_target_pairs={{4,0},{8,4},{12,8},{16,12},{20,16},{24,20},{28,24},{5,1},{9,5},{13... | collective-permute-start | bytes 49160 | tf_op jit(solution)/shard_map/ppermute | solution.py:10
  83.9 3.9 %collective-permute-start = (bf16[2,32,128]{2,1,0:T(8,128)(2,1)S(1)}, bf16[2,32,128]{2,1,0:T(8,128)(2,1)S(1)}, u32[]{:S(2)}, u32[]{:S(2)}) collective-permute-start(bf16[2,32,128]{2,1,0:T(8,128)(2,1)S(1)} %get-tuple-element.21), channel_id=1, source_target_pairs={{0,4},{4,8},{8,12},{12,16},{16,20},{20,24},{24,28},{1,5},{5,9},{9,... | collective-permute-start | bytes 49160 | tf_op jit(solution)/shard_map/ppermute | solution.py:10
  88.5 108.1 %copy-start.4 = (f32[32,1024]{1,0:T(8,128)S(1)}, f32[32,1024]{1,0:T(8,128)}, u32[]{:S(2)}) copy-start(f32[32,1024]{1,0:T(8,128)} %param.13) | copy-start | bytes 393220
  198.6 8.5 %collective-permute-start.4 = (bf16[2,32,128]{2,1,0:T(8,128)(2,1)S(1)}, bf16[2,32,128]{2,1,0:T(8,128)(2,1)S(1)}, u32[]{:S(2)}, u32[]{:S(2)}) collective-permute-start(bf16[2,32,128]{2,1,0:T(8,128)(2,1)S(1)} %get-tuple-element.17), channel_id=1, source_target_pairs={{0,4},{4,8},{8,12},{12,16},{16,20},{20,24},{24,28},{1,5},{5,9},{9,... | collective-permute-start | bytes 49160 | tf_op jit(solution)/shard_map/ppermute | solution.py:10
  199.9 9.0 %collective-permute-start.7 = (bf16[2,32,128]{2,1,0:T(8,128)(2,1)S(1)}, bf16[2,32,128]{2,1,0:T(8,128)(2,1)S(1)}, u32[]{:S(2)}, u32[]{:S(2)}) collective-permute-start(bf16[2,32,128]{2,1,0:T(8,128)(2,1)S(1)} %get-tuple-element.14), channel_id=1, source_target_pairs={{1,0},{2,1},{3,2},{5,4},{6,5},{7,6},{9,8},{10,9},{11,10},{13,12},{... | collective-permute-start | bytes 49160 | tf_op jit(solution)/shard_map/ppermute | solution.py:10
  201.2 7.6 %collective-permute-start.6 = (bf16[2,32,128]{2,1,0:T(8,128)(2,1)S(1)}, bf16[2,32,128]{2,1,0:T(8,128)(2,1)S(1)}, u32[]{:S(2)}, u32[]{:S(2)}) collective-permute-start(bf16[2,32,128]{2,1,0:T(8,128)(2,1)S(1)} %get-tuple-element.15), channel_id=1, source_target_pairs={{0,1},{1,2},{2,3},{4,5},{5,6},{6,7},{8,9},{9,10},{10,11},{12,13},{... | collective-permute-start | bytes 49160 | tf_op jit(solution)/shard_map/ppermute | solution.py:10
  205.7 3.1 %collective-permute-start.5 = (bf16[2,32,128]{2,1,0:T(8,128)(2,1)S(1)}, bf16[2,32,128]{2,1,0:T(8,128)(2,1)S(1)}, u32[]{:S(2)}, u32[]{:S(2)}) collective-permute-start(bf16[2,32,128]{2,1,0:T(8,128)(2,1)S(1)} %get-tuple-element.16), channel_id=1, source_target_pairs={{4,0},{8,4},{12,8},{16,12},{20,16},{24,20},{28,24},{5,1},{9,5},{13... | collective-permute-start | bytes 49160 | tf_op jit(solution)/shard_map/ppermute | solution.py:10
where the time goes:
time: 249 us; the launch traced here: 248 us
  blocking collectives  214 us (86%)
  starting transfers between devices  18.6 us (7%)
  matrix products  6.59 us (3%)
  local copies, waits for them, and re-layouts  3.39 us (1%)
    all_gather x2, blocking collectives, coarse_solve(): piece = lax.all_gather(flat, ('sx', 'sy'), axis=0, tiled=True)  137 us
    psum x2, blocking collectives, step_weight(): lax.psum((jnp.sum(residual * image, axis=(0, 2)), jnp.sum(image * image,...  76.8 us
    ppermute x8, starting transfers between devices, shifted(): lax.ppermute(value, axis, [(source, source + steps) for source in range(i...  18.6 us
  transfers between devices with their start and end apart: 8, of which 2 were waited for; matrix products, arithmetic and copies ran while one was open for 0% of the time, Pallas kernels for 0%

commit v1 on v0

v1 whole, which is shorter than its diff:
```python
import jax
import jax.numpy as jnp
from jax import lax
from jax.sharding import PartitionSpec as P

AXES = ("sx", "sy")
BF = jnp.bfloat16
F32 = jnp.float32


def swap(value, axis, odd):
    count = lax.axis_size(axis)
    pairs = []
    for place in range(count):
        step = 1 if (place % 2 == 0) != odd else -1
        pairs.append((place, (place + step) % count))
    return lax.ppermute(value, axis, pairs)


def swap_plan():
    plan = []
    for number, axis in enumerate(AXES):
        place, count = lax.axis_index(axis), lax.axis_size(axis)
        for odd in (False, True):
            up = (place % 2 == 0) != odd
            valid = jnp.where(up, place < count - 1, place > 0)
            plan.append((axis, odd, 2 * number + jnp.where(up, 0, 1), 2 * number + jnp.where(up, 1, 0), valid))
    return plan


def split(value):
    high = value.astype(BF)
    return high, (value - high.astype(F32)).astype(BF)


def local_part(vector, block_inverse):
    return sum(
        jnp.einsum("bik,brk->bri", block_inverse, part, preferred_element_type=F32) for part in split(vector)
    )


def restrict(vector, coarse_basis):
    high, low = split(vector)
    return sum(jnp.einsum("bki,bri->kr", coarse_basis, part, preferred_element_type=F32) for part in (high, low))


def spread(coarse, basis):
    return jnp.einsum("ski,skr->sri", basis, coarse.astype(BF), preferred_element_type=F32)


def gather(slot):
    count = lax.axis_size("sx") * lax.axis_size("sy")
    return lax.all_to_all(jnp.broadcast_to(slot[None], (count,) + slot.shape), AXES, 0, 0, tiled=True)


def image_of(packed, tiles, tile_cols):
    stacked = jnp.concatenate([packed[:8, None], packed[tile_cols]], axis=1)
    return jnp.einsum("btik,btrk->bri", tiles, stacked, preferred_element_type=F32)


def body(right_sides, tiles, tile_cols, send_rows, block_inverse, coarse_basis, coarse_inverse):
    blocks, rhs, order = right_sides.shape
    vectors = coarse_basis.shape[1]
    plan = swap_plan()

    def exchange(buffers):
        arrived = [swap(lax.dynamic_index_in_dim(buffers, send, 0, False), axis, odd) for axis, odd, send, _, _ in plan]
        arrived = [jnp.where(valid, value, 0) for value, (_, _, _, _, valid) in zip(arrived, plan)]
        up = [plan[0][3] == 1, plan[2][3] == 3]
        return [
            jnp.where(up[0], arrived[1], arrived[0]),
            jnp.where(up[0], arrived[0], arrived[1]),
            jnp.where(up[1], arrived[3], arrived[2]),
            jnp.where(up[1], arrived[2], arrived[3]),
        ]

    halo = send_rows.shape[1]
    inverse = coarse_inverse.astype(BF)
    local0 = local_part(right_sides, block_inverse)
    first = jnp.concatenate(
        [
            jnp.broadcast_to(inverse.reshape(1, -1, order), (4, inverse.size // order, order)),
            coarse_basis[send_rows].reshape(4, halo * vectors, order),
            local0.astype(BF)[send_rows].reshape(4, halo * rhs, order),
        ],
        axis=1,
    )
    slot = restrict(right_sides, coarse_basis).astype(BF).reshape(-1, order)
    restricted = gather(slot).reshape(-1, rhs)
    received = exchange(first)
    rows = inverse.size // order
    inverses = jnp.concatenate([inverse] + [value[:rows].reshape(inverse.shape) for value in received], axis=0)
    basis = jnp.concatenate(
        [coarse_basis] + [value[rows : rows + halo * vectors].reshape(halo, vectors, order) for value in received]
    )
    local0 = jnp.concatenate(
        [local0] + [value[rows + halo * vectors :].reshape(halo, rhs, order).astype(F32) for value in received]
    )

    def coarse_part(restricted):
        coarse = jnp.dot(inverses, restricted, preferred_element_type=F32).reshape(5, vectors, rhs)
        chosen = jnp.concatenate(
            [jnp.broadcast_to(coarse[0], (blocks, vectors, rhs)), jnp.repeat(coarse[1:], halo, axis=0)], axis=0
        )
        return spread(chosen, basis)

    update = local0 + coarse_part(restricted)
    image = image_of(update.astype(BF), tiles, tile_cols)

    sums = jnp.stack([jnp.sum(right_sides * image, axis=(0, 2)), jnp.sum(image * image, axis=(0, 2))])
    high, low = split(sums)
    slot = jnp.concatenate(
        [
            restrict(image, coarse_basis).astype(BF).reshape(-1, order),
            jnp.concatenate([high.reshape(1, -1), low.reshape(1, -1)], axis=1),
            jnp.zeros((7, order), BF),
        ]
    )
    arrived = gather(slot)
    local1 = local_part(image, block_inverse)
    received = exchange(local1.astype(BF)[send_rows].reshape(4, halo * rhs, order))
    restricted = arrived[:, :-8].reshape(-1, rhs)
    sums = jnp.sum(arrived[:, -8].astype(F32), axis=0).reshape(2, 2, rhs).sum(axis=0)
    weight = (sums[0] / (sums[1] + 1e-6))[None, :, None]
    local1 = jnp.concatenate([local1] + [value.reshape(halo, rhs, order).astype(F32) for value in received])
    second = update - weight * (local1 + coarse_part(restricted))
    residual = right_sides - weight * image
    image2 = image_of(second.astype(BF), tiles, tile_cols)
    sums = jnp.stack([jnp.sum(residual * image2, axis=(0, 2)), jnp.sum(image2 * image2, axis=(0, 2))])
    slot = jnp.concatenate([sums.reshape(1, -1), jnp.zeros((1, order - 2 * rhs), F32)], axis=1)
    sums = jnp.sum(gather(slot), axis=(0, 1))[: 2 * rhs].reshape(2, rhs)
    weight2 = (sums[0] / (sums[1] + 1e-6))[None, :, None]
    return weight * update[:blocks] + weight2 * second[:blocks], residual - weight2 * image2


def solution(mesh):
    block3 = P(AXES, None, None)
    placed = (block3, P(AXES, None, None, None), P(AXES, None), P(AXES, None), block3, block3, P(AXES, None))
    return jax.shard_map(body, mesh=mesh, in_specs=placed, out_specs=(block3, block3), check_vma=False)
```

time: 249 us -> 62.7 us (0.25)
  blocking collectives: 214 us -> 9.17 us
  waiting for transfers between devices: 2.48 us -> 11.4 us
  local copies, waits for them, and re-layouts: 3.39 us -> 8.93 us
  other arithmetic: 2.36 us -> 5.5 us
    all_gather x2 -> x0, blocking collectives: 137 us -> none  [coarse_solve(): piece = lax.all_gather(flat, ('sx', 'sy'), axis=0, tiled=True)]
    psum x2 -> x0, blocking collectives: 76.8 us -> none  [step_weight(): lax.psum((jnp.sum(residual * image, axis=(0, 2)), jnp.sum(image * image,...]
    all_to_all x0 -> x1, blocking collectives: none -> 9.17 us  [gather(): lax.all_to_all(jnp.broadcast_to(slot[None], (count,) + slot.shape), AXES,...]
    all_to_all x0 -> x2, waiting for transfers between devices: none -> 7.1 us  [gather(): lax.all_to_all(jnp.broadcast_to(slot[None], (count,) + slot.shape), AXES,...]
    ppermute x8, starting transfers between devices: 18.6 us -> 11.6 us  [swap(): return lax.ppermute(value, axis, pairs)]
    all_to_all x0 -> x2, starting transfers between devices: none -> 6.23 us  [gather(): lax.all_to_all(jnp.broadcast_to(slot[None], (count,) + slot.shape), AXES,...]
    dot_general x10 -> x14, matrix products: 6.59 us -> 8.24 us  [the longest x4 3.11 us: local_part(): jnp.einsum('bik,brk->bri', block_inverse, part, preferred_element_type=F32)]
  transfers between devices with their start and end apart: 8 -> 10, of which waited for: 2 -> 5; matrix products, arithmetic and copies ran while one was open for 0% -> 5% of each run, Pallas kernels for 0% -> 0%
where the time goes in v1:
time: 62.7 us; the launch traced here: 62.2 us
  starting transfers between devices  17.8 us (28%)
  waiting for transfers between devices  11.4 us (18%)
  blocking collectives  9.17 us (15%)
  local copies, waits for them, and re-layouts  8.93 us (14%)
  matrix products  8.24 us (13%)
  other arithmetic  5.5 us (9%)
  between operations  1.22 us (2%)
    ppermute x8, starting transfers between devices, swap(): return lax.ppermute(value, axis, pairs)  11.6 us
    all_to_all x1, blocking collectives, gather(): lax.all_to_all(jnp.broadcast_to(slot[None], (count,) + slot.shape), AXES,...  9.17 us
    all_to_all x2, waiting for transfers between devices, gather(): lax.all_to_all(jnp.broadcast_to(slot[None], (count,) + slot.shape), AXES,...  7.1 us
    all_to_all x2, starting transfers between devices, gather(): lax.all_to_all(jnp.broadcast_to(slot[None], (count,) + slot.shape), AXES,...  6.23 us
    ppermute x8, waiting for transfers between devices, swap(): return lax.ppermute(value, axis, pairs)  4.28 us
    dot_general x4, matrix products, local_part(): jnp.einsum('bik,brk->bri', block_inverse, part, preferred_element_type=F32)  3.11 us
    dot_general x2, matrix products, image_of(): jnp.einsum('btik,btrk->bri', tiles, stacked, preferred_element_type=F32)  3.06 us
    broadcast_in_dim x5, local copies, waits for them, and re-layouts, gather(): jnp.broadcast_to(slot[None], (count,) + slot.shape)  1.44 us
  transfers between devices with their start and end apart: 10, of which 5 were waited for; matrix products, arithmetic and copies ran while one was open for 5% of the time, Pallas kernels for 0%

profile of v1, /device:TPU:0, one launch (start us, length us, event | category | flops | bytes accessed | tf_op | source)
XLA Modules:
  0.0 62.2 jit_solution(7830465244923139306)
XLA Ops:
  0.7 0.8 %compare_select_fusion = s32[8,6]{1,0:T(8,128)S(1)} fusion(s32[8,6]{1,0:T(8,128)} %param.9), kind=kLoop, calls=%fused_computation.98 | loop fusion | flops 144 | bytes 384 | tf_op jit(solution)/shard_map/select_n | solution.py:57
  1.6 0.7 %compare_select_fusion.1 = s32[4,2]{0,1:T(2,128)S(1)} fusion(s32[4,2]{0,1:T(2,128)} %param.10), kind=kLoop, calls=%fused_computation.102 | loop fusion | flops 24 | bytes 64 | tf_op jit(solution)/shard_map/select_n | solution.py:83
  2.5 1.3 %fusion.30 = f32[8,32,128]{2,1,0:T(8,128)S(1)} fusion(bf16[8,128,128]{2,1,0:T(8,128)(2,1)} %param.11, f32[8,32,128]{2,1,0:T(8,128)} %param.7), kind=kOutput, calls=%fused_computation.118 | convolution fusion | flops 8421376 | bytes 524288 | tf_op jit(solution)/shard_map/bik,brk->bri/dot_general | solution.py:38
  3.7 1.3 %fusion.33 = (bf16[8,32,128]{2,1,0:T(8,128)(2,1)S(1)}, f32[16,32,128]{2,1,0:T(8,128)S(1)}) fusion(f32[8,32,128]{2,1,0:T(8,128)S(1)} %fusion.30, bf16[8,128,128]{2,1,0:T(8,128)(2,1)} %param.11, f32[8,32,128]{2,1,0:T(8,128)} %param.7), kind=kOutput, calls=%fused_computation.121 | convolution fusion | flops 8585215 | bytes 720896 | tf_op jit(solution)/shard_map/bik,brk->bri/dot_general | solution.py:38
  5.1 0.6 gather_fusion.1
  5.7 1.4 %gather_fusion = bf16[8,32,128]{2,1,0:T(8,128)(2,1)S(1)} fusion(bf16[8,32,128]{2,1,0:T(8,128)(2,1)} %param.12, s32[1024]{0:T(1024)S(1)} %get-tuple-element.47), kind=kCustom, calls=%fused_computation | custom fusion | bytes 131104 | tf_op jit(solution)/shard_map/gather | solution.py:83
  7.1 0.9 %constant_dynamic-update-slice_fusion.9 = (bf16[160,1024]{1,0:T(8,128)(2,1)S(1)}, bf16[32,1024]{1,0:T(8,128)(2,1)S(1)}) fusion(f32[32,1024]{1,0:T(8,128)} %param.13), kind=kLoop, calls=%fused_computation.69 | loop fusion | flops 32767 | bytes 262144
  8.1 0.7 %dynamic-slice_bitcast_fusion = (bf16[384,128]{1,0:T(8,128)(2,1)}, bf16[384,128]{1,0:T(8,128)(2,1)}, bf16[384,128]{1,0:T(8,128)(2,1)S(1)}, bf16[384,128]{1,0:T(8,128)(2,1)S(1)}) fusion(bf16[4,384,128]{2,1,0:T(8,128)(2,1)S(1)} %pad_maximum_fusion, s32[]{:T(128)S(6)} %select_n.191, s32[]{:T(128)S(6)} %select_n.186, s32[]{:T(128)S(6)} %select_n.176, ...), kind=kLoop, calls=%fused_computation.46 | loop fusion | bytes 786448 | tf_op jit(solution)/shard_map/jit(dynamic_index_in_dim)/squeeze | solution.py:67
  8.8 4.5 %collective-permute-start = (bf16[384,128]{1,0:T(8,128)(2,1)S(1)}, bf16[384,128]{1,0:T(8,128)(2,1)S(1)}, u32[]{:S(2)}, u32[]{:S(2)}) collective-permute-start(bf16[384,128]{1,0:T(8,128)(2,1)S(1)} %get-tuple-element.11), channel_id=1, source_target_pairs={{0,28},{4,8},{8,4},{12,16},{16,12},{20,24},{24,20},{28,0},{1,29},{... | collective-permute-start | bytes 294920 | tf_op jit(solution)/shard_map/ppermute | solution.py:17
  13.3 2.4 %collective-permute-start.2 = (bf16[384,128]{1,0:T(8,128)(2,1)}, bf16[384,128]{1,0:T(8,128)(2,1)S(1)}, u32[]{:S(2)}, u32[]{:S(2)}) collective-permute-start(bf16[384,128]{1,0:T(8,128)(2,1)} %get-tuple-element.9), channel_id=1, source_target_pairs={{0,3},{1,2},{2,1},{3,0},{4,7},{5,6},{6,5},{7,4},{8,11},{9,10},{10,... | collective-permute-start | bytes 294920 | tf_op jit(solution)/shard_map/ppermute | solution.py:17
  16.7 0.7 %broadcast_in_dim.80 = bf16[32,8,128]{2,1,0:T(8,128)(2,1)} broadcast(bf16[8,128]{1,0:T(8,128)(2,1)S(1)} %broadcast_in_dim.79), dimensions={1,2} | broadcast | bytes 67584 | tf_op jit(solution)/shard_map/broadcast_in_dim | solution.py:53
  17.4 2.6 %all-to-all-start = ((bf16[32,8,128]{2,1,0:T(8,128)(2,1)}), bf16[32,8,128]{2,1,0:T(8,128)(2,1)S(1)}, u32[]{:S(2)}, u32[]{:S(2)}) async-start(bf16[32,8,128]{2,1,0:T(8,128)(2,1)} %broadcast_in_dim.80), calls=%async_computation | async-start | bytes 131072 | tf_op jit(solution)/shard_map/all_to_all | solution.py:53
  20.0 0.6 pad.10.clone
  20.7 1.1 %collective-permute-done.3 = bf16[384,128]{1,0:T(8,128)(2,1)S(1)} collective-permute-done((bf16[384,128]{1,0:T(8,128)(2,1)}, bf16[384,128]{1,0:T(8,128)(2,1)S(1)}, u32[]{:S(2)}, u32[]{:S(2)}) %collective-permute-start.3) | collective-permute-done | bytes 98336 | tf_op jit(solution)/shard_map/ppermute | solution.py:17
  22.2 5.2 %all-to-all-done = bf16[32,8,128]{2,1,0:T(8,128)(2,1)S(1)} async-done(((bf16[32,8,128]{2,1,0:T(8,128)(2,1)}), bf16[32,8,128]{2,1,0:T(8,128)(2,1)S(1)}, u32[]{:S(2)}, u32[]{:S(2)}) %all-to-all-start) | async-done | bytes 65568 | tf_op jit(solution)/shard_map/all_to_all | solution.py:53
  28.2 0.6 %slice_bitcast_fusion.1 = bf16[8,1,32,128]{3,2,1,0:T(8,128)(2,1)} fusion(bf16[16,32,128]{2,1,0:T(8,128)(2,1)S(1)} %get-tuple-element.40), kind=kLoop, calls=%fused_computation.59 | loop fusion | bytes 131072 | tf_op jit(solution)/shard_map/broadcast_in_dim | solution.py:57
  28.9 0.6 %gather_fusion.2 = bf16[48,32,128]{2,1,0:T(8,128)(2,1)S(1)} fusion(bf16[16,32,128]{2,1,0:T(8,128)(2,1)S(1)} %get-tuple-element.40, s32[1024]{0:T(1024)S(1)} %get-tuple-element.46), kind=kCustom, calls=%fused_computation.2 | custom fusion | bytes 786624 | tf_op jit(solution)/shard_map/gather | solution.py:57
  29.5 2.2 %multiply_reduce_fusion.3 = (f32[32]{0:T(128)S(1)}, f32[32]{0:T(128)}, f32[8,32,128]{2,1,0:T(8,128)S(1)}) fusion(f32[8,32,128]{2,1,0:T(8,128)S(1)} %copy-done.1, bf16[8,7,128,128]{3,2,1,0:T(8,128)(2,1)S(1)} %copy-done, bf16[8,6,32,128]{3,2,1,0:T(8,128)(2,1)S(1)} %bitcast.108, bf16[8,1,32,128]{3,2,1,0:T(8,128)(2,1)} %slice_bitcast_fusion.1), kind=kOutput, calls=%fused_computation.43 | convolution fusion | flops 59080640 | bytes 2556160 | tf_op jit(solution)/shard_map/btik,btrk->bri/dot_general | solution.py:58
  32.4 0.7 %pad_maximum_fusion.1 = f32[2,32]{1,0:T(2,128)S(1)} fusion(f32[1,32]{1,0:T(1,128)} %bitcast.129, f32[1,32]{1,0:T(1,128)S(1)} %bitcast.128), kind=kLoop, calls=%fused_computation.103 | loop fusion | flops 64 | bytes 512 | tf_op jit(solution)/shard_map/stack | solution.py:110
  34.0 0.6 gather_fusion.3
  35.3 0.7 %maximum_maximum_fusion = bf16[16,128]{1,0:T(8,128)(2,1)S(1)} fusion(bf16[1,64]{1,0:T(2,128)(2,1)} %get-tuple-element.39, bf16[1,64]{1,0:T(2,128)(2,1)S(1)} %get-tuple-element.38, bf16[8,128]{1,0:T(8,128)(2,1)S(1)} %reshape.166, bf16[16]{0:T(256)(128)(2,1)} %pad.10.clone), kind=kLoop, calls=%fused_computation.101 | loop fusion | flops 16384 | bytes 6432 | tf_op jit(solution)/shard_map/concatenate | solution.py:112
  36.1 0.7 %broadcast_in_dim.86 = bf16[32,16,128]{2,1,0:T(8,128)(2,1)} broadcast(bf16[16,128]{1,0:T(8,128)(2,1)S(1)} %maximum_maximum_fusion), dimensions={1,2} | broadcast | bytes 135168 | tf_op jit(solution)/shard_map/broadcast_in_dim | solution.py:53
  36.8 3.7 %all-to-all-start.1 = ((bf16[32,16,128]{2,1,0:T(8,128)(2,1)}), bf16[32,16,128]{2,1,0:T(8,128)(2,1)S(1)}, u32[]{:S(2)}, u32[]{:S(2)}) async-start(bf16[32,16,128]{2,1,0:T(8,128)(2,1)} %broadcast_in_dim.86), calls=%async_computation.1 | async-start | bytes 262144 | tf_op jit(solution)/shard_map/all_to_all | solution.py:53
  40.4 2.7 %collective-permute-start.6 = (bf16[64,128]{1,0:T(8,128)(2,1)S(1)}, bf16[64,128]{1,0:T(8,128)(2,1)S(1)}, u32[]{:S(2)}, u32[]{:S(2)}) collective-permute-start(bf16[64,128]{1,0:T(8,128)(2,1)S(1)} %get-tuple-element.29), channel_id=1, source_target_pairs={{0,3},{1,2},{2,1},{3,0},{4,7},{5,6},{6,5},{7,4},{8,11},{9,10},{10,... | collective-permute-start | bytes 49160 | tf_op jit(solution)/shard_map/ppermute | solution.py:17
  43.8 1.4 %collective-permute-done.6 = bf16[64,128]{1,0:T(8,128)(2,1)S(1)} collective-permute-done((bf16[64,128]{1,0:T(8,128)(2,1)S(1)}, bf16[64,128]{1,0:T(8,128)(2,1)S(1)}, u32[]{:S(2)}, u32[]{:S(2)}) %collective-permute-start.6) | collective-permute-done | bytes 16416 | tf_op jit(solution)/shard_map/ppermute | solution.py:17
  45.2 1.7 %collective-permute-done.7 = bf16[64,128]{1,0:T(8,128)(2,1)S(1)} collective-permute-done((bf16[64,128]{1,0:T(8,128)(2,1)S(1)}, bf16[64,128]{1,0:T(8,128)(2,1)S(1)}, u32[]{:S(2)}, u32[]{:S(2)}) %collective-permute-start.7) | collective-permute-done | bytes 16416 | tf_op jit(solution)/shard_map/ppermute | solution.py:17
  46.9 1.9 %all-to-all-done.1 = bf16[32,16,128]{2,1,0:T(8,128)(2,1)S(1)} async-done(((bf16[32,16,128]{2,1,0:T(8,128)(2,1)}), bf16[32,16,128]{2,1,0:T(8,128)(2,1)S(1)}, u32[]{:S(2)}, u32[]{:S(2)}) %all-to-all-start.1) | async-done | bytes 131104 | tf_op jit(solution)/shard_map/all_to_all | solution.py:53
  49.6 0.9 %fusion.40 = (bf16[16,32,128]{2,1,0:T(8,128)(2,1)S(1)}, f32[16,32,128]{2,1,0:T(8,128)}) fusion(f32[16,32,128]{2,1,0:T(8,128)S(1)} %get-tuple-element.41, f32[16,32,128]{2,1,0:T(8,128)S(1)} %constant_dynamic-update-slice_fusion.15, bf16[16,32,128]{2,1,0:T(8,128)(2,1)S(1)} %constant_dynamic-update-slice_fusion.10, bf16[8,32,32]{1,2,0:T(8,128)(2,1)S(1)} %bitcast.113, ...), kind=kOutput, calls=%fused_computation.128 | convolution fusion | flops 4472832 | bytes 1081472 | tf_op jit(solution)/shard_map/ski,skr->sri/dot_general | solution.py:48
  50.5 0.6 %gather_fusion.4 = bf16[48,32,128]{2,1,0:T(8,128)(2,1)S(1)} fusion(bf16[16,32,128]{2,1,0:T(8,128)(2,1)S(1)} %get-tuple-element.43, s32[1024]{0:T(1024)S(1)} %get-tuple-element.46), kind=kCustom, calls=%fused_computation.4 | custom fusion | bytes 786624 | tf_op jit(solution)/shard_map/gather | solution.py:57
  51.2 0.8 %multiply_reduce_fusion.1 = (f32[32]{0:T(128)S(1)}, f32[32]{0:T(128)S(1)}, f32[8,32,128]{2,1,0:T(8,128)S(1)}) fusion(f32[8,32,128]{2,1,0:T(8,128)S(1)} %copy-done.1, f32[8,32,128]{2,1,0:T(8,128)S(1)} %get-tuple-element.42, f32[32]{0:T(128)S(1)} %fusion.21, bf16[8,7,128,128]{3,2,1,0:T(8,128)(2,1)S(1)} %copy-done, bf16[8,6,32,128]{3,2,1,0:T(8,128)(2,1)S(1)} %bitcast.109, ...), kind=kOutput, calls=%fused_computation.40 | convolution fusion | flops 59146176 | bytes 2687360 | tf_op jit(solution)/shard_map/btik,btrk->bri/dot_general | solution.py:58
  52.1 9.2 %all_to_all.15 = f32[32,1,128]{2,1,0:T(1,128)S(1)} all-to-all(f32[32,1,128]{2,1,0:T(1,128)S(1)} %broadcast_in_dim.92), channel_id=1, replica_groups=mesh['sx'=8,'sy'=4] {'sx','sy'}, dimensions={0} | all-to-all | bytes 32768 | tf_op jit(solution)/shard_map/all_to_all | solution.py:53
  61.4 0.8 %multiply_subtract_fusion = (f32[8,32,128]{2,1,0:T(8,128)}, f32[8,32,128]{2,1,0:T(8,128)}) fusion(f32[8,32,128]{2,1,0:T(8,128)S(1)} %get-tuple-element.45, f32[32]{0:T(128)S(1)} %add_divide_fusion, f32[8,32,128]{2,1,0:T(8,128)S(1)} %copy-done.1, f32[8,32,128]{2,1,0:T(8,128)S(1)} %get-tuple-element.42, f32[32]{0:T(128)S(1)} %fusion.21, ...), kind=kLoop, calls=%fused_computation.38 | loop fusion | flops 229376 | bytes 917760 | tf_op jit(solution)/shard_map/sub | solution.py:133
  (102 shorter events, 6.3 us)
Async XLA Ops:
  0.6 28.9 %copy-start = (bf16[8,7,128,128]{3,2,1,0:T(8,128)(2,1)S(1)}, bf16[8,7,128,128]{3,2,1,0:T(8,128)(2,1)}, u32[]{:S(2)}) copy-start(bf16[8,7,128,128]{3,2,1,0:T(8,128)(2,1)} %param.8) | copy-start | bytes 5505028
  2.5 13.9 %copy-start.1 = (f32[8,32,128]{2,1,0:T(8,128)S(1)}, f32[8,32,128]{2,1,0:T(8,128)}, u32[]{:S(2)}) copy-start(f32[8,32,128]{2,1,0:T(8,128)} %param.7) | copy-start | bytes 393220
  2.5 13.9 %copy-start.3 = (bf16[8,32,128]{2,1,0:T(8,128)(2,1)S(1)}, bf16[8,32,128]{2,1,0:T(8,128)(2,1)}, u32[]{:S(2)}) copy-start(bf16[8,32,128]{2,1,0:T(8,128)(2,1)} %param.12) | copy-start | bytes 196612
  8.8 11.7 %collective-permute-start = (bf16[384,128]{1,0:T(8,128)(2,1)S(1)}, bf16[384,128]{1,0:T(8,128)(2,1)S(1)}, u32[]{:S(2)}, u32[]{:S(2)}) collective-permute-start(bf16[384,128]{1,0:T(8,128)(2,1)S(1)} %get-tuple-element.11), channel_id=1, source_target_pairs={{0,28},{4,8},{8,4},{12,16},{16,12},{20,24},{24,20},{28,0},{1,29},{... | collective-permute-start | bytes 294920 | tf_op jit(solution)/shard_map/ppermute | solution.py:17
  13.3 7.2 %collective-permute-start.1 = (bf16[384,128]{1,0:T(8,128)(2,1)S(1)}, bf16[384,128]{1,0:T(8,128)(2,1)S(1)}, u32[]{:S(2)}, u32[]{:S(2)}) collective-permute-start(bf16[384,128]{1,0:T(8,128)(2,1)S(1)} %get-tuple-element.10), channel_id=1, source_target_pairs={{0,4},{4,0},{8,12},{12,8},{16,20},{20,16},{24,28},{28,24},{1,5},{5... | collective-permute-start | bytes 294920 | tf_op jit(solution)/shard_map/ppermute | solution.py:17
  13.3 7.3 %collective-permute-start.2 = (bf16[384,128]{1,0:T(8,128)(2,1)}, bf16[384,128]{1,0:T(8,128)(2,1)S(1)}, u32[]{:S(2)}, u32[]{:S(2)}) collective-permute-start(bf16[384,128]{1,0:T(8,128)(2,1)} %get-tuple-element.9), channel_id=1, source_target_pairs={{0,3},{1,2},{2,1},{3,0},{4,7},{5,6},{6,5},{7,4},{8,11},{9,10},{10,... | collective-permute-start | bytes 294920 | tf_op jit(solution)/shard_map/ppermute | solution.py:17
  15.8 6.0 %collective-permute-start.3 = (bf16[384,128]{1,0:T(8,128)(2,1)}, bf16[384,128]{1,0:T(8,128)(2,1)S(1)}, u32[]{:S(2)}, u32[]{:S(2)}) collective-permute-start(bf16[384,128]{1,0:T(8,128)(2,1)} %get-tuple-element.8), channel_id=1, source_target_pairs={{0,1},{1,0},{2,3},{3,2},{4,5},{5,4},{6,7},{7,6},{8,9},{9,8},{10,11... | collective-permute-start | bytes 294920 | tf_op jit(solution)/shard_map/ppermute | solution.py:17
  17.4 10.1 %all-to-all-start = ((bf16[32,8,128]{2,1,0:T(8,128)(2,1)}), bf16[32,8,128]{2,1,0:T(8,128)(2,1)S(1)}, u32[]{:S(2)}, u32[]{:S(2)}) async-start(bf16[32,8,128]{2,1,0:T(8,128)(2,1)} %broadcast_in_dim.80), calls=%async_computation | async-start | bytes 131072 | tf_op jit(solution)/shard_map/all_to_all | solution.py:53
  28.2 3.6 %copy-start.2 = (bf16[8,128,128]{2,1,0:T(8,128)(2,1)S(1)}, bf16[8,128,128]{2,1,0:T(8,128)(2,1)}, u32[]{:S(2)}) copy-start(bf16[8,128,128]{2,1,0:T(8,128)(2,1)} %param.11) | copy-start | bytes 786436
  34.6 9.2 %collective-permute-start.4 = (bf16[64,128]{1,0:T(8,128)(2,1)S(1)}, bf16[64,128]{1,0:T(8,128)(2,1)S(1)}, u32[]{:S(2)}, u32[]{:S(2)}) collective-permute-start(bf16[64,128]{1,0:T(8,128)(2,1)S(1)} %get-tuple-element.31), channel_id=1, source_target_pairs={{0,28},{4,8},{8,4},{12,16},{16,12},{20,24},{24,20},{28,0},{1,29},{... | collective-permute-start | bytes 49160 | tf_op jit(solution)/shard_map/ppermute | solution.py:17
  34.9 8.9 %collective-permute-start.5 = (bf16[64,128]{1,0:T(8,128)(2,1)S(1)}, bf16[64,128]{1,0:T(8,128)(2,1)S(1)}, u32[]{:S(2)}, u32[]{:S(2)}) collective-permute-start(bf16[64,128]{1,0:T(8,128)(2,1)S(1)} %get-tuple-element.30), channel_id=1, source_target_pairs={{0,4},{4,0},{8,12},{12,8},{16,20},{20,16},{24,28},{28,24},{1,5},{5... | collective-permute-start | bytes 49160 | tf_op jit(solution)/shard_map/ppermute | solution.py:17
  36.8 12.1 %all-to-all-start.1 = ((bf16[32,16,128]{2,1,0:T(8,128)(2,1)}), bf16[32,16,128]{2,1,0:T(8,128)(2,1)S(1)}, u32[]{:S(2)}, u32[]{:S(2)}) async-start(bf16[32,16,128]{2,1,0:T(8,128)(2,1)} %broadcast_in_dim.86), calls=%async_computation.1 | async-start | bytes 262144 | tf_op jit(solution)/shard_map/all_to_all | solution.py:53
  40.4 4.7 %collective-permute-start.6 = (bf16[64,128]{1,0:T(8,128)(2,1)S(1)}, bf16[64,128]{1,0:T(8,128)(2,1)S(1)}, u32[]{:S(2)}, u32[]{:S(2)}) collective-permute-start(bf16[64,128]{1,0:T(8,128)(2,1)S(1)} %get-tuple-element.29), channel_id=1, source_target_pairs={{0,3},{1,2},{2,1},{3,0},{4,7},{5,6},{6,5},{7,4},{8,11},{9,10},{10,... | collective-permute-start | bytes 49160 | tf_op jit(solution)/shard_map/ppermute | solution.py:17
  43.2 3.7 %collective-permute-start.7 = (bf16[64,128]{1,0:T(8,128)(2,1)S(1)}, bf16[64,128]{1,0:T(8,128)(2,1)S(1)}, u32[]{:S(2)}, u32[]{:S(2)}) collective-permute-start(bf16[64,128]{1,0:T(8,128)(2,1)S(1)} %get-tuple-element.28), channel_id=1, source_target_pairs={{0,1},{1,0},{2,3},{3,2},{4,5},{5,4},{6,7},{7,6},{8,9},{9,8},{10,11... | collective-permute-start | bytes 49160 | tf_op jit(solution)/shard_map/ppermute | solution.py:17
  50.5 10.9 %copy-start.4 = (f32[16,32,128]{2,1,0:T(8,128)S(1)}, f32[16,32,128]{2,1,0:T(8,128)}, u32[]{:S(2)}) copy-start(f32[16,32,128]{2,1,0:T(8,128)} %get-tuple-element.44) | copy-start | bytes 786436

commit v2 on v1

v2 whole, which is shorter than its diff:
```python
import functools

import jax
import jax.numpy as jnp
from jax import lax
from jax.experimental import pallas as pl
from jax.experimental.pallas import tpu as pltpu
from jax.sharding import PartitionSpec as P

AXES = ("sx", "sy")
BF = jnp.bfloat16
F32 = jnp.float32
NT = (((1,), (1,)), ((), ()))
LANES = 128
SLOT = 8
SWAPS = tuple((axis, odd) for axis in range(2) for odd in (False, True))


def swap(value, axis, odd):
    count = lax.axis_size(axis)
    pairs = []
    for place in range(count):
        step = 1 if (place % 2 == 0) != odd else -1
        pairs.append((place, (place + step) % count))
    return lax.ppermute(value, axis, pairs)


def swap_ends(number, odd):
    axis = AXES[number]
    place, count = lax.axis_index(axis), lax.axis_size(axis)
    up = (lax.rem(place, 2) == 0) != odd
    send = 2 * number + jnp.where(up, 0, 1)
    slot = 2 * number + jnp.where(up, 1, 0)
    valid = jnp.where(up, place < count - 1, place > 0)
    return send, slot, valid


def split(value):
    high = value.astype(BF)
    return high, (value - high.astype(F32)).astype(BF)


def restrict_slot(vectors, basis_ref):
    left, right = [], []
    for b, vector in enumerate(vectors):
        for part in split(vector):
            left.append(basis_ref[b])
            right.append(jnp.concatenate([part] * 4, axis=0))
    full = lax.dot_general(
        jnp.concatenate(left, axis=1), jnp.concatenate(right, axis=1), NT, preferred_element_type=F32
    )
    group = lax.broadcasted_iota(jnp.int32, (SLOT, LANES), 1) // 32
    slot = full[:SLOT]
    for j in range(1, 4):
        slot = jnp.where(group == j, full[SLOT * j : SLOT * (j + 1)], slot)
    return slot


def coarse_parts(arrived, inverses):
    count = arrived.shape[0]
    lane = lax.broadcasted_iota(jnp.int32, (1, 4, SLOT, LANES), 3) // 32
    part = lax.broadcasted_iota(jnp.int32, (1, 4, SLOT, LANES), 1)
    spread_out = jnp.where(lane == part, arrived[:, None].astype(F32), 0.0)
    column = spread_out.reshape(count * 4 * SLOT, LANES).astype(BF)
    product = jnp.dot(jnp.concatenate(inverses, axis=0), column, preferred_element_type=F32)
    parts = []
    for s in range(len(inverses)):
        turned = product[32 * s : 32 * (s + 1)].T
        parts.append((turned[:32] + turned[32:64] + turned[64:96] + turned[96:]).astype(BF))
    return parts


def local_product(vector, inverse):
    rows = vector.shape[0]
    both = lax.dot_general(jnp.concatenate(split(vector), axis=0), inverse, NT, preferred_element_type=F32)
    return both[:rows] + both[rows:]


def image_block(b, extended, tiles, cols_ref):
    vectors = [extended[b]] + [extended[cols_ref[b, t]] for t in range(tiles.shape[1] - 1)]
    blocks = [tiles[b, t] for t in range(tiles.shape[1])]
    return lax.dot_general(
        jnp.concatenate(vectors, axis=1), jnp.concatenate(blocks, axis=1), NT, preferred_element_type=F32
    )


def sums_row(upper, lower):
    return jnp.sum(jnp.concatenate([upper, lower, upper, lower], axis=0).T, axis=0, keepdims=True)


def start_tiles(tiles_hbm, tiles, sems):
    copies = [pltpu.make_async_copy(tiles_hbm.at[b], tiles.at[b], sems.at[b]) for b in range(tiles.shape[0])]
    for copy in copies:
        copy.start()
    return copies


def restrict_kernel(right_ref, basis_ref, slot_ref):
    vectors = [right_ref[b] for b in range(right_ref.shape[0])]
    slot_ref[...] = jnp.broadcast_to(restrict_slot(vectors, basis_ref).astype(BF)[None], slot_ref.shape)


def first_halo_kernel(send_ref, right_ref, block_inverse_ref, basis_ref, inverse_ref, local_ref, *out_refs):
    blocks, rhs, order = right_ref.shape
    halo = send_ref.shape[1]
    total = inverse_ref.shape[1]
    for b in range(blocks):
        local_ref[b] = local_product(right_ref[b], block_inverse_ref[b])
    inverse = inverse_ref[...].astype(BF)
    for (number, odd), out_ref in zip(SWAPS, out_refs):
        send, _, _ = swap_ends(number, odd)
        out_ref[:, :total] = inverse
        for m in range(halo):
            row = send_ref[send, m]
            out_ref[:, total + m * order : total + (m + 1) * order] = basis_ref[row]
            start = total + (halo + m) * order
            out_ref[:, start : start + order] = local_ref[row].astype(BF)


def first_image_kernel(
    cols_ref, arrived_ref, inverse_ref, halo0, halo1, halo2, halo3, basis_ref, local_ref, right_ref, tiles_hbm,
    slot_ref, update_ref, image_ref,
    tiles, extended, sems,
):
    copies = start_tiles(tiles_hbm, tiles, sems)
    blocks, rhs, order = right_ref.shape
    total = inverse_ref.shape[1]
    halos = (halo0, halo1, halo2, halo3)
    halo = (halo0.shape[1] - total) // (2 * order)
    inverses = [inverse_ref[...].astype(BF)] + [ref[:, :total] for ref in halos]
    coarse = coarse_parts(arrived_ref[...], inverses)
    for b in range(blocks):
        update = local_ref[b] + jnp.dot(coarse[0], basis_ref[b], preferred_element_type=F32)
        update_ref[b] = update
        extended[b] = update.astype(BF)
    for q, (number, odd) in enumerate(SWAPS):
        _, slot, valid = swap_ends(number, odd)
        for m in range(halo):
            basis = halos[q][:, total + m * order : total + (m + 1) * order]
            start = total + (halo + m) * order
            local = halos[q][:, start : start + order].astype(F32)
            update = local + jnp.dot(coarse[1 + q], basis, preferred_element_type=F32)
            update_ref[blocks + halo * q + m] = update
            extended[blocks + halo * slot + m] = jnp.where(valid, update, 0.0).astype(BF)
    upper = lower = jnp.zeros((rhs, order), F32)
    images = []
    for b in range(blocks):
        copies[b].wait()
        image = image_block(b, extended, tiles, cols_ref)
        image_ref[b] = image
        images.append(image)
        upper += right_ref[b] * image
        lower += image * image
    row = sums_row(upper, lower)
    high, low = split(row)
    lane = lax.broadcasted_iota(jnp.int32, (1, LANES), 1)
    row = jnp.where(lane < 64, high.astype(F32), low.astype(F32))
    whole = jnp.concatenate([restrict_slot(images, basis_ref), jnp.broadcast_to(row, (SLOT, LANES))], axis=0)
    slot_ref[...] = jnp.broadcast_to(whole.astype(BF)[None], slot_ref.shape)


def second_halo_kernel(send_ref, image_ref, block_inverse_ref, local_ref, *out_refs):
    blocks, rhs, order = image_ref.shape
    for b in range(blocks):
        local_ref[b] = local_product(image_ref[b], block_inverse_ref[b])
    for (number, odd), out_ref in zip(SWAPS, out_refs):
        send, _, _ = swap_ends(number, odd)
        for m in range(send_ref.shape[1]):
            out_ref[:, m * order : (m + 1) * order] = local_ref[send_ref[send, m]].astype(BF)


def second_image_kernel(
    cols_ref, arrived_ref, inverse_ref, halo0, halo1, halo2, halo3, next0, next1, next2, next3,
    basis_ref, local_ref, update_ref, image_ref, right_ref, tiles_hbm,
    slot_ref, scaled_ref, second_ref, residual_ref, image2_ref,
    tiles, extended, sems,
):
    copies = start_tiles(tiles_hbm, tiles, sems)
    blocks, rhs, order = right_ref.shape
    total = inverse_ref.shape[1]
    halos, nexts = (halo0, halo1, halo2, halo3), (next0, next1, next2, next3)
    halo = next0.shape[1] // order
    inverses = [inverse_ref[...].astype(BF)] + [ref[:, :total] for ref in halos]
    arrived = arrived_ref[...].astype(F32)
    coarse = coarse_parts(arrived[:, :SLOT], inverses)
    sums = jnp.sum(arrived[:, SLOT:], axis=0)
    turned = jnp.concatenate([sums] * (LANES // SLOT), axis=0).T
    weight = (turned[:32] + turned[64:96]) / (turned[32:64] + turned[96:] + 1e-6)
    for b in range(blocks):
        change = local_ref[b] + jnp.dot(coarse[0], basis_ref[b], preferred_element_type=F32)
        update = update_ref[b]
        second = update - weight * change
        scaled_ref[b] = weight * update
        second_ref[b] = second
        extended[b] = second.astype(BF)
    for q, (number, odd) in enumerate(SWAPS):
        _, slot, valid = swap_ends(number, odd)
        for m in range(halo):
            basis = halos[q][:, total + m * order : total + (m + 1) * order]
            local = nexts[q][:, m * order : (m + 1) * order].astype(F32)
            change = local + jnp.dot(coarse[1 + q], basis, preferred_element_type=F32)
            second = update_ref[blocks + halo * q + m] - weight * change
            extended[blocks + halo * slot + m] = jnp.where(valid, second, 0.0).astype(BF)
    upper = lower = jnp.zeros((rhs, order), F32)
    for b in range(blocks):
        residual = right_ref[b] - weight * image_ref[b]
        residual_ref[b] = residual
        copies[b].wait()
        image = image_block(b, extended, tiles, cols_ref)
        image2_ref[b] = image
        upper += residual * image
        lower += image * image
    slot_ref[...] = jnp.broadcast_to(sums_row(upper, lower)[None], slot_ref.shape)


def last_kernel(arrived_ref, scaled_ref, second_ref, residual_ref, image_ref, solution_ref, out_ref):
    sums = jnp.sum(arrived_ref[...], axis=0)
    turned = jnp.broadcast_to(sums, (LANES, LANES)).T
    weight = turned[:32] / (turned[32:64] + 1e-6)
    for b in range(scaled_ref.shape[0]):
        solution_ref[b] = scaled_ref[b] + weight * second_ref[b]
        out_ref[b] = residual_ref[b] - weight * image_ref[b]


def call(kernel, inputs, places, outputs, scratch=()):
    vmem, smem, anywhere = pltpu.VMEM, pltpu.SMEM, pl.ANY
    kinds = {"v": vmem, "s": smem, "a": anywhere}
    return pl.pallas_call(
        kernel,
        out_shape=[jax.ShapeDtypeStruct(shape, dtype) for shape, dtype in outputs],
        in_specs=[pl.BlockSpec(memory_space=kinds[place]) for place in places],
        out_specs=[pl.BlockSpec(memory_space=vmem)] * len(outputs),
        scratch_shapes=scratch,
        compiler_params=pltpu.CompilerParams(vmem_limit_bytes=48 * 1024 * 1024),
        name=kernel.__name__,
    )(*inputs)


def exchange(slots):
    return lax.all_to_all(slots, AXES, 0, 0, tiled=True)


def body(right_sides, tiles, tile_cols, send_rows, block_inverse, coarse_basis, coarse_inverse):
    blocks, rhs, order = right_sides.shape
    rows, total = coarse_inverse.shape
    halo = send_rows.shape[1]
    count = lax.axis_size("sx") * lax.axis_size("sy")
    field = ((blocks, rhs, order), F32)
    scratch = (
        pltpu.VMEM(tiles.shape, BF),
        pltpu.VMEM((blocks + 4 * halo, rhs, order), BF),
        pltpu.SemaphoreType.DMA((blocks,)),
    )

    (slots,) = call(restrict_kernel, (right_sides, coarse_basis), "vv", [((count, SLOT, LANES), BF)])
    arrived = exchange(slots)
    local, *halos = call(
        first_halo_kernel,
        (send_rows, right_sides, block_inverse, coarse_basis, coarse_inverse),
        "svvvv",
        [field] + [((rhs, total + 2 * halo * order), BF)] * 4,
    )
    halos = [swap(value, AXES[number], odd) for value, (number, odd) in zip(halos, SWAPS)]
    slots, update, image = call(
        first_image_kernel,
        (tile_cols, arrived, coarse_inverse, *halos, coarse_basis, local, right_sides, tiles),
        "svvvvvvvvva",
        [((count, 2 * SLOT, LANES), BF), ((blocks + 4 * halo, rhs, order), F32), field],
        scratch,
    )
    arrived = exchange(slots)
    local, *nexts = call(
        second_halo_kernel,
        (send_rows, image, block_inverse),
        "svv",
        [field] + [((rhs, halo * order), BF)] * 4,
    )
    nexts = [swap(value, AXES[number], odd) for value, (number, odd) in zip(nexts, SWAPS)]
    slots, scaled, second, residual, image = call(
        second_image_kernel,
        (tile_cols, arrived, coarse_inverse, *halos, *nexts, coarse_basis, local, update, image, right_sides, tiles),
        "svvvvvvvvvvvvvvva",
        [((count, 1, LANES), F32)] + [field] * 4,
        scratch,
    )
    return tuple(call(last_kernel, (exchange(slots), scaled, second, residual, image), "vvvvv", [field] * 2))


def solution(mesh):
    block3 = P(AXES, None, None)
    placed = (block3, P(AXES, None, None, None), P(AXES, None), P(AXES, None), block3, block3, P(AXES, None))
    return jax.shard_map(body, mesh=mesh, in_specs=placed, out_specs=(block3, block3), check_vma=False)
```

time: 62.7 us -> 67 us (1.069)
  Pallas kernels: 0 us -> 15.2 us
  matrix products: 8.24 us -> 0 us
  starting transfers between devices: 17.8 us -> 23.4 us
  other arithmetic: 5.5 us -> 0 us
  waiting for transfers between devices: 11.4 us -> 7.2 us
  local copies, waits for them, and re-layouts: 8.93 us -> 11 us
    pallas_call x0 -> x6, Pallas kernels: none -> 15.2 us  [call(): pl.pallas_call(kernel, out_shape=[jax.ShapeDtypeStruct(shape, dtype) for...]
    unnamed x17 -> x35, local copies, waits for them, and re-layouts: 0.08 us -> 11 us
    dot_general x14 -> x0, matrix products: 8.24 us -> none  [the longest x4 3.11 us: local_part(): jnp.einsum('bik,brk->bri', block_inverse, part, preferred_element_type=F32)]
    all_to_all x2, waiting for transfers between devices: 7.1 us -> 0.01 us  [exchange(): return lax.all_to_all(slots, AXES, 0, 0, tiled=True)]
    gather x5 -> x0, local copies, waits for them, and re-layouts: 3.8 us -> none  [the longest x1 1.4 us: body(): coarse_basis[send_rows].reshape(4, halo * vectors, order)]
    all_to_all x2, starting transfers between devices: 6.23 us -> 9.93 us  [exchange(): return lax.all_to_all(slots, AXES, 0, 0, tiled=True)]
    ppermute x8, waiting for transfers between devices: 4.28 us -> 7.19 us  [swap(): return lax.ppermute(value, axis, pairs)]
    broadcast_in_dim x16 -> x0, local copies, waits for them, and re-layouts: 2.36 us -> none  [the longest x5 1.44 us: gather(): jnp.broadcast_to(slot[None], (count,) + slot.shape)]
  transfers between devices with their start and end apart: 10 -> 10, of which waited for: 5 -> 4; matrix products, arithmetic and copies ran while one was open for 5% -> 1% of each run, Pallas kernels for 0% -> 3%
where the time goes in v2:
time: 67 us; the launch traced here: 66.4 us
  starting transfers between devices  23.4 us (35%)
  Pallas kernels  15.2 us (23%)
  local copies, waits for them, and re-layouts  11 us (16%)
  blocking collectives  8.87 us (13%)
  waiting for transfers between devices  7.2 us (11%)
  between operations  0.75 us (1%)
    pallas_call x6, Pallas kernels, call(): pl.pallas_call(kernel, out_shape=[jax.ShapeDtypeStruct(shape, dtype) for...  15.2 us
    ppermute x8, starting transfers between devices, swap(): return lax.ppermute(value, axis, pairs)  13.5 us
    unnamed x35, local copies, waits for them, and re-layouts  11 us
    all_to_all x2, starting transfers between devices, exchange(): return lax.all_to_all(slots, AXES, 0, 0, tiled=True)  9.93 us
    all_to_all x1, blocking collectives, exchange(): return lax.all_to_all(slots, AXES, 0, 0, tiled=True)  8.87 us
    ppermute x8, waiting for transfers between devices, swap(): return lax.ppermute(value, axis, pairs)  7.19 us
  transfers between devices with their start and end apart: 10, of which 4 were waited for; matrix products, arithmetic and copies ran while one was open for 1% of the time, Pallas kernels for 3%

profile of v2, /device:TPU:0, one launch (start us, length us, event | category | flops | bytes accessed | tf_op | source)
XLA Modules:
  0.0 66.4 jit_solution(15270924950907888023)
XLA Ops:
  0.6 0.9 %copy-done.2 = f32[8,32,128]{2,1,0:T(8,128)S(1)} copy-done((f32[8,32,128]{2,1,0:T(8,128)S(1)}, f32[8,32,128]{2,1,0:T(8,128)}, u32[]{:S(2)}) %copy-start.2) | copy-done | bytes 131096
  1.5 0.8 %copy-done.9 = bf16[8,32,128]{2,1,0:T(8,128)(2,1)S(1)} copy-done((bf16[8,32,128]{2,1,0:T(8,128)(2,1)S(1)}, bf16[8,32,128]{2,1,0:T(8,128)(2,1)}, u32[]{:S(2)}) %copy-start.9) | copy-done | bytes 65560
  2.4 0.9 %restrict_kernel.1 = bf16[32,8,128]{2,1,0:T(8,128)(2,1)} custom-call(f32[8,32,128]{2,1,0:T(8,128)S(1)} %copy-done.2, bf16[8,32,128]{2,1,0:T(8,128)(2,1)S(1)} %copy-done.9), custom_call_target="tpu_custom_call" | custom-call | tf_op jit(solution)/shard_map/restrict_kernel/pallas_call | solution.py:228
  3.3 7.3 %all-to-all-start = ((bf16[32,8,128]{2,1,0:T(8,128)(2,1)}), bf16[32,8,128]{2,1,0:T(8,128)(2,1)S(1)}, u32[]{:S(2)}, u32[]{:S(2)}) async-start(bf16[32,8,128]{2,1,0:T(8,128)(2,1)} %restrict_kernel.1), calls=%async_computation | async-start | bytes 131072 | tf_op jit(solution)/shard_map/all_to_all | solution.py:240
  10.6 0.8 %copy.9.send_ref = s32[4,2]{1,0:T(4,128)S(1)} copy(s32[4,2]{0,1:T(2,128)} %param.10) | data formatting | bytes 64 | tf_op args[3]
  11.4 0.9 %copy-done.3 = f32[8,32,128]{2,1,0:T(8,128)S(1)} copy-done((f32[8,32,128]{2,1,0:T(8,128)S(1)}, f32[8,32,128]{2,1,0:T(8,128)}, u32[]{:S(2)}) %copy-start.3) | copy-done | bytes 131096
  12.3 0.9 %copy-done.6 = f32[32,1024]{1,0:T(8,128)S(1)} copy-done((f32[32,1024]{1,0:T(8,128)S(1)}, f32[32,1024]{1,0:T(8,128)}, u32[]{:S(2)}) %copy-start.6) | copy-done | bytes 131096
  13.2 0.8 %copy-done.10 = bf16[8,32,128]{2,1,0:T(8,128)(2,1)S(1)} copy-done((bf16[8,32,128]{2,1,0:T(8,128)(2,1)S(1)}, bf16[8,32,128]{2,1,0:T(8,128)(2,1)}, u32[]{:S(2)}) %copy-start.10) | copy-done | bytes 65560
  14.0 0.9 %copy-done.13 = bf16[8,128,128]{2,1,0:T(8,128)(2,1)S(1)} copy-done((bf16[8,128,128]{2,1,0:T(8,128)(2,1)S(1)}, bf16[8,128,128]{2,1,0:T(8,128)(2,1)}, u32[]{:S(2)}) %copy-start.13) | copy-done | bytes 262168
  15.0 0.9 %first_halo_kernel.1 = (f32[8,32,128]{2,1,0:T(8,128)S(1)}, bf16[32,1536]{1,0:T(8,128)(2,1)S(1)}, bf16[32,1536]{1,0:T(8,128)(2,1)S(1)}, bf16[32,1536]{1,0:T(8,128)(2,1)S(1)}, bf16[32,1536]{1,0:T(8,128)(2,1)S(1)}) custom-call(s32[4,2]{1,0:T(4,128)S(1)} %copy.9.send_ref, f32[8,32,128]{2,1,0:T(8,128)S(1)} %copy-done.3, bf16[8,128,128]{2,1,0:T(8,128)(2,1)S(1)} %copy-done.13, ...), custom_call_target="tpu_custom_call" | custom-call | tf_op jit(solution)/shard_map/first_halo_kernel/pallas_call | solution.py:228
  15.9 0.3 collective-permute-start
  16.2 3.5 %collective-permute-start.1 = (bf16[32,1536]{1,0:T(8,128)(2,1)S(1)}, bf16[32,1536]{1,0:T(8,128)(2,1)S(1)}, u32[]{:S(2)}, u32[]{:S(2)}) collective-permute-start(bf16[32,1536]{1,0:T(8,128)(2,1)S(1)} %get-tuple-element.21), channel_id=1, source_target_pairs={{0,28},{4,8},{8,4},{12,16},{16,12},{20,24},{24,20},{28,0},{1,29},{... | collective-permute-start | bytes 294920 | tf_op jit(solution)/shard_map/ppermute | solution.py:25
  19.7 1.5 %collective-permute-start.2 = (bf16[32,1536]{1,0:T(8,128)(2,1)S(1)}, bf16[32,1536]{1,0:T(8,128)(2,1)S(1)}, u32[]{:S(2)}, u32[]{:S(2)}) collective-permute-start(bf16[32,1536]{1,0:T(8,128)(2,1)S(1)} %get-tuple-element.22), channel_id=1, source_target_pairs={{0,1},{1,0},{2,3},{3,2},{4,5},{5,4},{6,7},{7,6},{8,9},{9,8},{10,11... | collective-permute-start | bytes 294920 | tf_op jit(solution)/shard_map/ppermute | solution.py:25
  21.1 1.5 %collective-permute-start.3 = (bf16[32,1536]{1,0:T(8,128)(2,1)S(1)}, bf16[32,1536]{1,0:T(8,128)(2,1)S(1)}, u32[]{:S(2)}, u32[]{:S(2)}) collective-permute-start(bf16[32,1536]{1,0:T(8,128)(2,1)S(1)} %get-tuple-element.23), channel_id=1, source_target_pairs={{0,3},{1,2},{2,1},{3,0},{4,7},{5,6},{6,5},{7,4},{8,11},{9,10},{10,... | collective-permute-start | bytes 294920 | tf_op jit(solution)/shard_map/ppermute | solution.py:25
  22.6 2.1 %collective-permute-done.2.halo2 = bf16[32,1536]{1,0:T(8,128)(2,1)S(1)} collective-permute-done((bf16[32,1536]{1,0:T(8,128)(2,1)S(1)}, bf16[32,1536]{1,0:T(8,128)(2,1)S(1)}, u32[]{:S(2)}, u32[]{:S(2)}) %collective-permute-start.2) | collective-permute-done | bytes 98336 | tf_op jit(solution)/shard_map/ppermute | solution.py:25
  24.8 1.9 %collective-permute-done.3.halo3 = bf16[32,1536]{1,0:T(8,128)(2,1)S(1)} collective-permute-done((bf16[32,1536]{1,0:T(8,128)(2,1)S(1)}, bf16[32,1536]{1,0:T(8,128)(2,1)S(1)}, u32[]{:S(2)}, u32[]{:S(2)}) %collective-permute-start.3) | collective-permute-done | bytes 98336 | tf_op jit(solution)/shard_map/ppermute | solution.py:25
  26.7 1.5 %copy-done = bf16[8,7,128,128]{3,2,1,0:T(8,128)(2,1)S(1)} copy-done((bf16[8,7,128,128]{3,2,1,0:T(8,128)(2,1)S(1)}, bf16[8,7,128,128]{3,2,1,0:T(8,128)(2,1)}, u32[]{:S(2)}) %copy-start) | copy-done | bytes 1835032
  28.2 0.9 %copy-done.4 = f32[8,32,128]{2,1,0:T(8,128)S(1)} copy-done((f32[8,32,128]{2,1,0:T(8,128)S(1)}, f32[8,32,128]{2,1,0:T(8,128)}, u32[]{:S(2)}) %copy-start.4) | copy-done | bytes 131096
  29.1 0.9 %copy-done.7 = f32[32,1024]{1,0:T(8,128)S(1)} copy-done((f32[32,1024]{1,0:T(8,128)S(1)}, f32[32,1024]{1,0:T(8,128)}, u32[]{:S(2)}) %copy-start.7) | copy-done | bytes 131096
  30.0 0.8 %copy-done.11 = bf16[8,32,128]{2,1,0:T(8,128)(2,1)S(1)} copy-done((bf16[8,32,128]{2,1,0:T(8,128)(2,1)S(1)}, bf16[8,32,128]{2,1,0:T(8,128)(2,1)}, u32[]{:S(2)}) %copy-start.11) | copy-done | bytes 65560
  30.8 0.7 %copy-done.15 = s32[8,6]{1,0:T(8,128)S(1)} copy-done((s32[8,6]{1,0:T(8,128)S(1)}, s32[8,6]{1,0:T(8,128)}, u32[]{:S(2)}) %copy-start.15) | copy-done | bytes 216
  31.5 6.3 %first_image_kernel.1 = (bf16[32,16,128]{2,1,0:T(8,128)(2,1)}, f32[16,32,128]{2,1,0:T(8,128)S(1)}, f32[8,32,128]{2,1,0:T(8,128)S(1)}) custom-call(s32[8,6]{1,0:T(8,128)S(1)} %copy-done.15, bf16[32,8,128]{2,1,0:T(8,128)(2,1)S(1)} %all-to-all-done.arrived_ref, f32[32,1024]{1,0:T(8,128)S(1)} %copy-done.7, bf16[32,1536]{1,0:T(8,128)(2,1)S(1)} %collective-permute-done.halo0, ...), custom_call_target="tpu_custom_call" | custom-call | tf_op jit(solution)/shard_map/first_image_kernel/pallas_call | solution.py:228
  37.8 2.6 %all-to-all-start.1 = ((bf16[32,16,128]{2,1,0:T(8,128)(2,1)}), bf16[32,16,128]{2,1,0:T(8,128)(2,1)S(1)}, u32[]{:S(2)}, u32[]{:S(2)}) async-start(bf16[32,16,128]{2,1,0:T(8,128)(2,1)} %get-tuple-element.25), calls=%async_computation.1 | async-start | bytes 262144 | tf_op jit(solution)/shard_map/all_to_all | solution.py:240
  40.4 0.9 %second_halo_kernel.1 = (f32[8,32,128]{2,1,0:T(8,128)S(1)}, bf16[32,256]{1,0:T(8,128)(2,1)S(1)}, bf16[32,256]{1,0:T(8,128)(2,1)S(1)}, bf16[32,256]{1,0:T(8,128)(2,1)S(1)}, bf16[32,256]{1,0:T(8,128)(2,1)S(1)}) custom-call(s32[4,2]{1,0:T(4,128)S(1)} %copy.9.send_ref, f32[8,32,128]{2,1,0:T(8,128)S(1)} %get-tuple-element.26.image_ref, ...), custom_call_target="tpu_custom_call" | custom-call | tf_op jit(solution)/shard_map/second_halo_kernel/pallas_call | solution.py:228
  41.6 3.5 %collective-permute-start.5 = (bf16[32,256]{1,0:T(8,128)(2,1)S(1)}, bf16[32,256]{1,0:T(8,128)(2,1)S(1)}, u32[]{:S(2)}, u32[]{:S(2)}) collective-permute-start(bf16[32,256]{1,0:T(8,128)(2,1)S(1)} %get-tuple-element.28), channel_id=1, source_target_pairs={{0,28},{4,8},{8,4},{12,16},{16,12},{20,24},{24,20},{28,0},{1,29},{... | collective-permute-start | bytes 49160 | tf_op jit(solution)/shard_map/ppermute | solution.py:25
  45.1 1.5 %collective-permute-start.6 = (bf16[32,256]{1,0:T(8,128)(2,1)S(1)}, bf16[32,256]{1,0:T(8,128)(2,1)S(1)}, u32[]{:S(2)}, u32[]{:S(2)}) collective-permute-start(bf16[32,256]{1,0:T(8,128)(2,1)S(1)} %get-tuple-element.29), channel_id=1, source_target_pairs={{0,1},{1,0},{2,3},{3,2},{4,5},{5,4},{6,7},{7,6},{8,9},{9,8},{10,11... | collective-permute-start | bytes 49160 | tf_op jit(solution)/shard_map/ppermute | solution.py:25
  46.6 1.5 %collective-permute-start.7 = (bf16[32,256]{1,0:T(8,128)(2,1)S(1)}, bf16[32,256]{1,0:T(8,128)(2,1)S(1)}, u32[]{:S(2)}, u32[]{:S(2)}) collective-permute-start(bf16[32,256]{1,0:T(8,128)(2,1)S(1)} %get-tuple-element.30), channel_id=1, source_target_pairs={{0,3},{1,2},{2,1},{3,0},{4,7},{5,6},{6,5},{7,4},{8,11},{9,10},{10,... | collective-permute-start | bytes 49160 | tf_op jit(solution)/shard_map/ppermute | solution.py:25
  48.0 0.8 %collective-permute-done.6.next2 = bf16[32,256]{1,0:T(8,128)(2,1)S(1)} collective-permute-done((bf16[32,256]{1,0:T(8,128)(2,1)S(1)}, bf16[32,256]{1,0:T(8,128)(2,1)S(1)}, u32[]{:S(2)}, u32[]{:S(2)}) %collective-permute-start.6) | collective-permute-done | bytes 16416 | tf_op jit(solution)/shard_map/ppermute | solution.py:25
  48.8 2.4 %collective-permute-done.7.next3 = bf16[32,256]{1,0:T(8,128)(2,1)S(1)} collective-permute-done((bf16[32,256]{1,0:T(8,128)(2,1)S(1)}, bf16[32,256]{1,0:T(8,128)(2,1)S(1)}, u32[]{:S(2)}, u32[]{:S(2)}) %collective-permute-start.7) | collective-permute-done | bytes 16416 | tf_op jit(solution)/shard_map/ppermute | solution.py:25
  51.2 5.5 %second_image_kernel.1 = (f32[32,1,128]{2,1,0:T(1,128)S(1)}, f32[8,32,128]{2,1,0:T(8,128)S(1)}, f32[8,32,128]{2,1,0:T(8,128)S(1)}, f32[8,32,128]{2,1,0:T(8,128)S(1)}, f32[8,32,128]{2,1,0:T(8,128)S(1)}) custom-call(s32[8,6]{1,0:T(8,128)S(1)} %copy-done.16, bf16[32,16,128]{2,1,0:T(8,128)(2,1)S(1)} %all-to-all-done.1.arrived_ref, f32[32,1024]{1,0:T(8,128)S(1)} %copy-done.8, ...), custom_call_target="tpu_custom_call" | custom-call | tf_op jit(solution)/shard_map/second_image_kernel/pallas_call | solution.py:228
  56.7 8.9 %all_to_all.15.arrived_ref = f32[32,1,128]{2,1,0:T(1,128)S(1)} all-to-all(f32[32,1,128]{2,1,0:T(1,128)S(1)} %get-tuple-element.33), channel_id=1, replica_groups=mesh['sx'=8,'sy'=4] {'sx','sy'}, dimensions={0} | all-to-all | bytes 32768 | tf_op jit(solution)/shard_map/all_to_all | solution.py:240
  65.6 0.9 %last_kernel.1 = (f32[8,32,128]{2,1,0:T(8,128)}, f32[8,32,128]{2,1,0:T(8,128)}) custom-call(f32[32,1,128]{2,1,0:T(1,128)S(1)} %all_to_all.15.arrived_ref, f32[8,32,128]{2,1,0:T(8,128)S(1)} %get-tuple-element.34.scaled_ref, f32[8,32,128]{2,1,0:T(8,128)S(1)} %get-tuple-element.35.second_ref, f32[8,32,128]{2,1,0:T(8,128)S(1)} %get-tuple-element.36.residual_ref, ...), custom_call_target="tpu_custom_call" | custom-call | tf_op jit(solution)/shard_map/last_kernel/pallas_call | solution.py:228
  (30 shorter events, 0.4 us)
Async XLA Ops:
  0.6 0.9 %copy-start.2 = (f32[8,32,128]{2,1,0:T(8,128)S(1)}, f32[8,32,128]{2,1,0:T(8,128)}, u32[]{:S(2)}) copy-start(f32[8,32,128]{2,1,0:T(8,128)} %right_ref.7) | copy-start | bytes 393220
  1.5 0.8 %copy-start.9 = (bf16[8,32,128]{2,1,0:T(8,128)(2,1)S(1)}, bf16[8,32,128]{2,1,0:T(8,128)(2,1)}, u32[]{:S(2)}) copy-start(bf16[8,32,128]{2,1,0:T(8,128)(2,1)} %basis_ref.7) | copy-start | bytes 196612
  3.3 23.4 %all-to-all-start = ((bf16[32,8,128]{2,1,0:T(8,128)(2,1)}), bf16[32,8,128]{2,1,0:T(8,128)(2,1)S(1)}, u32[]{:S(2)}, u32[]{:S(2)}) async-start(bf16[32,8,128]{2,1,0:T(8,128)(2,1)} %restrict_kernel.1), calls=%async_computation | async-start | bytes 131072 | tf_op jit(solution)/shard_map/all_to_all | solution.py:240
  11.4 0.9 %copy-start.3 = (f32[8,32,128]{2,1,0:T(8,128)S(1)}, f32[8,32,128]{2,1,0:T(8,128)}, u32[]{:S(2)}) copy-start(f32[8,32,128]{2,1,0:T(8,128)} %right_ref.7) | copy-start | bytes 393220
  12.3 0.9 %copy-start.6 = (f32[32,1024]{1,0:T(8,128)S(1)}, f32[32,1024]{1,0:T(8,128)}, u32[]{:S(2)}) copy-start(f32[32,1024]{1,0:T(8,128)} %inverse_ref.5) | copy-start | bytes 393220
  13.2 0.8 %copy-start.10 = (bf16[8,32,128]{2,1,0:T(8,128)(2,1)S(1)}, bf16[8,32,128]{2,1,0:T(8,128)(2,1)}, u32[]{:S(2)}) copy-start(bf16[8,32,128]{2,1,0:T(8,128)(2,1)} %basis_ref.7) | copy-start | bytes 196612
  14.0 0.9 %copy-start.13 = (bf16[8,128,128]{2,1,0:T(8,128)(2,1)S(1)}, bf16[8,128,128]{2,1,0:T(8,128)(2,1)}, u32[]{:S(2)}) copy-start(bf16[8,128,128]{2,1,0:T(8,128)(2,1)} %block_inverse_ref.3) | copy-start | bytes 786436
  15.0 25.4 %copy-start.14 = (bf16[8,128,128]{2,1,0:T(8,128)(2,1)S(1)}, bf16[8,128,128]{2,1,0:T(8,128)(2,1)}, u32[]{:S(2)}) copy-start(bf16[8,128,128]{2,1,0:T(8,128)(2,1)} %block_inverse_ref.3) | copy-start | bytes 786436
  15.0 36.2 %copy-start.5 = (f32[8,32,128]{2,1,0:T(8,128)S(1)}, f32[8,32,128]{2,1,0:T(8,128)}, u32[]{:S(2)}) copy-start(f32[8,32,128]{2,1,0:T(8,128)} %right_ref.7) | copy-start | bytes 393220
  15.0 36.2 %copy-start.8 = (f32[32,1024]{1,0:T(8,128)S(1)}, f32[32,1024]{1,0:T(8,128)}, u32[]{:S(2)}) copy-start(f32[32,1024]{1,0:T(8,128)} %inverse_ref.5) | copy-start | bytes 393220
  15.0 36.2 %copy-start.12 = (bf16[8,32,128]{2,1,0:T(8,128)(2,1)S(1)}, bf16[8,32,128]{2,1,0:T(8,128)(2,1)}, u32[]{:S(2)}) copy-start(bf16[8,32,128]{2,1,0:T(8,128)(2,1)} %basis_ref.7) | copy-start | bytes 196612
  15.9 35.4 %copy-start.16 = (s32[8,6]{1,0:T(8,128)S(1)}, s32[8,6]{1,0:T(8,128)}, u32[]{:S(2)}) copy-start(s32[8,6]{1,0:T(8,128)} %cols_ref.3) | copy-start | bytes 580
  15.9 6.8 %collective-permute-start = (bf16[32,1536]{1,0:T(8,128)(2,1)S(1)}, bf16[32,1536]{1,0:T(8,128)(2,1)S(1)}, u32[]{:S(2)}, u32[]{:S(2)}) collective-permute-start(bf16[32,1536]{1,0:T(8,128)(2,1)S(1)} %get-tuple-element.20), channel_id=1, source_target_pairs={{0,4},{4,0},{8,12},{12,8},{16,20},{20,16},{24,28},{28,24},{1,5},{5... | collective-permute-start | bytes 294920 | tf_op jit(solution)/shard_map/ppermute | solution.py:25
  16.2 6.5 %collective-permute-start.1 = (bf16[32,1536]{1,0:T(8,128)(2,1)S(1)}, bf16[32,1536]{1,0:T(8,128)(2,1)S(1)}, u32[]{:S(2)}, u32[]{:S(2)}) collective-permute-start(bf16[32,1536]{1,0:T(8,128)(2,1)S(1)} %get-tuple-element.21), channel_id=1, source_target_pairs={{0,28},{4,8},{8,4},{12,16},{16,12},{20,24},{24,20},{28,0},{1,29},{... | collective-permute-start | bytes 294920 | tf_op jit(solution)/shard_map/ppermute | solution.py:25
  19.7 5.1 %collective-permute-start.2 = (bf16[32,1536]{1,0:T(8,128)(2,1)S(1)}, bf16[32,1536]{1,0:T(8,128)(2,1)S(1)}, u32[]{:S(2)}, u32[]{:S(2)}) collective-permute-start(bf16[32,1536]{1,0:T(8,128)(2,1)S(1)} %get-tuple-element.22), channel_id=1, source_target_pairs={{0,1},{1,0},{2,3},{3,2},{4,5},{5,4},{6,7},{7,6},{8,9},{9,8},{10,11... | collective-permute-start | bytes 294920 | tf_op jit(solution)/shard_map/ppermute | solution.py:25
  21.1 5.5 %collective-permute-start.3 = (bf16[32,1536]{1,0:T(8,128)(2,1)S(1)}, bf16[32,1536]{1,0:T(8,128)(2,1)S(1)}, u32[]{:S(2)}, u32[]{:S(2)}) collective-permute-start(bf16[32,1536]{1,0:T(8,128)(2,1)S(1)} %get-tuple-element.23), channel_id=1, source_target_pairs={{0,3},{1,2},{2,1},{3,0},{4,7},{5,6},{6,5},{7,4},{8,11},{9,10},{10,... | collective-permute-start | bytes 294920 | tf_op jit(solution)/shard_map/ppermute | solution.py:25
  26.7 1.5 %copy-start = (bf16[8,7,128,128]{3,2,1,0:T(8,128)(2,1)S(1)}, bf16[8,7,128,128]{3,2,1,0:T(8,128)(2,1)}, u32[]{:S(2)}) copy-start(bf16[8,7,128,128]{3,2,1,0:T(8,128)(2,1)} %tiles_hbm.3) | copy-start | bytes 5505028
  28.2 0.9 %copy-start.4 = (f32[8,32,128]{2,1,0:T(8,128)S(1)}, f32[8,32,128]{2,1,0:T(8,128)}, u32[]{:S(2)}) copy-start(f32[8,32,128]{2,1,0:T(8,128)} %right_ref.7) | copy-start | bytes 393220
  29.1 0.9 %copy-start.7 = (f32[32,1024]{1,0:T(8,128)S(1)}, f32[32,1024]{1,0:T(8,128)}, u32[]{:S(2)}) copy-start(f32[32,1024]{1,0:T(8,128)} %inverse_ref.5) | copy-start | bytes 393220
  30.0 0.8 %copy-start.11 = (bf16[8,32,128]{2,1,0:T(8,128)(2,1)S(1)}, bf16[8,32,128]{2,1,0:T(8,128)(2,1)}, u32[]{:S(2)}) copy-start(bf16[8,32,128]{2,1,0:T(8,128)(2,1)} %basis_ref.7) | copy-start | bytes 196612
  30.8 0.7 %copy-start.15 = (s32[8,6]{1,0:T(8,128)S(1)}, s32[8,6]{1,0:T(8,128)}, u32[]{:S(2)}) copy-start(s32[8,6]{1,0:T(8,128)} %cols_ref.3) | copy-start | bytes 580
  31.5 19.7 %copy-start.1 = (bf16[8,7,128,128]{3,2,1,0:T(8,128)(2,1)S(1)}, bf16[8,7,128,128]{3,2,1,0:T(8,128)(2,1)}, u32[]{:S(2)}) copy-start(bf16[8,7,128,128]{3,2,1,0:T(8,128)(2,1)} %tiles_hbm.3) | copy-start | bytes 5505028
  37.8 13.4 %all-to-all-start.1 = ((bf16[32,16,128]{2,1,0:T(8,128)(2,1)}), bf16[32,16,128]{2,1,0:T(8,128)(2,1)S(1)}, u32[]{:S(2)}, u32[]{:S(2)}) async-start(bf16[32,16,128]{2,1,0:T(8,128)(2,1)} %get-tuple-element.25), calls=%async_computation.1 | async-start | bytes 262144 | tf_op jit(solution)/shard_map/all_to_all | solution.py:240
  41.3 6.8 %collective-permute-start.4 = (bf16[32,256]{1,0:T(8,128)(2,1)S(1)}, bf16[32,256]{1,0:T(8,128)(2,1)S(1)}, u32[]{:S(2)}, u32[]{:S(2)}) collective-permute-start(bf16[32,256]{1,0:T(8,128)(2,1)S(1)} %get-tuple-element.27), channel_id=1, source_target_pairs={{0,4},{4,0},{8,12},{12,8},{16,20},{20,16},{24,28},{28,24},{1,5},{5... | collective-permute-start | bytes 49160 | tf_op jit(solution)/shard_map/ppermute | solution.py:25
  41.6 6.4 %collective-permute-start.5 = (bf16[32,256]{1,0:T(8,128)(2,1)S(1)}, bf16[32,256]{1,0:T(8,128)(2,1)S(1)}, u32[]{:S(2)}, u32[]{:S(2)}) collective-permute-start(bf16[32,256]{1,0:T(8,128)(2,1)S(1)} %get-tuple-element.28), channel_id=1, source_target_pairs={{0,28},{4,8},{8,4},{12,16},{16,12},{20,24},{24,20},{28,0},{1,29},{... | collective-permute-start | bytes 49160 | tf_op jit(solution)/shard_map/ppermute | solution.py:25
  45.1 3.7 %collective-permute-start.6 = (bf16[32,256]{1,0:T(8,128)(2,1)S(1)}, bf16[32,256]{1,0:T(8,128)(2,1)S(1)}, u32[]{:S(2)}, u32[]{:S(2)}) collective-permute-start(bf16[32,256]{1,0:T(8,128)(2,1)S(1)} %get-tuple-element.29), channel_id=1, source_target_pairs={{0,1},{1,0},{2,3},{3,2},{4,5},{5,4},{6,7},{7,6},{8,9},{9,8},{10,11... | collective-permute-start | bytes 49160 | tf_op jit(solution)/shard_map/ppermute | solution.py:25
  46.6 4.6 %collective-permute-start.7 = (bf16[32,256]{1,0:T(8,128)(2,1)S(1)}, bf16[32,256]{1,0:T(8,128)(2,1)S(1)}, u32[]{:S(2)}, u32[]{:S(2)}) collective-permute-start(bf16[32,256]{1,0:T(8,128)(2,1)S(1)} %get-tuple-element.30), channel_id=1, source_target_pairs={{0,3},{1,2},{2,1},{3,0},{4,7},{5,6},{6,5},{7,4},{8,11},{9,10},{10,... | collective-permute-start | bytes 49160 | tf_op jit(solution)/shard_map/ppermute | solution.py:25

commit v3 on v2

--- a/solution.py
+++ b/solution.py
@@ -13,7 +13,7 @@
 NT = (((1,), (1,)), ((), ()))
 LANES = 128
 SLOT = 8
-SWAPS = tuple((axis, odd) for axis in range(2) for odd in (False, True))
+SWAPS = ((1, True), (0, True), (1, False), (0, False))
 
 
 def swap(value, axis, odd):
@@ -88,47 +88,73 @@
     return jnp.sum(jnp.concatenate([upper, lower, upper, lower], axis=0).T, axis=0, keepdims=True)
 
 
-def start_tiles(tiles_hbm, tiles, sems):
-    copies = [pltpu.make_async_copy(tiles_hbm.at[b], tiles.at[b], sems.at[b]) for b in range(tiles.shape[0])]
+def fetch(pairs, sems):
+    copies = [pltpu.make_async_copy(source, target, sems.at[k]) for k, (source, target) in enumerate(pairs)]
     for copy in copies:
         copy.start()
     return copies
 
 
-def restrict_kernel(right_ref, basis_ref, slot_ref):
-    vectors = [right_ref[b] for b in range(right_ref.shape[0])]
+def start_kernel(
+    send_hbm, right_hbm, block_inverse_hbm, basis_hbm, inverse_hbm,
+    slot_hbm, right_ref, block_inverse_ref, basis_ref, inverse_ref, local_ref, out0, out1, out2, out3,
+    slot_ref, out_ref, send_ref, wide, sems, out_sems,
+):
+    copies = fetch(
+        [
+            (right_hbm, right_ref),
+            (basis_hbm, basis_ref),
+            (block_inverse_hbm, block_inverse_ref),
+            (inverse_hbm, wide),
+            (send_hbm, send_ref),
+        ],
+        sems,
+    )
+    blocks, rhs, order = right_ref.shape
+    halo = send_ref.shape[0]
+    total = wide.shape[1]
+    for copy in copies[:2]:
+        copy.wait()
+    vectors = [right_ref[b] for b in range(blocks)]
     slot_ref[...] = jnp.broadcast_to(restrict_slot(vectors, basis_ref).astype(BF)[None], slot_ref.shape)
-
-
-def first_halo_kernel(send_ref, right_ref, block_inverse_ref, basis_ref, inverse_ref, local_ref, *out_refs):
-    blocks, rhs, order = right_ref.shape
-    halo = send_ref.shape[1]
-    total = inverse_ref.shape[1]
+    leaving = fetch([(slot_ref, slot_hbm)], out_sems)
+    copies[2].wait()
     for b in range(blocks):
         local_ref[b] = local_product(right_ref[b], block_inverse_ref[b])
-    inverse = inverse_ref[...].astype(BF)
-    for (number, odd), out_ref in zip(SWAPS, out_refs):
+    copies[3].wait()
+    inverse = wide[...].astype(BF)
+    inverse_ref[...] = inverse
+    copies[4].wait()
+    for q, ((number, odd), out_hbm) in enumerate(zip(SWAPS, (out0, out1, out2, out3))):
         send, _, _ = swap_ends(number, odd)
-        out_ref[:, :total] = inverse
+        out_ref[q, :, :total] = inverse
         for m in range(halo):
-            row = send_ref[send, m]
-            out_ref[:, total + m * order : total + (m + 1) * order] = basis_ref[row]
+            row = send_ref[m, send]
+            out_ref[q, :, total + m * order : total + (m + 1) * order] = basis_ref[row]
             start = total + (halo + m) * order
-            out_ref[:, start : start + order] = local_ref[row].astype(BF)
-
-
-def first_image_kernel(
-    cols_ref, arrived_ref, inverse_ref, halo0, halo1, halo2, halo3, basis_ref, local_ref, right_ref, tiles_hbm,
-    slot_ref, update_ref, image_ref,
-    tiles, extended, sems,
+            out_ref[q, :, start : start + order] = local_ref[row].astype(BF)
+        leaving += fetch([(out_ref.at[q], out_hbm)], out_sems.at[pl.ds(1 + q, 1)])
+    for copy in leaving:
+        copy.wait()
+
+
+def load_kernel(after_ref, tiles_hbm, tiles_ref, sems):
+    for copy in fetch([(tiles_hbm.at[b], tiles_ref.at[b]) for b in range(tiles_ref.shape[0])], sems):
+        copy.wait()
+
+
+def first_kernel(
+    cols_hbm, send_hbm, arrived_ref, inverse_ref, halo0, halo1, halo2, halo3,
+    block_inverse_ref, basis_ref, local_ref, right_ref, tiles_ref,
+    slot_hbm, update_ref, image_ref, next_local_ref, out0, out1, out2, out3,
+    slot_ref, out_ref, cols_ref, send_ref, extended, sems, out_sems,
 ):
-    copies = start_tiles(tiles_hbm, tiles, sems)
+    copies = fetch([(cols_hbm, cols_ref), (send_hbm, send_ref)], sems)
     blocks, rhs, order = right_ref.shape
     total = inverse_ref.shape[1]
     halos = (halo0, halo1, halo2, halo3)
-    halo = (halo0.shape[1] - total) // (2 * order)
-    inverses = [inverse_ref[...].astype(BF)] + [ref[:, :total] for ref in halos]
-    coarse = coarse_parts(arrived_ref[...], inverses)
+    halo = send_ref.shape[0]
+    coarse = coarse_parts(arrived_ref[...], [inverse_ref[...]] + [ref[:, :total] for ref in halos])
     for b in range(blocks):
         update = local_ref[b] + jnp.dot(coarse[0], basis_ref[b], preferred_element_type=F32)
         update_ref[b] = update
@@ -142,11 +168,12 @@
             update = local + jnp.dot(coarse[1 + q], basis, preferred_element_type=F32)
             update_ref[blocks + halo * q + m] = update
             extended[blocks + halo * slot + m] = jnp.where(valid, update, 0.0).astype(BF)
+    for copy in copies:
+        copy.wait()
     upper = lower = jnp.zeros((rhs, order), F32)
     images = []
     for b in range(blocks):
-        copies[b].wait()
-        image = image_block(b, extended, tiles, cols_ref)
+        image = image_block(b, extended, tiles_ref, cols_ref)
         image_ref[b] = image
         images.append(image)
         upper += right_ref[b] * image
@@ -157,32 +184,31 @@
     row = jnp.where(lane < 64, high.astype(F32), low.astype(F32))
     whole = jnp.concatenate([restrict_slot(images, basis_ref), jnp.broadcast_to(row, (SLOT, LANES))], axis=0)
     slot_ref[...] = jnp.broadcast_to(whole.astype(BF)[None], slot_ref.shape)
-
-
-def second_halo_kernel(send_ref, image_ref, block_inverse_ref, local_ref, *out_refs):
-    blocks, rhs, order = image_ref.shape
-    for b in range(blocks):
-        local_ref[b] = local_product(image_ref[b], block_inverse_ref[b])
-    for (number, odd), out_ref in zip(SWAPS, out_refs):
+    leaving = fetch([(slot_ref, slot_hbm)], out_sems)
+    for b in range(blocks):
+        next_local_ref[b] = local_product(images[b], block_inverse_ref[b])
+    for q, ((number, odd), out_hbm) in enumerate(zip(SWAPS, (out0, out1, out2, out3))):
         send, _, _ = swap_ends(number, odd)
-        for m in range(send_ref.shape[1]):
-            out_ref[:, m * order : (m + 1) * order] = local_ref[send_ref[send, m]].astype(BF)
-
-
-def second_image_kernel(
-    cols_ref, arrived_ref, inverse_ref, halo0, halo1, halo2, halo3, next0, next1, next2, next3,
-    basis_ref, local_ref, update_ref, image_ref, right_ref, tiles_hbm,
+        for m in range(halo):
+            out_ref[q, :, m * order : (m + 1) * order] = next_local_ref[send_ref[m, send]].astype(BF)
+        leaving += fetch([(out_ref.at[q], out_hbm)], out_sems.at[pl.ds(1 + q, 1)])
+    for copy in leaving:
+        copy.wait()
+
+
+def second_kernel(
+    cols_hbm, arrived_ref, inverse_ref, halo0, halo1, halo2, halo3, next0, next1, next2, next3,
+    basis_ref, local_ref, update_ref, image_ref, right_ref, tiles_ref,
     slot_ref, scaled_ref, second_ref, residual_ref, image2_ref,
-    tiles, extended, sems,
+    cols_ref, extended, sems,
 ):
-    copies = start_tiles(tiles_hbm, tiles, sems)
+    (copy,) = fetch([(cols_hbm, cols_ref)], sems)
     blocks, rhs, order = right_ref.shape
     total = inverse_ref.shape[1]
     halos, nexts = (halo0, halo1, halo2, halo3), (next0, next1, next2, next3)
     halo = next0.shape[1] // order
-    inverses = [inverse_ref[...].astype(BF)] + [ref[:, :total] for ref in halos]
     arrived = arrived_ref[...].astype(F32)
-    coarse = coarse_parts(arrived[:, :SLOT], inverses)
+    coarse = coarse_parts(arrived[:, :SLOT], [inverse_ref[...]] + [ref[:, :total] for ref in halos])
     sums = jnp.sum(arrived[:, SLOT:], axis=0)
     turned = jnp.concatenate([sums] * (LANES // SLOT), axis=0).T
     weight = (turned[:32] + turned[64:96]) / (turned[32:64] + turned[96:] + 1e-6)
@@ -201,12 +227,12 @@
             change = local + jnp.dot(coarse[1 + q], basis, preferred_element_type=F32)
             second = update_ref[blocks + halo * q + m] - weight * change
             extended[blocks + halo * slot + m] = jnp.where(valid, second, 0.0).astype(BF)
+    copy.wait()
     upper = lower = jnp.zeros((rhs, order), F32)
     for b in range(blocks):
         residual = right_ref[b] - weight * image_ref[b]
         residual_ref[b] = residual
-        copies[b].wait()
-        image = image_block(b, extended, tiles, cols_ref)
+        image = image_block(b, extended, tiles_ref, cols_ref)
         image2_ref[b] = image
         upper += residual * image
         lower += image * image
@@ -223,15 +249,19 @@
 
 
 def call(kernel, inputs, places, outputs, scratch=()):
-    vmem, smem, anywhere = pltpu.VMEM, pltpu.SMEM, pl.ANY
-    kinds = {"v": vmem, "s": smem, "a": anywhere}
+    kinds = {"v": pltpu.VMEM, "h": pltpu.HBM}
+    into, out = places.split(">")
+    inputs = [pltpu.with_memory_space_constraint(x, pltpu.HBM) if p == "h" else x for x, p in zip(inputs, into)]
     return pl.pallas_call(
         kernel,
-        out_shape=[jax.ShapeDtypeStruct(shape, dtype) for shape, dtype in outputs],
-        in_specs=[pl.BlockSpec(memory_space=kinds[place]) for place in places],
-        out_specs=[pl.BlockSpec(memory_space=vmem)] * len(outputs),
+        out_shape=[
+            pltpu.HBM(shape, dtype) if p == "h" else jax.ShapeDtypeStruct(shape, dtype)
+            for (shape, dtype), p in zip(outputs, out)
+        ],
+        in_specs=[pl.BlockSpec(memory_space=kinds[p]) for p in into],
+        out_specs=[pl.BlockSpec(memory_space=kinds[p]) for p in out],
         scratch_shapes=scratch,
-        compiler_params=pltpu.CompilerParams(vmem_limit_bytes=48 * 1024 * 1024),
+        compiler_params=pltpu.CompilerParams(vmem_limit_bytes=32 * 1024 * 1024),
         name=kernel.__name__,
     )(*inputs)
 
@@ -245,45 +275,69 @@
     rows, total = coarse_inverse.shape
     halo = send_rows.shape[1]
     count = lax.axis_size("sx") * lax.axis_size("sy")
-    field = ((blocks, rhs, order), F32)
-    scratch = (
-        pltpu.VMEM(tiles.shape, BF),
-        pltpu.VMEM((blocks + 4 * halo, rhs, order), BF),
-        pltpu.SemaphoreType.DMA((blocks,)),
-    )
-
-    (slots,) = call(restrict_kernel, (right_sides, coarse_basis), "vv", [((count, SLOT, LANES), BF)])
+    field = (right_sides.shape, F32)
+    cols = pltpu.SMEM(tile_cols.shape, jnp.int32)
+    sends = pltpu.SMEM((halo, send_rows.shape[0]), jnp.int32)
+    turned_sends = send_rows.T
+    extended = pltpu.VMEM((blocks + 4 * halo, rhs, order), BF)
+
+    def sems(number):
+        return pltpu.SemaphoreType.DMA((number,))
+
+    def swapped(values):
+        return [swap(value, AXES[number], odd) for value, (number, odd) in zip(values, SWAPS)]
+
+    slots, right, inverses, basis, coarse_rows, local, *halos = call(
+        start_kernel,
+        (turned_sends, right_sides, block_inverse, coarse_basis, coarse_inverse),
+        "hhhhh>hvvvvvhhhh",
+        [
+            ((count, SLOT, LANES), BF),
+            field,
+            (block_inverse.shape, BF),
+            (coarse_basis.shape, BF),
+            (coarse_inverse.shape, BF),
+            field,
+        ]
+        + [((rhs, total + 2 * halo * order), BF)] * 4,
+        (
+            pltpu.VMEM((count, SLOT, LANES), BF),
+            pltpu.VMEM((4, rhs, total + 2 * halo * order), BF),
+            sends,
+            pltpu.VMEM(coarse_inverse.shape, F32),
+            sems(5),
+            sems(5),
+        ),
+    )
+    halos = swapped(halos)
     arrived = exchange(slots)
-    local, *halos = call(
-        first_halo_kernel,
-        (send_rows, right_sides, block_inverse, coarse_basis, coarse_inverse),
-        "svvvv",
-        [field] + [((rhs, total + 2 * halo * order), BF)] * 4,
-    )
-    halos = [swap(value, AXES[number], odd) for value, (number, odd) in zip(halos, SWAPS)]
-    slots, update, image = call(
-        first_image_kernel,
-        (tile_cols, arrived, coarse_inverse, *halos, coarse_basis, local, right_sides, tiles),
-        "svvvvvvvvva",
-        [((count, 2 * SLOT, LANES), BF), ((blocks + 4 * halo, rhs, order), F32), field],
-        scratch,
-    )
+    (blocks_of_a,) = call(load_kernel, (slots, tiles), "hh>v", [(tiles.shape, BF)], (sems(blocks),))
+    slots, update, image, local, *nexts = call(
+        first_kernel,
+        (tile_cols, turned_sends, arrived, coarse_rows, *halos, inverses, basis, local, right, blocks_of_a),
+        "hhvvvvvvvvvvv>hvvvhhhh",
+        [((count, 2 * SLOT, LANES), BF), ((blocks + 4 * halo, rhs, order), F32), field, field]
+        + [((rhs, halo * order), BF)] * 4,
+        (
+            pltpu.VMEM((count, 2 * SLOT, LANES), BF),
+            pltpu.VMEM((4, rhs, halo * order), BF),
+            cols,
+            sends,
+            extended,
+            sems(2),
+            sems(5),
+        ),
+    )
+    nexts = swapped(nexts)
     arrived = exchange(slots)
-    local, *nexts = call(
-        second_halo_kernel,
-        (send_rows, image, block_inverse),
-        "svv",
-        [field] + [((rhs, halo * order), BF)] * 4,
-    )
-    nexts = [swap(value, AXES[number], odd) for value, (number, odd) in zip(nexts, SWAPS)]
     slots, scaled, second, residual, image = call(
-        second_image_kernel,
-        (tile_cols, arrived, coarse_inverse, *halos, *nexts, coarse_basis, local, update, image, right_sides, tiles),
-        "svvvvvvvvvvvvvvva",
+        second_kernel,
+        (tile_cols, arrived, coarse_rows, *halos, *nexts, basis, local, update, image, right, blocks_of_a),
+        "hvvvvvvvvvvvvvvvv>vvvvv",
         [((count, 1, LANES), F32)] + [field] * 4,
-        scratch,
-    )
-    return tuple(call(last_kernel, (exchange(slots), scaled, second, residual, image), "vvvvv", [field] * 2))
+        (cols, extended, sems(1)),
+    )
+    return tuple(call(last_kernel, (exchange(slots), scaled, second, residual, image), "vvvvv>vv", [field] * 2))
 
 
 def solution(mesh):

time: 67 us -> 47.8 us (0.71)
  local copies, waits for them, and re-layouts: 11 us -> 0 us
  Pallas kernels: 15.2 us -> 9.63 us
  starting transfers between devices: 23.4 us -> 22.2 us
  waiting for transfers between devices: 7.2 us -> 6.04 us
    unnamed x35 -> x0, local copies, waits for them, and re-layouts: 11 us -> none
    pallas_call x6 -> x5, Pallas kernels: 15.2 us -> 9.63 us  [call(): pl.pallas_call(kernel, out_shape=[pltpu.HBM(shape, dtype) if p == 'h' els...]
    ppermute x8, starting transfers between devices: 13.5 us -> 12.2 us  [swap(): return lax.ppermute(value, axis, pairs)]
    ppermute x8, waiting for transfers between devices: 7.19 us -> 6.04 us  [swap(): return lax.ppermute(value, axis, pairs)]
  transfers between devices with their start and end apart: 10 -> 10, of which waited for: 4 -> 4; matrix products, arithmetic and copies ran while one was open for 1% -> 0% of each run, Pallas kernels for 3% -> 3%
where the time goes in v3:
time: 47.8 us; the launch traced here: 47.4 us
  starting transfers between devices  22.2 us (46%)
  Pallas kernels  9.63 us (20%)
  blocking collectives  8.87 us (19%)
  waiting for transfers between devices  6.04 us (13%)
  between operations  0.7 us (1%)
    ppermute x8, starting transfers between devices, swap(): return lax.ppermute(value, axis, pairs)  12.2 us
    all_to_all x2, starting transfers between devices, exchange(): return lax.all_to_all(slots, AXES, 0, 0, tiled=True)  9.98 us
    pallas_call x5, Pallas kernels, call(): pl.pallas_call(kernel, out_shape=[pltpu.HBM(shape, dtype) if p == 'h' els...  9.63 us
    all_to_all x1, blocking collectives, exchange(): return lax.all_to_all(slots, AXES, 0, 0, tiled=True)  8.87 us
    ppermute x8, waiting for transfers between devices, swap(): return lax.ppermute(value, axis, pairs)  6.04 us
  transfers between devices with their start and end apart: 10, of which 4 were waited for; matrix products, arithmetic and copies ran while one was open for 0% of the time, Pallas kernels for 3%

profile of v3, /device:TPU:0, one launch (start us, length us, event | category | flops | bytes accessed | tf_op | source)
XLA Modules:
  0.0 47.4 jit_solution(3857059281047023253)
XLA Ops:
  0.6 2.6 %start_kernel.1 = (bf16[32,8,128]{2,1,0:T(8,128)(2,1)}, f32[8,32,128]{2,1,0:T(8,128)S(1)}, bf16[8,128,128]{2,1,0:T(8,128)(2,1)S(1)}, bf16[8,32,128]{2,1,0:T(8,12...) custom-call(s32[2,4]{1,0:T(2,128)} %bitcast.1, ...), custom_call_target="tpu_custom_call" | custom-call | tf_op jit(solution)/shard_map/start_kernel/pallas_call | solution.py:255
  3.2 7.3 %all-to-all-start = ((bf16[32,8,128]{2,1,0:T(8,128)(2,1)}), bf16[32,8,128]{2,1,0:T(8,128)(2,1)S(1)}, u32[]{:S(2)}, u32[]{:S(2)}) async-start(bf16[32,8,128]{2,1,0:T(8,128)(2,1)} %get-tuple-element.25.after_ref), calls=%async_computation | async-start | bytes 131072 | tf_op jit(solution)/shard_map/all_to_all | solution.py:270
  10.5 2.7 %collective-permute-start = (bf16[32,1536]{1,0:T(8,128)(2,1)}, bf16[32,1536]{1,0:T(8,128)(2,1)S(1)}, u32[]{:S(2)}, u32[]{:S(2)}) collective-permute-start(bf16[32,1536]{1,0:T(8,128)(2,1)} %get-tuple-element.27), channel_id=1, source_target_pairs={{0,3},{1,2},{2,1},{3,0},{4,7},{5,6},{6,5},{7,4},{8,11},{9,10},{10,... | collective-permute-start | bytes 294920 | tf_op jit(solution)/shard_map/ppermute | solution.py:25
  13.3 2.8 %collective-permute-start.1 = (bf16[32,1536]{1,0:T(8,128)(2,1)}, bf16[32,1536]{1,0:T(8,128)(2,1)S(1)}, u32[]{:S(2)}, u32[]{:S(2)}) collective-permute-start(bf16[32,1536]{1,0:T(8,128)(2,1)} %get-tuple-element.28), channel_id=1, source_target_pairs={{0,28},{4,8},{8,4},{12,16},{16,12},{20,24},{24,20},{28,0},{1,29},{... | collective-permute-start | bytes 294920 | tf_op jit(solution)/shard_map/ppermute | solution.py:25
  16.1 0.5 %collective-permute-start.2 = (bf16[32,1536]{1,0:T(8,128)(2,1)}, bf16[32,1536]{1,0:T(8,128)(2,1)S(1)}, u32[]{:S(2)}, u32[]{:S(2)}) collective-permute-start(bf16[32,1536]{1,0:T(8,128)(2,1)} %get-tuple-element.29), channel_id=1, source_target_pairs={{0,1},{1,0},{2,3},{3,2},{4,5},{5,4},{6,7},{7,6},{8,9},{9,8},{10,11... | collective-permute-start | bytes 294920 | tf_op jit(solution)/shard_map/ppermute | solution.py:25
  16.6 0.0 collective-permute-start.3
  16.6 1.6 %load_kernel.1.tiles_ref = bf16[8,7,128,128]{3,2,1,0:T(8,128)(2,1)S(1)} custom-call(bf16[32,8,128]{2,1,0:T(8,128)(2,1)} %get-tuple-element.25.after_ref, bf16[8,7,128,128]{3,2,1,0:T(8,128)(2,1)} %tiles_hbm.1), custom_call_target="tpu_custom_call" | custom-call | tf_op jit(solution)/shard_map/load_kernel/pallas_call | solution.py:255
  18.3 0.0 collective-permute-done.halo0
  18.3 2.0 %collective-permute-done.1.halo1 = bf16[32,1536]{1,0:T(8,128)(2,1)S(1)} collective-permute-done((bf16[32,1536]{1,0:T(8,128)(2,1)}, bf16[32,1536]{1,0:T(8,128)(2,1)S(1)}, u32[]{:S(2)}, u32[]{:S(2)}) %collective-permute-start.1) | collective-permute-done | bytes 98336 | tf_op jit(solution)/shard_map/ppermute | solution.py:25
  20.2 0.7 %collective-permute-done.2.halo2 = bf16[32,1536]{1,0:T(8,128)(2,1)S(1)} collective-permute-done((bf16[32,1536]{1,0:T(8,128)(2,1)}, bf16[32,1536]{1,0:T(8,128)(2,1)S(1)}, u32[]{:S(2)}, u32[]{:S(2)}) %collective-permute-start.2) | collective-permute-done | bytes 98336 | tf_op jit(solution)/shard_map/ppermute | solution.py:25
  20.9 0.0 collective-permute-done.3.halo3
  20.9 0.0 all-to-all-done.arrived_ref
  20.9 2.6 %first_kernel.1 = (bf16[32,16,128]{2,1,0:T(8,128)(2,1)}, f32[16,32,128]{2,1,0:T(8,128)S(1)}, f32[8,32,128]{2,1,0:T(8,128)S(1)}, f32[8,32,128]{2,1,0:T(8,128)S(1)...) custom-call(s32[8,6]{1,0:T(8,128)} %cols_hbm.3, ...), custom_call_target="tpu_custom_call" | custom-call | tf_op jit(solution)/shard_map/first_kernel/pallas_call | solution.py:255
  23.5 2.7 %all-to-all-start.1 = ((bf16[32,16,128]{2,1,0:T(8,128)(2,1)}), bf16[32,16,128]{2,1,0:T(8,128)(2,1)S(1)}, u32[]{:S(2)}, u32[]{:S(2)}) async-start(bf16[32,16,128]{2,1,0:T(8,128)(2,1)} %get-tuple-element.35), calls=%async_computation.1 | async-start | bytes 262144 | tf_op jit(solution)/shard_map/all_to_all | solution.py:270
  26.2 2.7 %collective-permute-start.4 = (bf16[32,256]{1,0:T(8,128)(2,1)}, bf16[32,256]{1,0:T(8,128)(2,1)S(1)}, u32[]{:S(2)}, u32[]{:S(2)}) collective-permute-start(bf16[32,256]{1,0:T(8,128)(2,1)} %get-tuple-element.36), channel_id=1, source_target_pairs={{0,3},{1,2},{2,1},{3,0},{4,7},{5,6},{6,5},{7,4},{8,11},{9,10},{10,... | collective-permute-start | bytes 49160 | tf_op jit(solution)/shard_map/ppermute | solution.py:25
  28.9 2.8 %collective-permute-start.5 = (bf16[32,256]{1,0:T(8,128)(2,1)}, bf16[32,256]{1,0:T(8,128)(2,1)S(1)}, u32[]{:S(2)}, u32[]{:S(2)}) collective-permute-start(bf16[32,256]{1,0:T(8,128)(2,1)} %get-tuple-element.37), channel_id=1, source_target_pairs={{0,28},{4,8},{8,4},{12,16},{16,12},{20,24},{24,20},{28,0},{1,29},{... | collective-permute-start | bytes 49160 | tf_op jit(solution)/shard_map/ppermute | solution.py:25
  31.8 0.5 %collective-permute-start.6 = (bf16[32,256]{1,0:T(8,128)(2,1)}, bf16[32,256]{1,0:T(8,128)(2,1)S(1)}, u32[]{:S(2)}, u32[]{:S(2)}) collective-permute-start(bf16[32,256]{1,0:T(8,128)(2,1)} %get-tuple-element.38), channel_id=1, source_target_pairs={{0,1},{1,0},{2,3},{3,2},{4,5},{5,4},{6,7},{7,6},{8,9},{9,8},{10,11... | collective-permute-start | bytes 49160 | tf_op jit(solution)/shard_map/ppermute | solution.py:25
  32.3 0.0 collective-permute-start.7
  32.3 0.0 collective-permute-done.4.next0
  32.3 1.8 %collective-permute-done.5.next1 = bf16[32,256]{1,0:T(8,128)(2,1)S(1)} collective-permute-done((bf16[32,256]{1,0:T(8,128)(2,1)}, bf16[32,256]{1,0:T(8,128)(2,1)S(1)}, u32[]{:S(2)}, u32[]{:S(2)}) %collective-permute-start.5) | collective-permute-done | bytes 16416 | tf_op jit(solution)/shard_map/ppermute | solution.py:25
  34.2 1.6 %collective-permute-done.6.next2 = bf16[32,256]{1,0:T(8,128)(2,1)S(1)} collective-permute-done((bf16[32,256]{1,0:T(8,128)(2,1)}, bf16[32,256]{1,0:T(8,128)(2,1)S(1)}, u32[]{:S(2)}, u32[]{:S(2)}) %collective-permute-start.6) | collective-permute-done | bytes 16416 | tf_op jit(solution)/shard_map/ppermute | solution.py:25
  35.7 0.0 collective-permute-done.7.next3
  35.7 0.0 all-to-all-done.1.arrived_ref
  35.7 2.0 %second_kernel.1 = (f32[32,1,128]{2,1,0:T(1,128)S(1)}, f32[8,32,128]{2,1,0:T(8,128)S(1)}, f32[8,32,128]{2,1,0:T(8,128)S(1)}, f32[8,32,128]{2,1,0:T(8,128)S(1)}, f32[8,32,128]{2,1,0:T(8,128)S(1)}) custom-call(s32[8,6]{1,0:T(8,128)} %cols_hbm.3, bf16[32,16,128]{2,1,0:T(8,128)(2,1)S(1)} %all-to-all-done.1.arrived_ref, ...), custom_call_target="tpu_custom_call" | custom-call | tf_op jit(solution)/shard_map/second_kernel/pallas_call | solution.py:255
  37.7 8.9 %all_to_all.15.arrived_ref = f32[32,1,128]{2,1,0:T(1,128)S(1)} all-to-all(f32[32,1,128]{2,1,0:T(1,128)S(1)} %get-tuple-element.43), channel_id=1, replica_groups=mesh['sx'=8,'sy'=4] {'sx','sy'}, dimensions={0} | all-to-all | bytes 32768 | tf_op jit(solution)/shard_map/all_to_all | solution.py:270
  46.6 0.8 %last_kernel.1 = (f32[8,32,128]{2,1,0:T(8,128)}, f32[8,32,128]{2,1,0:T(8,128)}) custom-call(f32[32,1,128]{2,1,0:T(1,128)S(1)} %all_to_all.15.arrived_ref, f32[8,32,128]{2,1,0:T(8,128)S(1)} %get-tuple-element.44.scaled_ref, f32[8,32,128]{2,1,0:T(8,128)S(1)} %get-tuple-element.45.second_ref, f32[8,32,128]{2,1,0:T(8,128)S(1)} %get-tuple-element.46.residual_ref, ...), custom_call_target="tpu_custom_call" | custom-call | tf_op jit(solution)/shard_map/last_kernel/pallas_call | solution.py:255
Async XLA Ops:
  3.2 17.7 %all-to-all-start = ((bf16[32,8,128]{2,1,0:T(8,128)(2,1)}), bf16[32,8,128]{2,1,0:T(8,128)(2,1)S(1)}, u32[]{:S(2)}, u32[]{:S(2)}) async-start(bf16[32,8,128]{2,1,0:T(8,128)(2,1)} %get-tuple-element.25.after_ref), calls=%async_computation | async-start | bytes 131072 | tf_op jit(solution)/shard_map/all_to_all | solution.py:270
  10.5 7.8 %collective-permute-start = (bf16[32,1536]{1,0:T(8,128)(2,1)}, bf16[32,1536]{1,0:T(8,128)(2,1)S(1)}, u32[]{:S(2)}, u32[]{:S(2)}) collective-permute-start(bf16[32,1536]{1,0:T(8,128)(2,1)} %get-tuple-element.27), channel_id=1, source_target_pairs={{0,3},{1,2},{2,1},{3,0},{4,7},{5,6},{6,5},{7,4},{8,11},{9,10},{10,... | collective-permute-start | bytes 294920 | tf_op jit(solution)/shard_map/ppermute | solution.py:25
  13.3 7.0 %collective-permute-start.1 = (bf16[32,1536]{1,0:T(8,128)(2,1)}, bf16[32,1536]{1,0:T(8,128)(2,1)S(1)}, u32[]{:S(2)}, u32[]{:S(2)}) collective-permute-start(bf16[32,1536]{1,0:T(8,128)(2,1)} %get-tuple-element.28), channel_id=1, source_target_pairs={{0,28},{4,8},{8,4},{12,16},{16,12},{20,24},{24,20},{28,0},{1,29},{... | collective-permute-start | bytes 294920 | tf_op jit(solution)/shard_map/ppermute | solution.py:25
  16.1 4.8 %collective-permute-start.2 = (bf16[32,1536]{1,0:T(8,128)(2,1)}, bf16[32,1536]{1,0:T(8,128)(2,1)S(1)}, u32[]{:S(2)}, u32[]{:S(2)}) collective-permute-start(bf16[32,1536]{1,0:T(8,128)(2,1)} %get-tuple-element.29), channel_id=1, source_target_pairs={{0,1},{1,0},{2,3},{3,2},{4,5},{5,4},{6,7},{7,6},{8,9},{9,8},{10,11... | collective-permute-start | bytes 294920 | tf_op jit(solution)/shard_map/ppermute | solution.py:25
  16.6 4.3 %collective-permute-start.3 = (bf16[32,1536]{1,0:T(8,128)(2,1)}, bf16[32,1536]{1,0:T(8,128)(2,1)S(1)}, u32[]{:S(2)}, u32[]{:S(2)}) collective-permute-start(bf16[32,1536]{1,0:T(8,128)(2,1)} %get-tuple-element.30), channel_id=1, source_target_pairs={{0,4},{4,0},{8,12},{12,8},{16,20},{20,16},{24,28},{28,24},{1,5},{5... | collective-permute-start | bytes 294920 | tf_op jit(solution)/shard_map/ppermute | solution.py:25
  23.5 12.2 %all-to-all-start.1 = ((bf16[32,16,128]{2,1,0:T(8,128)(2,1)}), bf16[32,16,128]{2,1,0:T(8,128)(2,1)S(1)}, u32[]{:S(2)}, u32[]{:S(2)}) async-start(bf16[32,16,128]{2,1,0:T(8,128)(2,1)} %get-tuple-element.35), calls=%async_computation.1 | async-start | bytes 262144 | tf_op jit(solution)/shard_map/all_to_all | solution.py:270
  26.2 6.1 %collective-permute-start.4 = (bf16[32,256]{1,0:T(8,128)(2,1)}, bf16[32,256]{1,0:T(8,128)(2,1)S(1)}, u32[]{:S(2)}, u32[]{:S(2)}) collective-permute-start(bf16[32,256]{1,0:T(8,128)(2,1)} %get-tuple-element.36), channel_id=1, source_target_pairs={{0,3},{1,2},{2,1},{3,0},{4,7},{5,6},{6,5},{7,4},{8,11},{9,10},{10,... | collective-permute-start | bytes 49160 | tf_op jit(solution)/shard_map/ppermute | solution.py:25
  28.9 5.2 %collective-permute-start.5 = (bf16[32,256]{1,0:T(8,128)(2,1)}, bf16[32,256]{1,0:T(8,128)(2,1)S(1)}, u32[]{:S(2)}, u32[]{:S(2)}) collective-permute-start(bf16[32,256]{1,0:T(8,128)(2,1)} %get-tuple-element.37), channel_id=1, source_target_pairs={{0,28},{4,8},{8,4},{12,16},{16,12},{20,24},{24,20},{28,0},{1,29},{... | collective-permute-start | bytes 49160 | tf_op jit(solution)/shard_map/ppermute | solution.py:25
  31.8 3.9 %collective-permute-start.6 = (bf16[32,256]{1,0:T(8,128)(2,1)}, bf16[32,256]{1,0:T(8,128)(2,1)S(1)}, u32[]{:S(2)}, u32[]{:S(2)}) collective-permute-start(bf16[32,256]{1,0:T(8,128)(2,1)} %get-tuple-element.38), channel_id=1, source_target_pairs={{0,1},{1,0},{2,3},{3,2},{4,5},{5,4},{6,7},{7,6},{8,9},{9,8},{10,11... | collective-permute-start | bytes 49160 | tf_op jit(solution)/shard_map/ppermute | solution.py:25
  32.3 3.4 %collective-permute-start.7 = (bf16[32,256]{1,0:T(8,128)(2,1)}, bf16[32,256]{1,0:T(8,128)(2,1)S(1)}, u32[]{:S(2)}, u32[]{:S(2)}) collective-permute-start(bf16[32,256]{1,0:T(8,128)(2,1)} %get-tuple-element.39), channel_id=1, source_target_pairs={{0,4},{4,0},{8,12},{12,8},{16,20},{20,16},{24,28},{28,24},{1,5},{5... | collective-permute-start | bytes 49160 | tf_op jit(solution)/shard_map/ppermute | solution.py:25

commit v4 on v3

--- a/solution.py
+++ b/solution.py
@@ -14,15 +14,21 @@
 LANES = 128
 SLOT = 8
 SWAPS = ((1, True), (0, True), (1, False), (0, False))
-
-
-def swap(value, axis, odd):
-    count = lax.axis_size(axis)
+EARLY = 1, 0
+
+
+def swap(value, number, odd):
+    counts = [lax.axis_size(axis) for axis in AXES]
     pairs = []
-    for place in range(count):
-        step = 1 if (place % 2 == 0) != odd else -1
-        pairs.append((place, (place + step) % count))
-    return lax.ppermute(value, axis, pairs)
+    for device in range(counts[0] * counts[1]):
+        place = list(divmod(device, counts[1]))
+        other = place[number] + (1 if (place[number] % 2 == 0) != odd else -1)
+        if 0 <= other < counts[number]:
+            place[number] = other
+        else:
+            place[1 - number] ^= 2 if number == 0 and counts[1] % 4 == 0 else 1
+        pairs.append((device, place[0] * counts[1] + place[1]))
+    return lax.ppermute(value, AXES, pairs)
 
 
 def swap_ends(number, odd):
@@ -62,9 +68,9 @@
     part = lax.broadcasted_iota(jnp.int32, (1, 4, SLOT, LANES), 1)
     spread_out = jnp.where(lane == part, arrived[:, None].astype(F32), 0.0)
     column = spread_out.reshape(count * 4 * SLOT, LANES).astype(BF)
-    product = jnp.dot(jnp.concatenate(inverses, axis=0), column, preferred_element_type=F32)
+    product = jnp.dot(inverses, column, preferred_element_type=F32)
     parts = []
-    for s in range(len(inverses)):
+    for s in range(inverses.shape[0] // 32):
         turned = product[32 * s : 32 * (s + 1)].T
         parts.append((turned[:32] + turned[32:64] + turned[64:96] + turned[96:]).astype(BF))
     return parts
@@ -138,36 +144,78 @@
         copy.wait()
 
 
-def load_kernel(after_ref, tiles_hbm, tiles_ref, sems):
-    for copy in fetch([(tiles_hbm.at[b], tiles_ref.at[b]) for b in range(tiles_ref.shape[0])], sems):
+def gather_kernel(inverse_ref, basis_ref, tiles_hbm, *refs):
+    halos, (inverses_ref, bases_ref, locals_ref, tiles_ref, sems, tile_sems) = refs[:-6], refs[-6:]
+    rows, total = inverse_ref.shape
+    blocks, _, order = basis_ref.shape
+    pairs = []
+    for q, ref in enumerate(halos):
+        pairs.append((ref.at[:, pl.ds(0, total)], inverses_ref.at[pl.ds(rows * (1 + q), rows)]))
+        halo = (ref.shape[1] - total) // (2 * order)
+        for m in range(halo):
+            at = total + m * order
+            pairs.append((ref.at[:, pl.ds(at, order)], bases_ref.at[blocks + halo * q + m]))
+            pairs.append((ref.at[:, pl.ds(at + halo * order, order)], locals_ref.at[halo * q + m]))
+    copies = fetch(pairs, sems)
+    copies += fetch([(tiles_hbm.at[b], tiles_ref.at[b]) for b in range(tiles_ref.shape[0])], tile_sems)
+    inverses_ref[:rows] = inverse_ref[...]
+    bases_ref[:blocks] = basis_ref[...]
+    for copy in copies:
         copy.wait()
 
 
+def all_inverses(inverses_ref, late):
+    total = inverses_ref.shape[1]
+    return jnp.concatenate([inverses_ref[...]] + [ref[:, :total] for ref in late], axis=0)
+
+
+def basis_block(k, bases_ref, late, total, halo):
+    if k < bases_ref.shape[0]:
+        return bases_ref[k]
+    q, m = divmod(k - bases_ref.shape[0], halo)
+    order = bases_ref.shape[2]
+    return late[q][:, total + m * order : total + (m + 1) * order]
+
+
+def pack(extended, k, value, blocks, halo):
+    if k < blocks:
+        extended[k] = value.astype(BF)
+    else:
+        q, m = divmod(k - blocks, halo)
+        _, slot, valid = swap_ends(*SWAPS[q])
+        extended[blocks + halo * slot + m] = jnp.where(valid, value, 0.0).astype(BF)
+
+
+def owner(k, blocks, halo):
+    return 0 if k < blocks else 1 + (k - blocks) // halo
+
+
 def first_kernel(
-    cols_hbm, send_hbm, arrived_ref, inverse_ref, halo0, halo1, halo2, halo3,
-    block_inverse_ref, basis_ref, local_ref, right_ref, tiles_ref,
-    slot_hbm, update_ref, image_ref, next_local_ref, out0, out1, out2, out3,
-    slot_ref, out_ref, cols_ref, send_ref, extended, sems, out_sems,
+    cols_hbm, send_hbm, arrived_ref, inverses_ref, bases_ref, local_ref, locals_ref, block_inverse_ref, right_ref,
+    tiles_ref, *refs,
 ):
+    late, refs = refs[: 4 - EARLY[0]], refs[4 - EARLY[0] :]
+    slot_hbm, update_ref, image_ref, out0, out1, out2, out3 = refs[:7]
+    slot_ref, out_ref, cols_ref, send_ref, extended, sems, out_sems = refs[7:]
     copies = fetch([(cols_hbm, cols_ref), (send_hbm, send_ref)], sems)
     blocks, rhs, order = right_ref.shape
-    total = inverse_ref.shape[1]
-    halos = (halo0, halo1, halo2, halo3)
     halo = send_ref.shape[0]
-    coarse = coarse_parts(arrived_ref[...], [inverse_ref[...]] + [ref[:, :total] for ref in halos])
-    for b in range(blocks):
-        update = local_ref[b] + jnp.dot(coarse[0], basis_ref[b], preferred_element_type=F32)
-        update_ref[b] = update
-        extended[b] = update.astype(BF)
-    for q, (number, odd) in enumerate(SWAPS):
-        _, slot, valid = swap_ends(number, odd)
-        for m in range(halo):
-            basis = halos[q][:, total + m * order : total + (m + 1) * order]
-            start = total + (halo + m) * order
-            local = halos[q][:, start : start + order].astype(F32)
-            update = local + jnp.dot(coarse[1 + q], basis, preferred_element_type=F32)
-            update_ref[blocks + halo * q + m] = update
-            extended[blocks + halo * slot + m] = jnp.where(valid, update, 0.0).astype(BF)
+    total = inverses_ref.shape[1]
+    coarse = coarse_parts(arrived_ref[...], all_inverses(inverses_ref, late))
+    early = blocks + halo * EARLY[0]
+    for k in range(update_ref.shape[0]):
+        basis = basis_block(k, bases_ref, late, total, halo)
+        if k < blocks:
+            local = local_ref[k]
+        elif k < early:
+            local = locals_ref[k - blocks].astype(F32)
+        else:
+            q, m = divmod(k - early, halo)
+            at = total + (halo + m) * order
+            local = late[q][:, at : at + order].astype(F32)
+        update = local + jnp.dot(coarse[owner(k, blocks, halo)], basis, preferred_element_type=F32)
+        update_ref[k] = update
+        pack(extended, k, update, blocks, halo)
     for copy in copies:
         copy.wait()
     upper = lower = jnp.zeros((rhs, order), F32)
@@ -182,51 +230,60 @@
     high, low = split(row)
     lane = lax.broadcasted_iota(jnp.int32, (1, LANES), 1)
     row = jnp.where(lane < 64, high.astype(F32), low.astype(F32))
-    whole = jnp.concatenate([restrict_slot(images, basis_ref), jnp.broadcast_to(row, (SLOT, LANES))], axis=0)
+    whole = jnp.concatenate([restrict_slot(images, bases_ref), jnp.broadcast_to(row, (SLOT, LANES))], axis=0)
     slot_ref[...] = jnp.broadcast_to(whole.astype(BF)[None], slot_ref.shape)
     leaving = fetch([(slot_ref, slot_hbm)], out_sems)
-    for b in range(blocks):
-        next_local_ref[b] = local_product(images[b], block_inverse_ref[b])
     for q, ((number, odd), out_hbm) in enumerate(zip(SWAPS, (out0, out1, out2, out3))):
         send, _, _ = swap_ends(number, odd)
         for m in range(halo):
-            out_ref[q, :, m * order : (m + 1) * order] = next_local_ref[send_ref[m, send]].astype(BF)
+            row = send_ref[m, send]
+            local = local_product(image_ref[row], block_inverse_ref[row])
+            out_ref[q, :, m * order : (m + 1) * order] = local.astype(BF)
         leaving += fetch([(out_ref.at[q], out_hbm)], out_sems.at[pl.ds(1 + q, 1)])
     for copy in leaving:
         copy.wait()
 
 
+def local_kernel(image_ref, block_inverse_ref, *refs):
+    blocks, _, order = image_ref.shape
+    local_ref = refs[-1]
+    for b in range(blocks):
+        local_ref[b] = local_product(image_ref[b], block_inverse_ref[b])
+    for q, ref in enumerate(refs[:-1]):
+        halo = ref.shape[1] // order
+        for m in range(halo):
+            local_ref[blocks + halo * q + m] = ref[:, m * order : (m + 1) * order].astype(F32)
+
+
 def second_kernel(
-    cols_hbm, arrived_ref, inverse_ref, halo0, halo1, halo2, halo3, next0, next1, next2, next3,
-    basis_ref, local_ref, update_ref, image_ref, right_ref, tiles_ref,
-    slot_ref, scaled_ref, second_ref, residual_ref, image2_ref,
-    cols_ref, extended, sems,
+    cols_hbm, arrived_ref, inverses_ref, bases_ref, local_ref, update_ref, image_ref, right_ref, tiles_ref, *refs,
 ):
+    late, refs = refs[: 4 - EARLY[0]], refs[4 - EARLY[0] :]
+    nexts, refs = refs[: 4 - EARLY[1]], refs[4 - EARLY[1] :]
+    slot_ref, scaled_ref, second_ref, residual_ref, image2_ref, cols_ref, extended, sems = refs
     (copy,) = fetch([(cols_hbm, cols_ref)], sems)
     blocks, rhs, order = right_ref.shape
-    total = inverse_ref.shape[1]
-    halos, nexts = (halo0, halo1, halo2, halo3), (next0, next1, next2, next3)
-    halo = next0.shape[1] // order
+    halo = (update_ref.shape[0] - blocks) // 4
+    total = inverses_ref.shape[1]
     arrived = arrived_ref[...].astype(F32)
-    coarse = coarse_parts(arrived[:, :SLOT], [inverse_ref[...]] + [ref[:, :total] for ref in halos])
+    coarse = coarse_parts(arrived[:, :SLOT], all_inverses(inverses_ref, late))
     sums = jnp.sum(arrived[:, SLOT:], axis=0)
     turned = jnp.concatenate([sums] * (LANES // SLOT), axis=0).T
     weight = (turned[:32] + turned[64:96]) / (turned[32:64] + turned[96:] + 1e-6)
-    for b in range(blocks):
-        change = local_ref[b] + jnp.dot(coarse[0], basis_ref[b], preferred_element_type=F32)
-        update = update_ref[b]
-        second = update - weight * change
-        scaled_ref[b] = weight * update
-        second_ref[b] = second
-        extended[b] = second.astype(BF)
-    for q, (number, odd) in enumerate(SWAPS):
-        _, slot, valid = swap_ends(number, odd)
-        for m in range(halo):
-            basis = halos[q][:, total + m * order : total + (m + 1) * order]
+    for k in range(update_ref.shape[0]):
+        basis = basis_block(k, bases_ref, late, total, halo)
+        if k < local_ref.shape[0]:
+            local = local_ref[k]
+        else:
+            q, m = divmod(k - local_ref.shape[0], halo)
             local = nexts[q][:, m * order : (m + 1) * order].astype(F32)
-            change = local + jnp.dot(coarse[1 + q], basis, preferred_element_type=F32)
-            second = update_ref[blocks + halo * q + m] - weight * change
-            extended[blocks + halo * slot + m] = jnp.where(valid, second, 0.0).astype(BF)
+        update = update_ref[k]
+        spread = jnp.dot(coarse[owner(k, blocks, halo)], basis, preferred_element_type=F32)
+        second = update - weight * (local + spread)
+        if k < blocks:
+            scaled_ref[k] = weight * update
+            second_ref[k] = second
+        pack(extended, k, second, blocks, halo)
     copy.wait()
     upper = lower = jnp.zeros((rhs, order), F32)
     for b in range(blocks):
@@ -248,7 +305,7 @@
         out_ref[b] = residual_ref[b] - weight * image_ref[b]
 
 
-def call(kernel, inputs, places, outputs, scratch=()):
+def call(kernel, inputs, places, outputs, scratch=(), flops=None):
     kinds = {"v": pltpu.VMEM, "h": pltpu.HBM}
     into, out = places.split(">")
     inputs = [pltpu.with_memory_space_constraint(x, pltpu.HBM) if p == "h" else x for x, p in zip(inputs, into)]
@@ -262,6 +319,7 @@
         out_specs=[pl.BlockSpec(memory_space=kinds[p]) for p in out],
         scratch_shapes=scratch,
         compiler_params=pltpu.CompilerParams(vmem_limit_bytes=32 * 1024 * 1024),
+        cost_estimate=flops and pl.CostEstimate(flops=flops, bytes_accessed=0, transcendentals=0),
         name=kernel.__name__,
     )(*inputs)
 
@@ -285,7 +343,7 @@
         return pltpu.SemaphoreType.DMA((number,))
 
     def swapped(values):
-        return [swap(value, AXES[number], odd) for value, (number, odd) in zip(values, SWAPS)]
+        return [swap(value, number, odd) for value, (number, odd) in zip(values, SWAPS)]
 
     slots, right, inverses, basis, coarse_rows, local, *halos = call(
         start_kernel,
@@ -310,13 +368,27 @@
         ),
     )
     halos = swapped(halos)
+    early, late = halos[: EARLY[0]], halos[EARLY[0] :]
     arrived = exchange(slots)
-    (blocks_of_a,) = call(load_kernel, (slots, tiles), "hh>v", [(tiles.shape, BF)], (sems(blocks),))
-    slots, update, image, local, *nexts = call(
+    reach = blocks + halo * EARLY[0]
+    coarse_rows, bases, locals_, blocks_of_a = call(
+        gather_kernel,
+        (coarse_rows, basis, tiles, *early),
+        "vvh" + "h" * len(early) + ">vvvv",
+        [
+            (((1 + EARLY[0]) * rows, total), BF),
+            ((reach,) + coarse_basis.shape[1:], BF),
+            ((max(reach - blocks, 1), rhs, order), BF),
+            (tiles.shape, BF),
+        ],
+        (sems(max(1, (1 + 2 * halo) * EARLY[0])), sems(blocks)),
+        flops=10**11 if EARLY[0] else None,
+    )
+    slots, update, image, *nexts = call(
         first_kernel,
-        (tile_cols, turned_sends, arrived, coarse_rows, *halos, inverses, basis, local, right, blocks_of_a),
-        "hhvvvvvvvvvvv>hvvvhhhh",
-        [((count, 2 * SLOT, LANES), BF), ((blocks + 4 * halo, rhs, order), F32), field, field]
+        (tile_cols, turned_sends, arrived, coarse_rows, bases, local, locals_, inverses, right, blocks_of_a, *late),
+        "hhvvvvvvvv" + "v" * len(late) + ">hvvhhhh",
+        [((count, 2 * SLOT, LANES), BF), ((blocks + 4 * halo, rhs, order), F32), field]
         + [((rhs, halo * order), BF)] * 4,
         (
             pltpu.VMEM((count, 2 * SLOT, LANES), BF),
@@ -329,11 +401,19 @@
         ),
     )
     nexts = swapped(nexts)
+    soon, nexts = nexts[: EARLY[1]], nexts[EARLY[1] :]
     arrived = exchange(slots)
+    (local,) = call(
+        local_kernel,
+        (image, inverses, *soon),
+        "vv" + "v" * len(soon) + ">v",
+        [((blocks + halo * EARLY[1], rhs, order), F32)],
+        flops=10**11 if EARLY[1] else None,
+    )
     slots, scaled, second, residual, image = call(
         second_kernel,
-        (tile_cols, arrived, coarse_rows, *halos, *nexts, basis, local, update, image, right, blocks_of_a),
-        "hvvvvvvvvvvvvvvvv>vvvvv",
+        (tile_cols, arrived, coarse_rows, bases, local, update, image, right, blocks_of_a, *late, *nexts),
+        "hvvvvvvvv" + "v" * (len(late) + len(nexts)) + ">vvvvv",
         [((count, 1, LANES), F32)] + [field] * 4,
         (cols, extended, sems(1)),
     )

time: 47.8 us -> 45.7 us (0.956)
  starting transfers between devices: 22.2 us -> 19.5 us
  waiting for transfers between devices: 6.04 us -> 5.35 us
  local copies, waits for them, and re-layouts: 0 us -> 0.64 us
    ppermute x8, starting transfers between devices: 12.2 us -> 8.42 us  [swap(): return lax.ppermute(value, AXES, pairs)]
    ppermute x8, waiting for transfers between devices: 6.04 us -> 3.98 us  [swap(): return lax.ppermute(value, AXES, pairs)]
    all_to_all x2, waiting for transfers between devices: 0.01 us -> 1.37 us  [exchange(): return lax.all_to_all(slots, AXES, 0, 0, tiled=True)]
    all_to_all x2, starting transfers between devices: 9.98 us -> 11.1 us  [exchange(): return lax.all_to_all(slots, AXES, 0, 0, tiled=True)]
    unnamed x0 -> x2, local copies, waits for them, and re-layouts: none -> 0.64 us
    pallas_call x5 -> x6, Pallas kernels: 9.63 us -> 9.91 us  [call(): pl.pallas_call(kernel, out_shape=[pltpu.HBM(shape, dtype) if p == 'h' els...]
  transfers between devices with their start and end apart: 10 -> 10, of which waited for: 4 -> 5; matrix products, arithmetic and copies ran while one was open for 0% -> 0% of each run, Pallas kernels for 3% -> 4%
where the time goes in v4:
time: 45.7 us; the launch traced here: 45.3 us
  starting transfers between devices  19.5 us (43%)
  Pallas kernels  9.91 us (22%)
  blocking collectives  9.2 us (20%)
  waiting for transfers between devices  5.35 us (12%)
  between operations  0.7 us (2%)
  local copies, waits for them, and re-layouts  0.64 us (1%)
    all_to_all x2, starting transfers between devices, exchange(): return lax.all_to_all(slots, AXES, 0, 0, tiled=True)  11.1 us
    pallas_call x6, Pallas kernels, call(): pl.pallas_call(kernel, out_shape=[pltpu.HBM(shape, dtype) if p == 'h' els...  9.91 us
    all_to_all x1, blocking collectives, exchange(): return lax.all_to_all(slots, AXES, 0, 0, tiled=True)  9.2 us
    ppermute x8, starting transfers between devices, swap(): return lax.ppermute(value, AXES, pairs)  8.42 us
    ppermute x8, waiting for transfers between devices, swap(): return lax.ppermute(value, AXES, pairs)  3.98 us
    all_to_all x2, waiting for transfers between devices, exchange(): return lax.all_to_all(slots, AXES, 0, 0, tiled=True)  1.37 us
  transfers between devices with their start and end apart: 10, of which 5 were waited for; matrix products, arithmetic and copies ran while one was open for 0% of the time, Pallas kernels for 4%

profile of v4, /device:TPU:0, one launch (start us, length us, event | category | flops | bytes accessed | tf_op | source)
XLA Modules:
  0.0 45.3 jit_solution(10303360575511612455)
XLA Ops:
  0.6 2.6 %start_kernel.1 = (bf16[32,8,128]{2,1,0:T(8,128)(2,1)}, f32[8,32,128]{2,1,0:T(8,128)S(1)}, bf16[8,128,128]{2,1,0:T(8,128)(2,1)S(1)}, bf16[8,32,128]{2,1,0:T(8,12...) custom-call(s32[2,4]{1,0:T(2,128)} %bitcast.1, ...), custom_call_target="tpu_custom_call" | custom-call | tf_op jit(solution)/shard_map/start_kernel/pallas_call | solution.py:312
  3.2 0.5 %collective-permute-start = (bf16[32,1536]{1,0:T(8,128)(2,1)}, bf16[32,1536]{1,0:T(8,128)(2,1)S(1)}, u32[]{:S(2)}, u32[]{:S(2)}) collective-permute-start(bf16[32,1536]{1,0:T(8,128)(2,1)} %get-tuple-element.31), channel_id=1, source_target_pairs={{0,4},{1,2},{2,1},{3,7},{4,0},{5,6},{6,5},{7,3},{8,12},{9,10},{10,... | collective-permute-start | bytes 294920 | tf_op jit(solution)/shard_map/ppermute | solution.py:31
  3.7 7.4 %all-to-all-start = ((bf16[32,8,128]{2,1,0:T(8,128)(2,1)}), bf16[32,8,128]{2,1,0:T(8,128)(2,1)S(1)}, u32[]{:S(2)}, u32[]{:S(2)}) async-start(bf16[32,8,128]{2,1,0:T(8,128)(2,1)} %get-tuple-element.28), calls=%async_computation | async-start | bytes 131072 | tf_op jit(solution)/shard_map/all_to_all | solution.py:328
  11.1 1.8 %collective-permute-start.1 = (bf16[32,1536]{1,0:T(8,128)(2,1)}, bf16[32,1536]{1,0:T(8,128)(2,1)S(1)}, u32[]{:S(2)}, u32[]{:S(2)}) collective-permute-start(bf16[32,1536]{1,0:T(8,128)(2,1)} %get-tuple-element.39), channel_id=1, source_target_pairs={{0,2},{1,3},{2,0},{3,1},{4,8},{5,9},{6,10},{7,11},{8,4},{9,5},{10,... | collective-permute-start | bytes 294920 | tf_op jit(solution)/shard_map/ppermute | solution.py:31
  12.9 1.5 %collective-permute-start.2 = (bf16[32,1536]{1,0:T(8,128)(2,1)}, bf16[32,1536]{1,0:T(8,128)(2,1)S(1)}, u32[]{:S(2)}, u32[]{:S(2)}) collective-permute-start(bf16[32,1536]{1,0:T(8,128)(2,1)} %get-tuple-element.40), channel_id=1, source_target_pairs={{0,1},{1,0},{2,3},{3,2},{4,5},{5,4},{6,7},{7,6},{8,9},{9,8},{10,11... | collective-permute-start | bytes 294920 | tf_op jit(solution)/shard_map/ppermute | solution.py:31
  14.4 0.0 collective-permute-start.3
  14.4 0.0 collective-permute-done.refs_0_
  14.4 0.0 copy-start
  14.4 0.6 %copy-done = bf16[32,1536]{1,0:T(8,128)(2,1)} copy-done((bf16[32,1536]{1,0:T(8,128)(2,1)}, bf16[32,1536]{1,0:T(8,128)(2,1)S(1)}, u32[]{:S(2)}) %copy-start) | copy-done | bytes 98328
  15.1 1.7 %gather_kernel.1 = (bf16[64,1024]{1,0:T(8,128)(2,1)S(1)}, bf16[10,32,128]{2,1,0:T(8,128)(2,1)S(1)}, bf16[2,32,128]{2,1,0:T(8,128)(2,1)S(1)}, bf16[8,7,128,128]{3,2,1,0:T(8,128)(2,1)S(1)}) custom-call(bf16[32,1024]{1,0:T(8,128)(2,1)S(1)} %get-tuple-element.29.inverse_ref, bf16[8,32,128]{2,1,0:T(8,128)(2,1)S(1)} %get-tuple-element.30.basis_ref, ...), custom_call_target="tpu_custom_call" | custom-call | flops 99999997952 | tf_op jit(solution)/shard_map/gather_kernel/pallas_call | solution.py:312
  16.8 0.0 collective-permute-done.1.refs_0_
  16.8 1.5 %collective-permute-done.2.refs_1_ = bf16[32,1536]{1,0:T(8,128)(2,1)S(1)} collective-permute-done((bf16[32,1536]{1,0:T(8,128)(2,1)}, bf16[32,1536]{1,0:T(8,128)(2,1)S(1)}, u32[]{:S(2)}, u32[]{:S(2)}) %collective-permute-start.2) | collective-permute-done | bytes 98336 | tf_op jit(solution)/shard_map/ppermute | solution.py:31
  18.3 0.0 collective-permute-done.3.refs_2_
  18.3 0.3 all-to-all-done.arrived_ref
  18.6 2.6 %first_kernel.1 = (bf16[32,16,128]{2,1,0:T(8,128)(2,1)}, f32[16,32,128]{2,1,0:T(8,128)S(1)}, f32[8,32,128]{2,1,0:T(8,128)S(1)}, bf16[32,256]{1,0:T(8,128)(2,1)},...) custom-call(s32[8,6]{1,0:T(8,128)} %cols_hbm.3, s32[2,4]{1,0:T(2,128)} %bitcast.2, ...), custom_call_target="tpu_custom_call" | custom-call | tf_op jit(solution)/shard_map/first_kernel/pallas_call | solution.py:312
  21.2 3.7 %all-to-all-start.1 = ((bf16[32,16,128]{2,1,0:T(8,128)(2,1)}), bf16[32,16,128]{2,1,0:T(8,128)(2,1)S(1)}, u32[]{:S(2)}, u32[]{:S(2)}) async-start(bf16[32,16,128]{2,1,0:T(8,128)(2,1)} %get-tuple-element.42), calls=%async_computation.1 | async-start | bytes 262144 | tf_op jit(solution)/shard_map/all_to_all | solution.py:328
  24.9 0.3 collective-permute-start.4
  25.2 3.0 %collective-permute-start.5 = (bf16[32,256]{1,0:T(8,128)(2,1)}, bf16[32,256]{1,0:T(8,128)(2,1)S(1)}, u32[]{:S(2)}, u32[]{:S(2)}) collective-permute-start(bf16[32,256]{1,0:T(8,128)(2,1)} %get-tuple-element.46), channel_id=1, source_target_pairs={{0,2},{1,3},{2,0},{3,1},{4,8},{5,9},{6,10},{7,11},{8,4},{9,5},{10,... | collective-permute-start | bytes 49160 | tf_op jit(solution)/shard_map/ppermute | solution.py:31
  28.2 0.2 collective-permute-start.6
  28.4 1.2 %collective-permute-start.7 = (bf16[32,256]{1,0:T(8,128)(2,1)}, bf16[32,256]{1,0:T(8,128)(2,1)S(1)}, u32[]{:S(2)}, u32[]{:S(2)}) collective-permute-start(bf16[32,256]{1,0:T(8,128)(2,1)} %get-tuple-element.48), channel_id=1, source_target_pairs={{0,4},{1,5},{2,6},{3,7},{4,0},{5,1},{6,2},{7,3},{8,12},{9,13},{10,... | collective-permute-start | bytes 49160 | tf_op jit(solution)/shard_map/ppermute | solution.py:31
  29.5 0.3 local_kernel.1.local_ref
  29.8 0.0 collective-permute-done.4.refs_3_
  29.8 0.4 collective-permute-done.5.refs_4_
  30.2 2.1 %collective-permute-done.6.refs_5_ = bf16[32,256]{1,0:T(8,128)(2,1)S(1)} collective-permute-done((bf16[32,256]{1,0:T(8,128)(2,1)}, bf16[32,256]{1,0:T(8,128)(2,1)S(1)}, u32[]{:S(2)}, u32[]{:S(2)}) %collective-permute-start.6) | collective-permute-done | bytes 16416 | tf_op jit(solution)/shard_map/ppermute | solution.py:31
  32.3 0.0 collective-permute-done.7.refs_6_
  32.3 1.1 %all-to-all-done.1.arrived_ref = bf16[32,16,128]{2,1,0:T(8,128)(2,1)S(1)} async-done(((bf16[32,16,128]{2,1,0:T(8,128)(2,1)}), bf16[32,16,128]{2,1,0:T(8,128)(2,1)S(1)}, u32[]{:S(2)}, u32[]{:S(2)}) %all-to-all-start.1) | async-done | bytes 131104 | tf_op jit(solution)/shard_map/all_to_all | solution.py:328
  33.3 1.9 %second_kernel.1 = (f32[32,1,128]{2,1,0:T(1,128)S(1)}, f32[8,32,128]{2,1,0:T(8,128)S(1)}, f32[8,32,128]{2,1,0:T(8,128)S(1)}, f32[8,32,128]{2,1,0:T(8,128)S(1)}, f32[8,32,128]{2,1,0:T(8,128)S(1)}) custom-call(s32[8,6]{1,0:T(8,128)} %cols_hbm.3, bf16[32,16,128]{2,1,0:T(8,128)(2,1)S(1)} %all-to-all-done.1.arrived_ref, ...), custom_call_target="tpu_custom_call" | custom-call | tf_op jit(solution)/shard_map/second_kernel/pallas_call | solution.py:312
  35.3 9.2 %all_to_all.15.arrived_ref = f32[32,1,128]{2,1,0:T(1,128)S(1)} all-to-all(f32[32,1,128]{2,1,0:T(1,128)S(1)} %get-tuple-element.49), channel_id=1, replica_groups=mesh['sx'=8,'sy'=4] {'sx','sy'}, dimensions={0} | all-to-all | bytes 32768 | tf_op jit(solution)/shard_map/all_to_all | solution.py:328
  44.5 0.8 %last_kernel.1 = (f32[8,32,128]{2,1,0:T(8,128)}, f32[8,32,128]{2,1,0:T(8,128)}) custom-call(f32[32,1,128]{2,1,0:T(1,128)S(1)} %all_to_all.15.arrived_ref, f32[8,32,128]{2,1,0:T(8,128)S(1)} %get-tuple-element.50.scaled_ref, f32[8,32,128]{2,1,0:T(8,128)S(1)} %get-tuple-element.51.second_ref, f32[8,32,128]{2,1,0:T(8,128)S(1)} %get-tuple-element.52.residual_ref, ...), custom_call_target="tpu_custom_call" | custom-call | tf_op jit(solution)/shard_map/last_kernel/pallas_call | solution.py:312
Async XLA Ops:
  3.2 11.2 %collective-permute-start = (bf16[32,1536]{1,0:T(8,128)(2,1)}, bf16[32,1536]{1,0:T(8,128)(2,1)S(1)}, u32[]{:S(2)}, u32[]{:S(2)}) collective-permute-start(bf16[32,1536]{1,0:T(8,128)(2,1)} %get-tuple-element.31), channel_id=1, source_target_pairs={{0,4},{1,2},{2,1},{3,7},{4,0},{5,6},{6,5},{7,3},{8,12},{9,10},{10,... | collective-permute-start | bytes 294920 | tf_op jit(solution)/shard_map/ppermute | solution.py:31
  3.7 14.9 %all-to-all-start = ((bf16[32,8,128]{2,1,0:T(8,128)(2,1)}), bf16[32,8,128]{2,1,0:T(8,128)(2,1)S(1)}, u32[]{:S(2)}, u32[]{:S(2)}) async-start(bf16[32,8,128]{2,1,0:T(8,128)(2,1)} %get-tuple-element.28), calls=%async_computation | async-start | bytes 131072 | tf_op jit(solution)/shard_map/all_to_all | solution.py:328
  11.1 5.7 %collective-permute-start.1 = (bf16[32,1536]{1,0:T(8,128)(2,1)}, bf16[32,1536]{1,0:T(8,128)(2,1)S(1)}, u32[]{:S(2)}, u32[]{:S(2)}) collective-permute-start(bf16[32,1536]{1,0:T(8,128)(2,1)} %get-tuple-element.39), channel_id=1, source_target_pairs={{0,2},{1,3},{2,0},{3,1},{4,8},{5,9},{6,10},{7,11},{8,4},{9,5},{10,... | collective-permute-start | bytes 294920 | tf_op jit(solution)/shard_map/ppermute | solution.py:31
  12.9 5.4 %collective-permute-start.2 = (bf16[32,1536]{1,0:T(8,128)(2,1)}, bf16[32,1536]{1,0:T(8,128)(2,1)S(1)}, u32[]{:S(2)}, u32[]{:S(2)}) collective-permute-start(bf16[32,1536]{1,0:T(8,128)(2,1)} %get-tuple-element.40), channel_id=1, source_target_pairs={{0,1},{1,0},{2,3},{3,2},{4,5},{5,4},{6,7},{7,6},{8,9},{9,8},{10,11... | collective-permute-start | bytes 294920 | tf_op jit(solution)/shard_map/ppermute | solution.py:31
  14.4 3.9 %collective-permute-start.3 = (bf16[32,1536]{1,0:T(8,128)(2,1)}, bf16[32,1536]{1,0:T(8,128)(2,1)S(1)}, u32[]{:S(2)}, u32[]{:S(2)}) collective-permute-start(bf16[32,1536]{1,0:T(8,128)(2,1)} %get-tuple-element.41), channel_id=1, source_target_pairs={{0,4},{1,5},{2,6},{3,7},{4,0},{5,1},{6,2},{7,3},{8,12},{9,13},{10,... | collective-permute-start | bytes 294920 | tf_op jit(solution)/shard_map/ppermute | solution.py:31
  14.4 0.6 %copy-start = (bf16[32,1536]{1,0:T(8,128)(2,1)}, bf16[32,1536]{1,0:T(8,128)(2,1)S(1)}, u32[]{:S(2)}) copy-start(bf16[32,1536]{1,0:T(8,128)(2,1)S(1)} %collective-permute-done.refs_0_) | copy-start | bytes 294916
  21.2 12.1 %all-to-all-start.1 = ((bf16[32,16,128]{2,1,0:T(8,128)(2,1)}), bf16[32,16,128]{2,1,0:T(8,128)(2,1)S(1)}, u32[]{:S(2)}, u32[]{:S(2)}) async-start(bf16[32,16,128]{2,1,0:T(8,128)(2,1)} %get-tuple-element.42), calls=%async_computation.1 | async-start | bytes 262144 | tf_op jit(solution)/shard_map/all_to_all | solution.py:328
  24.9 4.9 %collective-permute-start.4 = (bf16[32,256]{1,0:T(8,128)(2,1)}, bf16[32,256]{1,0:T(8,128)(2,1)S(1)}, u32[]{:S(2)}, u32[]{:S(2)}) collective-permute-start(bf16[32,256]{1,0:T(8,128)(2,1)} %get-tuple-element.45), channel_id=1, source_target_pairs={{0,4},{1,2},{2,1},{3,7},{4,0},{5,6},{6,5},{7,3},{8,12},{9,10},{10,... | collective-permute-start | bytes 49160 | tf_op jit(solution)/shard_map/ppermute | solution.py:31
  25.2 4.9 %collective-permute-start.5 = (bf16[32,256]{1,0:T(8,128)(2,1)}, bf16[32,256]{1,0:T(8,128)(2,1)S(1)}, u32[]{:S(2)}, u32[]{:S(2)}) collective-permute-start(bf16[32,256]{1,0:T(8,128)(2,1)} %get-tuple-element.46), channel_id=1, source_target_pairs={{0,2},{1,3},{2,0},{3,1},{4,8},{5,9},{6,10},{7,11},{8,4},{9,5},{10,... | collective-permute-start | bytes 49160 | tf_op jit(solution)/shard_map/ppermute | solution.py:31
  28.2 4.0 %collective-permute-start.6 = (bf16[32,256]{1,0:T(8,128)(2,1)}, bf16[32,256]{1,0:T(8,128)(2,1)S(1)}, u32[]{:S(2)}, u32[]{:S(2)}) collective-permute-start(bf16[32,256]{1,0:T(8,128)(2,1)} %get-tuple-element.47), channel_id=1, source_target_pairs={{0,1},{1,0},{2,3},{3,2},{4,5},{5,4},{6,7},{7,6},{8,9},{9,8},{10,11... | collective-permute-start | bytes 49160 | tf_op jit(solution)/shard_map/ppermute | solution.py:31
  28.4 3.9 %collective-permute-start.7 = (bf16[32,256]{1,0:T(8,128)(2,1)}, bf16[32,256]{1,0:T(8,128)(2,1)S(1)}, u32[]{:S(2)}, u32[]{:S(2)}) collective-permute-start(bf16[32,256]{1,0:T(8,128)(2,1)} %get-tuple-element.48), channel_id=1, source_target_pairs={{0,4},{1,5},{2,6},{3,7},{4,0},{5,1},{6,2},{7,3},{8,12},{9,13},{10,... | collective-permute-start | bytes 49160 | tf_op jit(solution)/shard_map/ppermute | solution.py:31

commit v5 on v4

--- a/solution.py
+++ b/solution.py
@@ -103,7 +103,7 @@
 
 def start_kernel(
     send_hbm, right_hbm, block_inverse_hbm, basis_hbm, inverse_hbm,
-    slot_hbm, right_ref, block_inverse_ref, basis_ref, inverse_ref, local_ref, out0, out1, out2, out3,
+    slot_hbm, right_ref, block_inverse_ref, basis_ref, inverse_ref, out0, out1, out2, out3,
     slot_ref, out_ref, send_ref, wide, sems, out_sems,
 ):
     copies = fetch(
@@ -124,12 +124,10 @@
     vectors = [right_ref[b] for b in range(blocks)]
     slot_ref[...] = jnp.broadcast_to(restrict_slot(vectors, basis_ref).astype(BF)[None], slot_ref.shape)
     leaving = fetch([(slot_ref, slot_hbm)], out_sems)
-    copies[2].wait()
-    for b in range(blocks):
-        local_ref[b] = local_product(right_ref[b], block_inverse_ref[b])
     copies[3].wait()
     inverse = wide[...].astype(BF)
     inverse_ref[...] = inverse
+    copies[2].wait()
     copies[4].wait()
     for q, ((number, odd), out_hbm) in enumerate(zip(SWAPS, (out0, out1, out2, out3))):
         send, _, _ = swap_ends(number, odd)
@@ -138,28 +136,32 @@
             row = send_ref[m, send]
             out_ref[q, :, total + m * order : total + (m + 1) * order] = basis_ref[row]
             start = total + (halo + m) * order
-            out_ref[q, :, start : start + order] = local_ref[row].astype(BF)
+            local = local_product(right_ref[row], block_inverse_ref[row])
+            out_ref[q, :, start : start + order] = local.astype(BF)
         leaving += fetch([(out_ref.at[q], out_hbm)], out_sems.at[pl.ds(1 + q, 1)])
     for copy in leaving:
         copy.wait()
 
 
-def gather_kernel(inverse_ref, basis_ref, tiles_hbm, *refs):
-    halos, (inverses_ref, bases_ref, locals_ref, tiles_ref, sems, tile_sems) = refs[:-6], refs[-6:]
+def gather_kernel(inverse_ref, basis_ref, right_ref, block_inverse_ref, tiles_hbm, cols_hbm, send_hbm, *refs):
+    halos, refs = refs[: EARLY[0]], refs[EARLY[0] :]
+    inverses_ref, bases_ref, locals_ref, tiles_ref, cols_ref, send_ref, local_ref, sems, tile_sems = refs
     rows, total = inverse_ref.shape
     blocks, _, order = basis_ref.shape
-    pairs = []
+    copies = fetch([(cols_hbm, cols_ref), (send_hbm, send_ref)], sems)
+    copies += fetch([(tiles_hbm.at[b], tiles_ref.at[b]) for b in range(tiles_ref.shape[0])], tile_sems)
+    for b in range(blocks):
+        local_ref[b] = local_product(right_ref[b], block_inverse_ref[b])
+    inverses_ref[:rows] = inverse_ref[...]
+    bases_ref[:blocks] = basis_ref[...]
     for q, ref in enumerate(halos):
-        pairs.append((ref.at[:, pl.ds(0, total)], inverses_ref.at[pl.ds(rows * (1 + q), rows)]))
+        inverses_ref[rows * (1 + q) : rows * (2 + q)] = ref[:, :total]
         halo = (ref.shape[1] - total) // (2 * order)
         for m in range(halo):
             at = total + m * order
-            pairs.append((ref.at[:, pl.ds(at, order)], bases_ref.at[blocks + halo * q + m]))
-            pairs.append((ref.at[:, pl.ds(at + halo * order, order)], locals_ref.at[halo * q + m]))
-    copies = fetch(pairs, sems)
-    copies += fetch([(tiles_hbm.at[b], tiles_ref.at[b]) for b in range(tiles_ref.shape[0])], tile_sems)
-    inverses_ref[:rows] = inverse_ref[...]
-    bases_ref[:blocks] = basis_ref[...]
+            bases_ref[blocks + halo * q + m] = ref[:, at : at + order]
+            at += halo * order
+            locals_ref[halo * q + m] = ref[:, at : at + order]
     for copy in copies:
         copy.wait()
 
@@ -191,13 +193,13 @@
 
 
 def first_kernel(
-    cols_hbm, send_hbm, arrived_ref, inverses_ref, bases_ref, local_ref, locals_ref, block_inverse_ref, right_ref,
+    cols_vmem, send_vmem, arrived_ref, inverses_ref, bases_ref, local_ref, locals_ref, block_inverse_ref, right_ref,
     tiles_ref, *refs,
 ):
     late, refs = refs[: 4 - EARLY[0]], refs[4 - EARLY[0] :]
     slot_hbm, update_ref, image_ref, out0, out1, out2, out3 = refs[:7]
     slot_ref, out_ref, cols_ref, send_ref, extended, sems, out_sems = refs[7:]
-    copies = fetch([(cols_hbm, cols_ref), (send_hbm, send_ref)], sems)
+    copies = fetch([(cols_vmem, cols_ref), (send_vmem, send_ref)], sems)
     blocks, rhs, order = right_ref.shape
     halo = send_ref.shape[0]
     total = inverses_ref.shape[1]
@@ -230,7 +232,9 @@
     high, low = split(row)
     lane = lax.broadcasted_iota(jnp.int32, (1, LANES), 1)
     row = jnp.where(lane < 64, high.astype(F32), low.astype(F32))
-    whole = jnp.concatenate([restrict_slot(images, bases_ref), jnp.broadcast_to(row, (SLOT, LANES))], axis=0)
+    slot = restrict_slot(images, bases_ref)
+    half = SLOT // 2
+    whole = jnp.concatenate([slot[:half], slot[half:], jnp.broadcast_to(row, (half, LANES))], axis=1)
     slot_ref[...] = jnp.broadcast_to(whole.astype(BF)[None], slot_ref.shape)
     leaving = fetch([(slot_ref, slot_hbm)], out_sems)
     for q, ((number, odd), out_hbm) in enumerate(zip(SWAPS, (out0, out1, out2, out3))):
@@ -256,19 +260,20 @@
 
 
 def second_kernel(
-    cols_hbm, arrived_ref, inverses_ref, bases_ref, local_ref, update_ref, image_ref, right_ref, tiles_ref, *refs,
+    cols_vmem, arrived_ref, inverses_ref, bases_ref, local_ref, update_ref, image_ref, right_ref, tiles_ref, *refs,
 ):
     late, refs = refs[: 4 - EARLY[0]], refs[4 - EARLY[0] :]
     nexts, refs = refs[: 4 - EARLY[1]], refs[4 - EARLY[1] :]
     slot_ref, scaled_ref, second_ref, residual_ref, image2_ref, cols_ref, extended, sems = refs
-    (copy,) = fetch([(cols_hbm, cols_ref)], sems)
+    (copy,) = fetch([(cols_vmem, cols_ref)], sems)
     blocks, rhs, order = right_ref.shape
     halo = (update_ref.shape[0] - blocks) // 4
     total = inverses_ref.shape[1]
     arrived = arrived_ref[...].astype(F32)
-    coarse = coarse_parts(arrived[:, :SLOT], all_inverses(inverses_ref, late))
-    sums = jnp.sum(arrived[:, SLOT:], axis=0)
-    turned = jnp.concatenate([sums] * (LANES // SLOT), axis=0).T
+    restricted = jnp.concatenate([arrived[:, :, :LANES], arrived[:, :, LANES : 2 * LANES]], axis=1)
+    coarse = coarse_parts(restricted, all_inverses(inverses_ref, late))
+    sums = jnp.sum(arrived[:, :1, 2 * LANES :], axis=0)
+    turned = jnp.broadcast_to(sums, (LANES, LANES)).T
     weight = (turned[:32] + turned[64:96]) / (turned[32:64] + turned[96:] + 1e-6)
     for k in range(update_ref.shape[0]):
         basis = basis_block(k, bases_ref, late, total, halo)
@@ -345,17 +350,16 @@
     def swapped(values):
         return [swap(value, number, odd) for value, (number, odd) in zip(values, SWAPS)]
 
-    slots, right, inverses, basis, coarse_rows, local, *halos = call(
+    slots, right, inverses, basis, coarse_rows, *halos = call(
         start_kernel,
         (turned_sends, right_sides, block_inverse, coarse_basis, coarse_inverse),
-        "hhhhh>hvvvvvhhhh",
+        "hhhhh>hvvvvhhhh",
         [
             ((count, SLOT, LANES), BF),
             field,
             (block_inverse.shape, BF),
             (coarse_basis.shape, BF),
             (coarse_inverse.shape, BF),
-            field,
         ]
         + [((rhs, total + 2 * halo * order), BF)] * 4,
         (
@@ -371,27 +375,30 @@
     early, late = halos[: EARLY[0]], halos[EARLY[0] :]
     arrived = exchange(slots)
     reach = blocks + halo * EARLY[0]
-    coarse_rows, bases, locals_, blocks_of_a = call(
+    coarse_rows, bases, locals_, blocks_of_a, tile_cols, turned_sends, local = call(
         gather_kernel,
-        (coarse_rows, basis, tiles, *early),
-        "vvh" + "h" * len(early) + ">vvvv",
+        (coarse_rows, basis, right, inverses, tiles, tile_cols, turned_sends, *early),
+        "vvvvhhh" + "v" * len(early) + ">vvvvvvv",
         [
             (((1 + EARLY[0]) * rows, total), BF),
             ((reach,) + coarse_basis.shape[1:], BF),
             ((max(reach - blocks, 1), rhs, order), BF),
             (tiles.shape, BF),
+            (tile_cols.shape, jnp.int32),
+            (turned_sends.shape, jnp.int32),
+            field,
         ],
-        (sems(max(1, (1 + 2 * halo) * EARLY[0])), sems(blocks)),
+        (sems(2), sems(blocks)),
         flops=10**11 if EARLY[0] else None,
     )
     slots, update, image, *nexts = call(
         first_kernel,
         (tile_cols, turned_sends, arrived, coarse_rows, bases, local, locals_, inverses, right, blocks_of_a, *late),
-        "hhvvvvvvvv" + "v" * len(late) + ">hvvhhhh",
-        [((count, 2 * SLOT, LANES), BF), ((blocks + 4 * halo, rhs, order), F32), field]
+        "vvvvvvvvvv" + "v" * len(late) + ">hvvhhhh",
+        [((count, SLOT // 2, 3 * LANES), BF), ((blocks + 4 * halo, rhs, order), F32), field]
         + [((rhs, halo * order), BF)] * 4,
         (
-            pltpu.VMEM((count, 2 * SLOT, LANES), BF),
+            pltpu.VMEM((count, SLOT // 2, 3 * LANES), BF),
             pltpu.VMEM((4, rhs, halo * order), BF),
             cols,
             sends,
@@ -413,7 +420,7 @@
     slots, scaled, second, residual, image = call(
         second_kernel,
         (tile_cols, arrived, coarse_rows, bases, local, update, image, right, blocks_of_a, *late, *nexts),
-        "hvvvvvvvv" + "v" * (len(late) + len(nexts)) + ">vvvvv",
+        "vvvvvvvvv" + "v" * (len(late) + len(nexts)) + ">vvvvv",
         [((count, 1, LANES), F32)] + [field] * 4,
         (cols, extended, sems(1)),
     )

time: 45.7 us -> 45.3 us (level)
  local copies, waits for them, and re-layouts: 0.64 us -> 0 us
    unnamed x2 -> x0, local copies, waits for them, and re-layouts: 0.64 us -> none
    ppermute x8, waiting for transfers between devices: 3.98 us -> 4.53 us  [swap(): return lax.ppermute(value, AXES, pairs)]
where the time goes in v5:
time: 45.3 us; the launch traced here: 45 us
  starting transfers between devices  19.5 us (43%)
  blocking collectives  9.65 us (21%)
  Pallas kernels  9.6 us (21%)
  waiting for transfers between devices  5.51 us (12%)
  between operations  0.69 us (2%)
    all_to_all x2, starting transfers between devices, exchange(): return lax.all_to_all(slots, AXES, 0, 0, tiled=True)  11.1 us
    all_to_all x1, blocking collectives, exchange(): return lax.all_to_all(slots, AXES, 0, 0, tiled=True)  9.65 us
    pallas_call x6, Pallas kernels, call(): pl.pallas_call(kernel, out_shape=[pltpu.HBM(shape, dtype) if p == 'h' els...  9.6 us
    ppermute x8, starting transfers between devices, swap(): return lax.ppermute(value, AXES, pairs)  8.42 us
    ppermute x8, waiting for transfers between devices, swap(): return lax.ppermute(value, AXES, pairs)  4.53 us
    all_to_all x2, waiting for transfers between devices, exchange(): return lax.all_to_all(slots, AXES, 0, 0, tiled=True)  0.99 us
  transfers between devices with their start and end apart: 10, of which 5 were waited for; matrix products, arithmetic and copies ran while one was open for 0% of the time, Pallas kernels for 4%

profile of v5, /device:TPU:0, one launch (start us, length us, event | category | flops | bytes accessed | tf_op | source)
XLA Modules:
  0.0 45.0 jit_solution(17148056350560461152)
XLA Ops:
  0.6 2.5 %start_kernel.1 = (bf16[32,8,128]{2,1,0:T(8,128)(2,1)}, f32[8,32,128]{2,1,0:T(8,128)S(1)}, bf16[8,128,128]{2,1,0:T(8,128)(2,1)S(1)}, bf16[8,32,128]{2,1,0:T(8,12...) custom-call(s32[2,4]{1,0:T(2,128)} %bitcast.1, ...), custom_call_target="tpu_custom_call" | custom-call | tf_op jit(solution)/shard_map/start_kernel/pallas_call | solution.py:317
  3.1 0.5 %collective-permute-start = (bf16[32,1536]{1,0:T(8,128)(2,1)}, bf16[32,1536]{1,0:T(8,128)(2,1)S(1)}, u32[]{:S(2)}, u32[]{:S(2)}) collective-permute-start(bf16[32,1536]{1,0:T(8,128)(2,1)} %get-tuple-element.34), channel_id=1, source_target_pairs={{0,4},{1,2},{2,1},{3,7},{4,0},{5,6},{6,5},{7,3},{8,12},{9,10},{10,... | collective-permute-start | bytes 294920 | tf_op jit(solution)/shard_map/ppermute | solution.py:31
  3.6 7.4 %all-to-all-start = ((bf16[32,8,128]{2,1,0:T(8,128)(2,1)}), bf16[32,8,128]{2,1,0:T(8,128)(2,1)S(1)}, u32[]{:S(2)}, u32[]{:S(2)}) async-start(bf16[32,8,128]{2,1,0:T(8,128)(2,1)} %get-tuple-element.37), calls=%async_computation | async-start | bytes 131072 | tf_op jit(solution)/shard_map/all_to_all | solution.py:333
  11.0 1.8 %collective-permute-start.1 = (bf16[32,1536]{1,0:T(8,128)(2,1)}, bf16[32,1536]{1,0:T(8,128)(2,1)S(1)}, u32[]{:S(2)}, u32[]{:S(2)}) collective-permute-start(bf16[32,1536]{1,0:T(8,128)(2,1)} %get-tuple-element.43), channel_id=1, source_target_pairs={{0,2},{1,3},{2,0},{3,1},{4,8},{5,9},{6,10},{7,11},{8,4},{9,5},{10,... | collective-permute-start | bytes 294920 | tf_op jit(solution)/shard_map/ppermute | solution.py:31
  12.8 1.5 %collective-permute-start.2 = (bf16[32,1536]{1,0:T(8,128)(2,1)}, bf16[32,1536]{1,0:T(8,128)(2,1)S(1)}, u32[]{:S(2)}, u32[]{:S(2)}) collective-permute-start(bf16[32,1536]{1,0:T(8,128)(2,1)} %get-tuple-element.44), channel_id=1, source_target_pairs={{0,1},{1,0},{2,3},{3,2},{4,5},{5,4},{6,7},{7,6},{8,9},{9,8},{10,11... | collective-permute-start | bytes 294920 | tf_op jit(solution)/shard_map/ppermute | solution.py:31
  14.3 0.0 collective-permute-start.3
  14.3 0.0 collective-permute-done.refs_0_
  14.3 1.8 %gather_kernel.1 = (bf16[64,1024]{1,0:T(8,128)(2,1)S(1)}, bf16[10,32,128]{2,1,0:T(8,128)(2,1)S(1)}, bf16[2,32,128]{2,1,0:T(8,128)(2,1)S(1)}, bf16[8,7,128,128]{3...) custom-call(bf16[32,1024]{1,0:T(8,128)(2,1)S(1)} %get-tuple-element.30.inverse_ref, ...), custom_call_target="tpu_custom_call" | custom-call | flops 99999997952 | tf_op jit(solution)/shard_map/gather_kernel/pallas_call | solution.py:317
  16.1 0.0 collective-permute-done.1.refs_0_
  16.1 2.1 %collective-permute-done.2.refs_1_ = bf16[32,1536]{1,0:T(8,128)(2,1)S(1)} collective-permute-done((bf16[32,1536]{1,0:T(8,128)(2,1)}, bf16[32,1536]{1,0:T(8,128)(2,1)S(1)}, u32[]{:S(2)}, u32[]{:S(2)}) %collective-permute-start.2) | collective-permute-done | bytes 98336 | tf_op jit(solution)/shard_map/ppermute | solution.py:31
  18.2 0.0 collective-permute-done.3.refs_2_
  18.2 0.3 all-to-all-done.arrived_ref
  18.5 2.4 %first_kernel.1 = (bf16[32,4,384]{2,1,0:T(4,128)(2,1)}, f32[16,32,128]{2,1,0:T(8,128)S(1)}, f32[8,32,128]{2,1,0:T(8,128)S(1)}, bf16[32,256]{1,0:T(8,128)(2,1)}, ...) custom-call(s32[8,6]{1,0:T(8,128)S(1)} %get-tuple-element.35.cols_vmem, ...), custom_call_target="tpu_custom_call" | custom-call | tf_op jit(solution)/shard_map/first_kernel/pallas_call | solution.py:317
  20.9 3.7 %all-to-all-start.1 = ((bf16[32,4,384]{2,1,0:T(4,128)(2,1)}), bf16[32,4,384]{2,1,0:T(4,128)(2,1)S(1)}, u32[]{:S(2)}, u32[]{:S(2)}) async-start(bf16[32,4,384]{2,1,0:T(4,128)(2,1)} %get-tuple-element.46), calls=%async_computation.1 | async-start | bytes 196608 | tf_op jit(solution)/shard_map/all_to_all | solution.py:333
  24.6 0.3 collective-permute-start.4
  25.0 3.0 %collective-permute-start.5 = (bf16[32,256]{1,0:T(8,128)(2,1)}, bf16[32,256]{1,0:T(8,128)(2,1)S(1)}, u32[]{:S(2)}, u32[]{:S(2)}) collective-permute-start(bf16[32,256]{1,0:T(8,128)(2,1)} %get-tuple-element.50), channel_id=1, source_target_pairs={{0,2},{1,3},{2,0},{3,1},{4,8},{5,9},{6,10},{7,11},{8,4},{9,5},{10,... | collective-permute-start | bytes 49160 | tf_op jit(solution)/shard_map/ppermute | solution.py:31
  27.9 0.2 collective-permute-start.6
  28.1 1.2 %collective-permute-start.7 = (bf16[32,256]{1,0:T(8,128)(2,1)}, bf16[32,256]{1,0:T(8,128)(2,1)S(1)}, u32[]{:S(2)}, u32[]{:S(2)}) collective-permute-start(bf16[32,256]{1,0:T(8,128)(2,1)} %get-tuple-element.52), channel_id=1, source_target_pairs={{0,4},{1,5},{2,6},{3,7},{4,0},{5,1},{6,2},{7,3},{8,12},{9,13},{10,... | collective-permute-start | bytes 49160 | tf_op jit(solution)/shard_map/ppermute | solution.py:31
  29.2 0.3 local_kernel.1.local_ref
  29.5 0.0 collective-permute-done.4.refs_3_
  29.5 0.4 collective-permute-done.5.refs_4_
  29.9 2.0 %collective-permute-done.6.refs_5_ = bf16[32,256]{1,0:T(8,128)(2,1)S(1)} collective-permute-done((bf16[32,256]{1,0:T(8,128)(2,1)}, bf16[32,256]{1,0:T(8,128)(2,1)S(1)}, u32[]{:S(2)}, u32[]{:S(2)}) %collective-permute-start.6) | collective-permute-done | bytes 16416 | tf_op jit(solution)/shard_map/ppermute | solution.py:31
  31.9 0.0 collective-permute-done.7.refs_6_
  31.9 0.7 %all-to-all-done.1.arrived_ref = bf16[32,4,384]{2,1,0:T(4,128)(2,1)S(1)} async-done(((bf16[32,4,384]{2,1,0:T(4,128)(2,1)}), bf16[32,4,384]{2,1,0:T(4,128)(2,1)S(1)}, u32[]{:S(2)}, u32[]{:S(2)}) %all-to-all-start.1) | async-done | bytes 98336 | tf_op jit(solution)/shard_map/all_to_all | solution.py:333
  32.6 1.9 %second_kernel.1 = (f32[32,1,128]{2,1,0:T(1,128)S(1)}, f32[8,32,128]{2,1,0:T(8,128)S(1)}, f32[8,32,128]{2,1,0:T(8,128)S(1)}, f32[8,32,128]{2,1,0:T(8,128)S(1)}, f32[8,32,128]{2,1,0:T(8,128)S(1)}) custom-call(s32[8,6]{1,0:T(8,128)S(1)} %get-tuple-element.35.cols_vmem, bf16[32,4,384]{2,1,0:T(4,128)(2,1)S(1)} %all-to-all-done.1.arrived_ref, ...), custom_call_target="tpu_custom_call" | custom-call | tf_op jit(solution)/shard_map/second_kernel/pallas_call | solution.py:317
  34.5 9.7 %all_to_all.15.arrived_ref = f32[32,1,128]{2,1,0:T(1,128)S(1)} all-to-all(f32[32,1,128]{2,1,0:T(1,128)S(1)} %get-tuple-element.53), channel_id=1, replica_groups=mesh['sx'=8,'sy'=4] {'sx','sy'}, dimensions={0} | all-to-all | bytes 32768 | tf_op jit(solution)/shard_map/all_to_all | solution.py:333
  44.1 0.8 %last_kernel.1 = (f32[8,32,128]{2,1,0:T(8,128)}, f32[8,32,128]{2,1,0:T(8,128)}) custom-call(f32[32,1,128]{2,1,0:T(1,128)S(1)} %all_to_all.15.arrived_ref, f32[8,32,128]{2,1,0:T(8,128)S(1)} %get-tuple-element.54.scaled_ref, f32[8,32,128]{2,1,0:T(8,128)S(1)} %get-tuple-element.55.second_ref, f32[8,32,128]{2,1,0:T(8,128)S(1)} %get-tuple-element.56.residual_ref, ...), custom_call_target="tpu_custom_call" | custom-call | tf_op jit(solution)/shard_map/last_kernel/pallas_call | solution.py:317
Async XLA Ops:
  3.1 11.2 %collective-permute-start = (bf16[32,1536]{1,0:T(8,128)(2,1)}, bf16[32,1536]{1,0:T(8,128)(2,1)S(1)}, u32[]{:S(2)}, u32[]{:S(2)}) collective-permute-start(bf16[32,1536]{1,0:T(8,128)(2,1)} %get-tuple-element.34), channel_id=1, source_target_pairs={{0,4},{1,2},{2,1},{3,7},{4,0},{5,6},{6,5},{7,3},{8,12},{9,10},{10,... | collective-permute-start | bytes 294920 | tf_op jit(solution)/shard_map/ppermute | solution.py:31
  3.6 14.9 %all-to-all-start = ((bf16[32,8,128]{2,1,0:T(8,128)(2,1)}), bf16[32,8,128]{2,1,0:T(8,128)(2,1)S(1)}, u32[]{:S(2)}, u32[]{:S(2)}) async-start(bf16[32,8,128]{2,1,0:T(8,128)(2,1)} %get-tuple-element.37), calls=%async_computation | async-start | bytes 131072 | tf_op jit(solution)/shard_map/all_to_all | solution.py:333
  11.0 5.1 %collective-permute-start.1 = (bf16[32,1536]{1,0:T(8,128)(2,1)}, bf16[32,1536]{1,0:T(8,128)(2,1)S(1)}, u32[]{:S(2)}, u32[]{:S(2)}) collective-permute-start(bf16[32,1536]{1,0:T(8,128)(2,1)} %get-tuple-element.43), channel_id=1, source_target_pairs={{0,2},{1,3},{2,0},{3,1},{4,8},{5,9},{6,10},{7,11},{8,4},{9,5},{10,... | collective-permute-start | bytes 294920 | tf_op jit(solution)/shard_map/ppermute | solution.py:31
  12.8 5.4 %collective-permute-start.2 = (bf16[32,1536]{1,0:T(8,128)(2,1)}, bf16[32,1536]{1,0:T(8,128)(2,1)S(1)}, u32[]{:S(2)}, u32[]{:S(2)}) collective-permute-start(bf16[32,1536]{1,0:T(8,128)(2,1)} %get-tuple-element.44), channel_id=1, source_target_pairs={{0,1},{1,0},{2,3},{3,2},{4,5},{5,4},{6,7},{7,6},{8,9},{9,8},{10,11... | collective-permute-start | bytes 294920 | tf_op jit(solution)/shard_map/ppermute | solution.py:31
  14.3 3.9 %collective-permute-start.3 = (bf16[32,1536]{1,0:T(8,128)(2,1)}, bf16[32,1536]{1,0:T(8,128)(2,1)S(1)}, u32[]{:S(2)}, u32[]{:S(2)}) collective-permute-start(bf16[32,1536]{1,0:T(8,128)(2,1)} %get-tuple-element.45), channel_id=1, source_target_pairs={{0,4},{1,5},{2,6},{3,7},{4,0},{5,1},{6,2},{7,3},{8,12},{9,13},{10,... | collective-permute-start | bytes 294920 | tf_op jit(solution)/shard_map/ppermute | solution.py:31
  20.9 11.7 %all-to-all-start.1 = ((bf16[32,4,384]{2,1,0:T(4,128)(2,1)}), bf16[32,4,384]{2,1,0:T(4,128)(2,1)S(1)}, u32[]{:S(2)}, u32[]{:S(2)}) async-start(bf16[32,4,384]{2,1,0:T(4,128)(2,1)} %get-tuple-element.46), calls=%async_computation.1 | async-start | bytes 196608 | tf_op jit(solution)/shard_map/all_to_all | solution.py:333
  24.6 4.9 %collective-permute-start.4 = (bf16[32,256]{1,0:T(8,128)(2,1)}, bf16[32,256]{1,0:T(8,128)(2,1)S(1)}, u32[]{:S(2)}, u32[]{:S(2)}) collective-permute-start(bf16[32,256]{1,0:T(8,128)(2,1)} %get-tuple-element.49), channel_id=1, source_target_pairs={{0,4},{1,2},{2,1},{3,7},{4,0},{5,6},{6,5},{7,3},{8,12},{9,10},{10,... | collective-permute-start | bytes 49160 | tf_op jit(solution)/shard_map/ppermute | solution.py:31
  25.0 4.9 %collective-permute-start.5 = (bf16[32,256]{1,0:T(8,128)(2,1)}, bf16[32,256]{1,0:T(8,128)(2,1)S(1)}, u32[]{:S(2)}, u32[]{:S(2)}) collective-permute-start(bf16[32,256]{1,0:T(8,128)(2,1)} %get-tuple-element.50), channel_id=1, source_target_pairs={{0,2},{1,3},{2,0},{3,1},{4,8},{5,9},{6,10},{7,11},{8,4},{9,5},{10,... | collective-permute-start | bytes 49160 | tf_op jit(solution)/shard_map/ppermute | solution.py:31
  27.9 4.0 %collective-permute-start.6 = (bf16[32,256]{1,0:T(8,128)(2,1)}, bf16[32,256]{1,0:T(8,128)(2,1)S(1)}, u32[]{:S(2)}, u32[]{:S(2)}) collective-permute-start(bf16[32,256]{1,0:T(8,128)(2,1)} %get-tuple-element.51), channel_id=1, source_target_pairs={{0,1},{1,0},{2,3},{3,2},{4,5},{5,4},{6,7},{7,6},{8,9},{9,8},{10,11... | collective-permute-start | bytes 49160 | tf_op jit(solution)/shard_map/ppermute | solution.py:31
  28.1 3.8 %collective-permute-start.7 = (bf16[32,256]{1,0:T(8,128)(2,1)}, bf16[32,256]{1,0:T(8,128)(2,1)S(1)}, u32[]{:S(2)}, u32[]{:S(2)}) collective-permute-start(bf16[32,256]{1,0:T(8,128)(2,1)} %get-tuple-element.52), channel_id=1, source_target_pairs={{0,4},{1,5},{2,6},{3,7},{4,0},{5,1},{6,2},{7,3},{8,12},{9,13},{10,... | collective-permute-start | bytes 49160 | tf_op jit(solution)/shard_map/ppermute | solution.py:31

commit v6 on v5

--- a/solution.py
+++ b/solution.py
@@ -82,16 +82,30 @@
     return both[:rows] + both[rows:]
 
 
-def image_block(b, extended, tiles, cols_ref):
-    vectors = [extended[b]] + [extended[cols_ref[b, t]] for t in range(tiles.shape[1] - 1)]
-    blocks = [tiles[b, t] for t in range(tiles.shape[1])]
-    return lax.dot_general(
-        jnp.concatenate(vectors, axis=1), jnp.concatenate(blocks, axis=1), NT, preferred_element_type=F32
-    )
+def image_blocks(extended, tiles, cols):
+    blocks, width = tiles.shape[:2]
+    rhs, order = extended.shape[1:]
+    images = []
+    for b in range(0, blocks, 2):
+        pair = range(b, min(b + 2, blocks))
+        vectors = [
+            jnp.concatenate([extended[x]] + [extended[cols[x, t]] for t in range(width - 1)], axis=1) for x in pair
+        ]
+        rows = [jnp.concatenate([tiles[x, t] for t in range(width)], axis=1) for x in pair]
+        both = lax.dot_general(
+            jnp.concatenate(vectors, axis=0), jnp.concatenate(rows, axis=0), NT, preferred_element_type=F32
+        )
+        for k in range(len(pair)):
+            images.append(both[rhs * k : rhs * (k + 1), order * k : order * (k + 1)])
+    return images
 
 
 def sums_row(upper, lower):
     return jnp.sum(jnp.concatenate([upper, lower, upper, lower], axis=0).T, axis=0, keepdims=True)
+
+
+def chosen(sends, m, direction):
+    return sum(jnp.where(direction == k, sends[m, k], 0) for k in range(sends.shape[1]))
 
 
 def fetch(pairs, sems):
@@ -193,15 +207,15 @@
 
 
 def first_kernel(
-    cols_vmem, send_vmem, arrived_ref, inverses_ref, bases_ref, local_ref, locals_ref, block_inverse_ref, right_ref,
+    cols_ref, send_ref, arrived_ref, inverses_ref, bases_ref, local_ref, locals_ref, block_inverse_ref, right_ref,
     tiles_ref, *refs,
 ):
     late, refs = refs[: 4 - EARLY[0]], refs[4 - EARLY[0] :]
     slot_hbm, update_ref, image_ref, out0, out1, out2, out3 = refs[:7]
-    slot_ref, out_ref, cols_ref, send_ref, extended, sems, out_sems = refs[7:]
-    copies = fetch([(cols_vmem, cols_ref), (send_vmem, send_ref)], sems)
+    slot_ref, out_ref, extended, out_sems = refs[7:]
+    cols, sends = cols_ref[...], send_ref[...]
     blocks, rhs, order = right_ref.shape
-    halo = send_ref.shape[0]
+    halo = sends.shape[0]
     total = inverses_ref.shape[1]
     coarse = coarse_parts(arrived_ref[...], all_inverses(inverses_ref, late))
     early = blocks + halo * EARLY[0]
@@ -218,14 +232,10 @@
         update = local + jnp.dot(coarse[owner(k, blocks, halo)], basis, preferred_element_type=F32)
         update_ref[k] = update
         pack(extended, k, update, blocks, halo)
-    for copy in copies:
-        copy.wait()
     upper = lower = jnp.zeros((rhs, order), F32)
-    images = []
-    for b in range(blocks):
-        image = image_block(b, extended, tiles_ref, cols_ref)
+    images = image_blocks(extended, tiles_ref, cols)
+    for b, image in enumerate(images):
         image_ref[b] = image
-        images.append(image)
         upper += right_ref[b] * image
         lower += image * image
     row = sums_row(upper, lower)
@@ -240,7 +250,7 @@
     for q, ((number, odd), out_hbm) in enumerate(zip(SWAPS, (out0, out1, out2, out3))):
         send, _, _ = swap_ends(number, odd)
         for m in range(halo):
-            row = send_ref[m, send]
+            row = chosen(sends, m, send)
             local = local_product(image_ref[row], block_inverse_ref[row])
             out_ref[q, :, m * order : (m + 1) * order] = local.astype(BF)
         leaving += fetch([(out_ref.at[q], out_hbm)], out_sems.at[pl.ds(1 + q, 1)])
@@ -260,12 +270,12 @@
 
 
 def second_kernel(
-    cols_vmem, arrived_ref, inverses_ref, bases_ref, local_ref, update_ref, image_ref, right_ref, tiles_ref, *refs,
+    cols_ref, arrived_ref, inverses_ref, bases_ref, local_ref, update_ref, image_ref, right_ref, tiles_ref, *refs,
 ):
     late, refs = refs[: 4 - EARLY[0]], refs[4 - EARLY[0] :]
     nexts, refs = refs[: 4 - EARLY[1]], refs[4 - EARLY[1] :]
-    slot_ref, scaled_ref, second_ref, residual_ref, image2_ref, cols_ref, extended, sems = refs
-    (copy,) = fetch([(cols_vmem, cols_ref)], sems)
+    slot_ref, scaled_ref, second_ref, residual_ref, image2_ref, extended = refs
+    cols = cols_ref[...]
     blocks, rhs, order = right_ref.shape
     halo = (update_ref.shape[0] - blocks) // 4
     total = inverses_ref.shape[1]
@@ -289,12 +299,10 @@
             scaled_ref[k] = weight * update
             second_ref[k] = second
         pack(extended, k, second, blocks, halo)
-    copy.wait()
     upper = lower = jnp.zeros((rhs, order), F32)
-    for b in range(blocks):
+    for b, image in enumerate(image_blocks(extended, tiles_ref, cols)):
         residual = right_ref[b] - weight * image_ref[b]
         residual_ref[b] = residual
-        image = image_block(b, extended, tiles_ref, cols_ref)
         image2_ref[b] = image
         upper += residual * image
         lower += image * image
@@ -339,7 +347,6 @@
     halo = send_rows.shape[1]
     count = lax.axis_size("sx") * lax.axis_size("sy")
     field = (right_sides.shape, F32)
-    cols = pltpu.SMEM(tile_cols.shape, jnp.int32)
     sends = pltpu.SMEM((halo, send_rows.shape[0]), jnp.int32)
     turned_sends = send_rows.T
     extended = pltpu.VMEM((blocks + 4 * halo, rhs, order), BF)
@@ -400,10 +407,7 @@
         (
             pltpu.VMEM((count, SLOT // 2, 3 * LANES), BF),
             pltpu.VMEM((4, rhs, halo * order), BF),
-            cols,
-            sends,
             extended,
-            sems(2),
             sems(5),
         ),
     )
@@ -422,7 +426,7 @@
         (tile_cols, arrived, coarse_rows, bases, local, update, image, right, blocks_of_a, *late, *nexts),
         "vvvvvvvvv" + "v" * (len(late) + len(nexts)) + ">vvvvv",
         [((count, 1, LANES), F32)] + [field] * 4,
-        (cols, extended, sems(1)),
+        (extended,),
     )
     return tuple(call(last_kernel, (exchange(slots), scaled, second, residual, image), "vvvvv>vv", [field] * 2))
 

time: 45.3 us -> 44.4 us (0.980)
  Pallas kernels: 9.6 us -> 8.75 us
    pallas_call x6, Pallas kernels: 9.6 us -> 8.75 us  [call(): pl.pallas_call(kernel, out_shape=[pltpu.HBM(shape, dtype) if p == 'h' els...]
  transfers between devices with their start and end apart: 10 -> 10, of which waited for: 5 -> 5; matrix products, arithmetic and copies ran while one was open for 0% -> 0% of each run, Pallas kernels for 4% -> 5%
where the time goes in v6:
time: 44.4 us; the launch traced here: 44.1 us
  starting transfers between devices  19.5 us (44%)
  blocking collectives  9.65 us (22%)
  Pallas kernels  8.75 us (20%)
  waiting for transfers between devices  5.51 us (12%)
  between operations  0.69 us (2%)
    all_to_all x2, starting transfers between devices, exchange(): return lax.all_to_all(slots, AXES, 0, 0, tiled=True)  11.1 us
    all_to_all x1, blocking collectives, exchange(): return lax.all_to_all(slots, AXES, 0, 0, tiled=True)  9.65 us
    pallas_call x6, Pallas kernels, call(): pl.pallas_call(kernel, out_shape=[pltpu.HBM(shape, dtype) if p == 'h' els...  8.75 us
    ppermute x8, starting transfers between devices, swap(): return lax.ppermute(value, AXES, pairs)  8.42 us
    ppermute x8, waiting for transfers between devices, swap(): return lax.ppermute(value, AXES, pairs)  4.53 us
    all_to_all x2, waiting for transfers between devices, exchange(): return lax.all_to_all(slots, AXES, 0, 0, tiled=True)  0.99 us
  transfers between devices with their start and end apart: 10, of which 5 were waited for; matrix products, arithmetic and copies ran while one was open for 0% of the time, Pallas kernels for 5%

profile of v6, /device:TPU:0, one launch (start us, length us, event | category | flops | bytes accessed | tf_op | source)
XLA Modules:
  0.0 44.1 jit_solution(6851176802010514667)
XLA Ops:
  0.6 2.5 %start_kernel.1 = (bf16[32,8,128]{2,1,0:T(8,128)(2,1)}, f32[8,32,128]{2,1,0:T(8,128)S(1)}, bf16[8,128,128]{2,1,0:T(8,128)(2,1)S(1)}, bf16[8,32,128]{2,1,0:T(8,12...) custom-call(s32[2,4]{1,0:T(2,128)} %bitcast.1, ...), custom_call_target="tpu_custom_call" | custom-call | tf_op jit(solution)/shard_map/start_kernel/pallas_call | solution.py:325
  3.1 0.5 %collective-permute-start = (bf16[32,1536]{1,0:T(8,128)(2,1)}, bf16[32,1536]{1,0:T(8,128)(2,1)S(1)}, u32[]{:S(2)}, u32[]{:S(2)}) collective-permute-start(bf16[32,1536]{1,0:T(8,128)(2,1)} %get-tuple-element.34), channel_id=1, source_target_pairs={{0,4},{1,2},{2,1},{3,7},{4,0},{5,6},{6,5},{7,3},{8,12},{9,10},{10,... | collective-permute-start | bytes 294920 | tf_op jit(solution)/shard_map/ppermute | solution.py:31
  3.6 7.4 %all-to-all-start = ((bf16[32,8,128]{2,1,0:T(8,128)(2,1)}), bf16[32,8,128]{2,1,0:T(8,128)(2,1)S(1)}, u32[]{:S(2)}, u32[]{:S(2)}) async-start(bf16[32,8,128]{2,1,0:T(8,128)(2,1)} %get-tuple-element.37), calls=%async_computation | async-start | bytes 131072 | tf_op jit(solution)/shard_map/all_to_all | solution.py:341
  11.0 1.8 %collective-permute-start.1 = (bf16[32,1536]{1,0:T(8,128)(2,1)}, bf16[32,1536]{1,0:T(8,128)(2,1)S(1)}, u32[]{:S(2)}, u32[]{:S(2)}) collective-permute-start(bf16[32,1536]{1,0:T(8,128)(2,1)} %get-tuple-element.43), channel_id=1, source_target_pairs={{0,2},{1,3},{2,0},{3,1},{4,8},{5,9},{6,10},{7,11},{8,4},{9,5},{10,... | collective-permute-start | bytes 294920 | tf_op jit(solution)/shard_map/ppermute | solution.py:31
  12.8 1.5 %collective-permute-start.2 = (bf16[32,1536]{1,0:T(8,128)(2,1)}, bf16[32,1536]{1,0:T(8,128)(2,1)S(1)}, u32[]{:S(2)}, u32[]{:S(2)}) collective-permute-start(bf16[32,1536]{1,0:T(8,128)(2,1)} %get-tuple-element.44), channel_id=1, source_target_pairs={{0,1},{1,0},{2,3},{3,2},{4,5},{5,4},{6,7},{7,6},{8,9},{9,8},{10,11... | collective-permute-start | bytes 294920 | tf_op jit(solution)/shard_map/ppermute | solution.py:31
  14.3 0.0 collective-permute-start.3
  14.3 0.0 collective-permute-done.refs_0_
  14.3 1.8 %gather_kernel.1 = (bf16[64,1024]{1,0:T(8,128)(2,1)S(1)}, bf16[10,32,128]{2,1,0:T(8,128)(2,1)S(1)}, bf16[2,32,128]{2,1,0:T(8,128)(2,1)S(1)}, bf16[8,7,128,128]{3...) custom-call(bf16[32,1024]{1,0:T(8,128)(2,1)S(1)} %get-tuple-element.30.inverse_ref, ...), custom_call_target="tpu_custom_call" | custom-call | flops 99999997952 | tf_op jit(solution)/shard_map/gather_kernel/pallas_call | solution.py:325
  16.1 0.0 collective-permute-done.1.refs_0_
  16.1 2.1 %collective-permute-done.2.refs_1_ = bf16[32,1536]{1,0:T(8,128)(2,1)S(1)} collective-permute-done((bf16[32,1536]{1,0:T(8,128)(2,1)}, bf16[32,1536]{1,0:T(8,128)(2,1)S(1)}, u32[]{:S(2)}, u32[]{:S(2)}) %collective-permute-start.2) | collective-permute-done | bytes 98336 | tf_op jit(solution)/shard_map/ppermute | solution.py:31
  18.2 0.0 collective-permute-done.3.refs_2_
  18.2 0.3 all-to-all-done.arrived_ref
  18.5 2.2 %first_kernel.1 = (bf16[32,4,384]{2,1,0:T(4,128)(2,1)}, f32[16,32,128]{2,1,0:T(8,128)S(1)}, f32[8,32,128]{2,1,0:T(8,128)S(1)}, bf16[32,256]{1,0:T(8,128)(2,1)}, ...) custom-call(s32[8,6]{1,0:T(8,128)S(1)} %get-tuple-element.35.cols_ref, ...), custom_call_target="tpu_custom_call" | custom-call | tf_op jit(solution)/shard_map/first_kernel/pallas_call | solution.py:325
  20.7 3.7 %all-to-all-start.1 = ((bf16[32,4,384]{2,1,0:T(4,128)(2,1)}), bf16[32,4,384]{2,1,0:T(4,128)(2,1)S(1)}, u32[]{:S(2)}, u32[]{:S(2)}) async-start(bf16[32,4,384]{2,1,0:T(4,128)(2,1)} %get-tuple-element.46), calls=%async_computation.1 | async-start | bytes 196608 | tf_op jit(solution)/shard_map/all_to_all | solution.py:341
  24.4 0.3 collective-permute-start.4
  24.7 3.0 %collective-permute-start.5 = (bf16[32,256]{1,0:T(8,128)(2,1)}, bf16[32,256]{1,0:T(8,128)(2,1)S(1)}, u32[]{:S(2)}, u32[]{:S(2)}) collective-permute-start(bf16[32,256]{1,0:T(8,128)(2,1)} %get-tuple-element.50), channel_id=1, source_target_pairs={{0,2},{1,3},{2,0},{3,1},{4,8},{5,9},{6,10},{7,11},{8,4},{9,5},{10,... | collective-permute-start | bytes 49160 | tf_op jit(solution)/shard_map/ppermute | solution.py:31
  27.7 0.2 collective-permute-start.6
  27.9 1.2 %collective-permute-start.7 = (bf16[32,256]{1,0:T(8,128)(2,1)}, bf16[32,256]{1,0:T(8,128)(2,1)S(1)}, u32[]{:S(2)}, u32[]{:S(2)}) collective-permute-start(bf16[32,256]{1,0:T(8,128)(2,1)} %get-tuple-element.52), channel_id=1, source_target_pairs={{0,4},{1,5},{2,6},{3,7},{4,0},{5,1},{6,2},{7,3},{8,12},{9,13},{10,... | collective-permute-start | bytes 49160 | tf_op jit(solution)/shard_map/ppermute | solution.py:31
  29.0 0.3 local_kernel.1.local_ref
  29.3 0.0 collective-permute-done.4.refs_3_
  29.3 0.4 collective-permute-done.5.refs_4_
  29.7 2.0 %collective-permute-done.6.refs_5_ = bf16[32,256]{1,0:T(8,128)(2,1)S(1)} collective-permute-done((bf16[32,256]{1,0:T(8,128)(2,1)}, bf16[32,256]{1,0:T(8,128)(2,1)S(1)}, u32[]{:S(2)}, u32[]{:S(2)}) %collective-permute-start.6) | collective-permute-done | bytes 16416 | tf_op jit(solution)/shard_map/ppermute | solution.py:31
  31.7 0.0 collective-permute-done.7.refs_6_
  31.7 0.7 %all-to-all-done.1.arrived_ref = bf16[32,4,384]{2,1,0:T(4,128)(2,1)S(1)} async-done(((bf16[32,4,384]{2,1,0:T(4,128)(2,1)}), bf16[32,4,384]{2,1,0:T(4,128)(2,1)S(1)}, u32[]{:S(2)}, u32[]{:S(2)}) %all-to-all-start.1) | async-done | bytes 98336 | tf_op jit(solution)/shard_map/all_to_all | solution.py:341
  32.4 1.2 %second_kernel.1 = (f32[32,1,128]{2,1,0:T(1,128)S(1)}, f32[8,32,128]{2,1,0:T(8,128)S(1)}, f32[8,32,128]{2,1,0:T(8,128)S(1)}, f32[8,32,128]{2,1,0:T(8,128)S(1)}, f32[8,32,128]{2,1,0:T(8,128)S(1)}) custom-call(s32[8,6]{1,0:T(8,128)S(1)} %get-tuple-element.35.cols_ref, bf16[32,4,384]{2,1,0:T(4,128)(2,1)S(1)} %all-to-all-done.1.arrived_ref, ...), custom_call_target="tpu_custom_call" | custom-call | tf_op jit(solution)/shard_map/second_kernel/pallas_call | solution.py:325
  33.6 9.7 %all_to_all.15.arrived_ref = f32[32,1,128]{2,1,0:T(1,128)S(1)} all-to-all(f32[32,1,128]{2,1,0:T(1,128)S(1)} %get-tuple-element.53), channel_id=1, replica_groups=mesh['sx'=8,'sy'=4] {'sx','sy'}, dimensions={0} | all-to-all | bytes 32768 | tf_op jit(solution)/shard_map/all_to_all | solution.py:341
  43.3 0.8 %last_kernel.1 = (f32[8,32,128]{2,1,0:T(8,128)}, f32[8,32,128]{2,1,0:T(8,128)}) custom-call(f32[32,1,128]{2,1,0:T(1,128)S(1)} %all_to_all.15.arrived_ref, f32[8,32,128]{2,1,0:T(8,128)S(1)} %get-tuple-element.54.scaled_ref, f32[8,32,128]{2,1,0:T(8,128)S(1)} %get-tuple-element.55.second_ref, f32[8,32,128]{2,1,0:T(8,128)S(1)} %get-tuple-element.56.residual_ref, ...), custom_call_target="tpu_custom_call" | custom-call | tf_op jit(solution)/shard_map/last_kernel/pallas_call | solution.py:325
Async XLA Ops:
  3.1 11.2 %collective-permute-start = (bf16[32,1536]{1,0:T(8,128)(2,1)}, bf16[32,1536]{1,0:T(8,128)(2,1)S(1)}, u32[]{:S(2)}, u32[]{:S(2)}) collective-permute-start(bf16[32,1536]{1,0:T(8,128)(2,1)} %get-tuple-element.34), channel_id=1, source_target_pairs={{0,4},{1,2},{2,1},{3,7},{4,0},{5,6},{6,5},{7,3},{8,12},{9,10},{10,... | collective-permute-start | bytes 294920 | tf_op jit(solution)/shard_map/ppermute | solution.py:31
  3.6 14.9 %all-to-all-start = ((bf16[32,8,128]{2,1,0:T(8,128)(2,1)}), bf16[32,8,128]{2,1,0:T(8,128)(2,1)S(1)}, u32[]{:S(2)}, u32[]{:S(2)}) async-start(bf16[32,8,128]{2,1,0:T(8,128)(2,1)} %get-tuple-element.37), calls=%async_computation | async-start | bytes 131072 | tf_op jit(solution)/shard_map/all_to_all | solution.py:341
  11.0 5.1 %collective-permute-start.1 = (bf16[32,1536]{1,0:T(8,128)(2,1)}, bf16[32,1536]{1,0:T(8,128)(2,1)S(1)}, u32[]{:S(2)}, u32[]{:S(2)}) collective-permute-start(bf16[32,1536]{1,0:T(8,128)(2,1)} %get-tuple-element.43), channel_id=1, source_target_pairs={{0,2},{1,3},{2,0},{3,1},{4,8},{5,9},{6,10},{7,11},{8,4},{9,5},{10,... | collective-permute-start | bytes 294920 | tf_op jit(solution)/shard_map/ppermute | solution.py:31
  12.8 5.4 %collective-permute-start.2 = (bf16[32,1536]{1,0:T(8,128)(2,1)}, bf16[32,1536]{1,0:T(8,128)(2,1)S(1)}, u32[]{:S(2)}, u32[]{:S(2)}) collective-permute-start(bf16[32,1536]{1,0:T(8,128)(2,1)} %get-tuple-element.44), channel_id=1, source_target_pairs={{0,1},{1,0},{2,3},{3,2},{4,5},{5,4},{6,7},{7,6},{8,9},{9,8},{10,11... | collective-permute-start | bytes 294920 | tf_op jit(solution)/shard_map/ppermute | solution.py:31
  14.3 3.9 %collective-permute-start.3 = (bf16[32,1536]{1,0:T(8,128)(2,1)}, bf16[32,1536]{1,0:T(8,128)(2,1)S(1)}, u32[]{:S(2)}, u32[]{:S(2)}) collective-permute-start(bf16[32,1536]{1,0:T(8,128)(2,1)} %get-tuple-element.45), channel_id=1, source_target_pairs={{0,4},{1,5},{2,6},{3,7},{4,0},{5,1},{6,2},{7,3},{8,12},{9,13},{10,... | collective-permute-start | bytes 294920 | tf_op jit(solution)/shard_map/ppermute | solution.py:31
  20.7 11.7 %all-to-all-start.1 = ((bf16[32,4,384]{2,1,0:T(4,128)(2,1)}), bf16[32,4,384]{2,1,0:T(4,128)(2,1)S(1)}, u32[]{:S(2)}, u32[]{:S(2)}) async-start(bf16[32,4,384]{2,1,0:T(4,128)(2,1)} %get-tuple-element.46), calls=%async_computation.1 | async-start | bytes 196608 | tf_op jit(solution)/shard_map/all_to_all | solution.py:341
  24.4 4.9 %collective-permute-start.4 = (bf16[32,256]{1,0:T(8,128)(2,1)}, bf16[32,256]{1,0:T(8,128)(2,1)S(1)}, u32[]{:S(2)}, u32[]{:S(2)}) collective-permute-start(bf16[32,256]{1,0:T(8,128)(2,1)} %get-tuple-element.49), channel_id=1, source_target_pairs={{0,4},{1,2},{2,1},{3,7},{4,0},{5,6},{6,5},{7,3},{8,12},{9,10},{10,... | collective-permute-start | bytes 49160 | tf_op jit(solution)/shard_map/ppermute | solution.py:31
  24.7 4.9 %collective-permute-start.5 = (bf16[32,256]{1,0:T(8,128)(2,1)}, bf16[32,256]{1,0:T(8,128)(2,1)S(1)}, u32[]{:S(2)}, u32[]{:S(2)}) collective-permute-start(bf16[32,256]{1,0:T(8,128)(2,1)} %get-tuple-element.50), channel_id=1, source_target_pairs={{0,2},{1,3},{2,0},{3,1},{4,8},{5,9},{6,10},{7,11},{8,4},{9,5},{10,... | collective-permute-start | bytes 49160 | tf_op jit(solution)/shard_map/ppermute | solution.py:31
  27.7 4.0 %collective-permute-start.6 = (bf16[32,256]{1,0:T(8,128)(2,1)}, bf16[32,256]{1,0:T(8,128)(2,1)S(1)}, u32[]{:S(2)}, u32[]{:S(2)}) collective-permute-start(bf16[32,256]{1,0:T(8,128)(2,1)} %get-tuple-element.51), channel_id=1, source_target_pairs={{0,1},{1,0},{2,3},{3,2},{4,5},{5,4},{6,7},{7,6},{8,9},{9,8},{10,11... | collective-permute-start | bytes 49160 | tf_op jit(solution)/shard_map/ppermute | solution.py:31
  27.9 3.8 %collective-permute-start.7 = (bf16[32,256]{1,0:T(8,128)(2,1)}, bf16[32,256]{1,0:T(8,128)(2,1)S(1)}, u32[]{:S(2)}, u32[]{:S(2)}) collective-permute-start(bf16[32,256]{1,0:T(8,128)(2,1)} %get-tuple-element.52), channel_id=1, source_target_pairs={{0,4},{1,5},{2,6},{3,7},{4,0},{5,1},{6,2},{7,3},{8,12},{9,13},{10,... | collective-permute-start | bytes 49160 | tf_op jit(solution)/shard_map/ppermute | solution.py:31

commit v7 on v6

--- a/solution.py
+++ b/solution.py
@@ -66,7 +66,7 @@
     count = arrived.shape[0]
     lane = lax.broadcasted_iota(jnp.int32, (1, 4, SLOT, LANES), 3) // 32
     part = lax.broadcasted_iota(jnp.int32, (1, 4, SLOT, LANES), 1)
-    spread_out = jnp.where(lane == part, arrived[:, None].astype(F32), 0.0)
+    spread_out = jnp.where(lane == part, arrived[:, None], 0.0)
     column = spread_out.reshape(count * 4 * SLOT, LANES).astype(BF)
     product = jnp.dot(inverses, column, preferred_element_type=F32)
     parts = []
@@ -104,6 +104,10 @@
     return jnp.sum(jnp.concatenate([upper, lower, upper, lower], axis=0).T, axis=0, keepdims=True)
 
 
+def repeated(slot, shape):
+    return jnp.broadcast_to(slot[None], (shape[0] // slot.shape[0],) + slot.shape).reshape(shape).astype(BF)
+
+
 def chosen(sends, m, direction):
     return sum(jnp.where(direction == k, sends[m, k], 0) for k in range(sends.shape[1]))
 
@@ -136,7 +140,7 @@
     for copy in copies[:2]:
         copy.wait()
     vectors = [right_ref[b] for b in range(blocks)]
-    slot_ref[...] = jnp.broadcast_to(restrict_slot(vectors, basis_ref).astype(BF)[None], slot_ref.shape)
+    slot_ref[...] = repeated(restrict_slot(vectors, basis_ref), slot_ref.shape)
     leaving = fetch([(slot_ref, slot_hbm)], out_sems)
     copies[3].wait()
     inverse = wide[...].astype(BF)
@@ -217,7 +221,8 @@
     blocks, rhs, order = right_ref.shape
     halo = sends.shape[0]
     total = inverses_ref.shape[1]
-    coarse = coarse_parts(arrived_ref[...], all_inverses(inverses_ref, late))
+    arrived = arrived_ref[...].astype(F32).reshape(-1, SLOT, LANES)
+    coarse = coarse_parts(arrived, all_inverses(inverses_ref, late))
     early = blocks + halo * EARLY[0]
     for k in range(update_ref.shape[0]):
         basis = basis_block(k, bases_ref, late, total, halo)
@@ -242,10 +247,8 @@
     high, low = split(row)
     lane = lax.broadcasted_iota(jnp.int32, (1, LANES), 1)
     row = jnp.where(lane < 64, high.astype(F32), low.astype(F32))
-    slot = restrict_slot(images, bases_ref)
-    half = SLOT // 2
-    whole = jnp.concatenate([slot[:half], slot[half:], jnp.broadcast_to(row, (half, LANES))], axis=1)
-    slot_ref[...] = jnp.broadcast_to(whole.astype(BF)[None], slot_ref.shape)
+    whole = jnp.concatenate([restrict_slot(images, bases_ref), jnp.broadcast_to(row, (SLOT, LANES))], axis=0)
+    slot_ref[...] = repeated(whole, slot_ref.shape)
     leaving = fetch([(slot_ref, slot_hbm)], out_sems)
     for q, ((number, odd), out_hbm) in enumerate(zip(SWAPS, (out0, out1, out2, out3))):
         send, _, _ = swap_ends(number, odd)
@@ -279,10 +282,9 @@
     blocks, rhs, order = right_ref.shape
     halo = (update_ref.shape[0] - blocks) // 4
     total = inverses_ref.shape[1]
-    arrived = arrived_ref[...].astype(F32)
-    restricted = jnp.concatenate([arrived[:, :, :LANES], arrived[:, :, LANES : 2 * LANES]], axis=1)
-    coarse = coarse_parts(restricted, all_inverses(inverses_ref, late))
-    sums = jnp.sum(arrived[:, :1, 2 * LANES :], axis=0)
+    arrived = arrived_ref[...].astype(F32).reshape(-1, 2 * SLOT, LANES)
+    coarse = coarse_parts(arrived[:, :SLOT], all_inverses(inverses_ref, late))
+    sums = jnp.sum(arrived[:, SLOT : SLOT + 1], axis=0)
     turned = jnp.broadcast_to(sums, (LANES, LANES)).T
     weight = (turned[:32] + turned[64:96]) / (turned[32:64] + turned[96:] + 1e-6)
     for k in range(update_ref.shape[0]):
@@ -338,7 +340,9 @@
 
 
 def exchange(slots):
-    return lax.all_to_all(slots, AXES, 0, 0, tiled=True)
+    count = lax.axis_size("sx") * lax.axis_size("sy")
+    split_up = slots.reshape(count, -1, slots.shape[-1])
+    return lax.all_to_all(split_up, AXES, 0, 0, tiled=True).reshape(slots.shape)
 
 
 def body(right_sides, tiles, tile_cols, send_rows, block_inverse, coarse_basis, coarse_inverse):
@@ -362,7 +366,7 @@
         (turned_sends, right_sides, block_inverse, coarse_basis, coarse_inverse),
         "hhhhh>hvvvvhhhh",
         [
-            ((count, SLOT, LANES), BF),
+            ((count * SLOT, LANES), BF),
             field,
             (block_inverse.shape, BF),
             (coarse_basis.shape, BF),
@@ -370,7 +374,7 @@
         ]
         + [((rhs, total + 2 * halo * order), BF)] * 4,
         (
-            pltpu.VMEM((count, SLOT, LANES), BF),
+            pltpu.VMEM((count * SLOT, LANES), BF),
             pltpu.VMEM((4, rhs, total + 2 * halo * order), BF),
             sends,
             pltpu.VMEM(coarse_inverse.shape, F32),
@@ -402,10 +406,10 @@
         first_kernel,
         (tile_cols, turned_sends, arrived, coarse_rows, bases, local, locals_, inverses, right, blocks_of_a, *late),
         "vvvvvvvvvv" + "v" * len(late) + ">hvvhhhh",
-        [((count, SLOT // 2, 3 * LANES), BF), ((blocks + 4 * halo, rhs, order), F32), field]
+        [((count * 2 * SLOT, LANES), BF), ((blocks + 4 * halo, rhs, order), F32), field]
         + [((rhs, halo * order), BF)] * 4,
         (
-            pltpu.VMEM((count, SLOT // 2, 3 * LANES), BF),
+            pltpu.VMEM((count * 2 * SLOT, LANES), BF),
             pltpu.VMEM((4, rhs, halo * order), BF),
             extended,
             sems(5),

time: 44.4 us -> 44.4 us (level)
  waiting for transfers between devices: 5.51 us -> 5.98 us
  blocking collectives: 9.65 us -> 9.2 us
    all_to_all x1, blocking collectives: 9.65 us -> 9.2 us  [exchange(): return lax.all_to_all(split_up, AXES, 0, 0, tiled=True).reshape(slots.shape)]
where the time goes in v7:
time: 44.4 us; the launch traced here: 44.1 us
  starting transfers between devices  19.5 us (44%)
  blocking collectives  9.2 us (21%)
  Pallas kernels  8.76 us (20%)
  waiting for transfers between devices  5.98 us (13%)
  between operations  0.69 us (2%)
    all_to_all x2, starting transfers between devices, exchange(): return lax.all_to_all(split_up, AXES, 0, 0, tiled=True).reshape(slots.shape)  11.1 us
    all_to_all x1, blocking collectives, exchange(): return lax.all_to_all(split_up, AXES, 0, 0, tiled=True).reshape(slots.shape)  9.2 us
    pallas_call x6, Pallas kernels, call(): pl.pallas_call(kernel, out_shape=[pltpu.HBM(shape, dtype) if p == 'h' els...  8.76 us
    ppermute x8, starting transfers between devices, swap(): return lax.ppermute(value, AXES, pairs)  8.42 us
    ppermute x8, waiting for transfers between devices, swap(): return lax.ppermute(value, AXES, pairs)  4.6 us
    all_to_all x2, waiting for transfers between devices, exchange(): return lax.all_to_all(split_up, AXES, 0, 0, tiled=True).reshape(slots.shape)  1.37 us
  transfers between devices with their start and end apart: 10, of which 5 were waited for; matrix products, arithmetic and copies ran while one was open for 0% of the time, Pallas kernels for 5%

profile of v7, /device:TPU:0, one launch (start us, length us, event | category | flops | bytes accessed | tf_op | source)
XLA Modules:
  0.0 44.1 jit_solution(10247914474623929540)
XLA Ops:
  0.6 2.5 %start_kernel.1 = (bf16[256,128]{1,0:T(8,128)(2,1)}, f32[8,32,128]{2,1,0:T(8,128)S(1)}, bf16[8,128,128]{2,1,0:T(8,128)(2,1)S(1)}, bf16[8,32,128]{2,1,0:T(8,128)(...) custom-call(s32[2,4]{1,0:T(2,128)} %bitcast.9, ...), custom_call_target="tpu_custom_call" | custom-call | tf_op jit(solution)/shard_map/start_kernel/pallas_call | solution.py:327
  3.1 0.5 %collective-permute-start = (bf16[32,1536]{1,0:T(8,128)(2,1)}, bf16[32,1536]{1,0:T(8,128)(2,1)S(1)}, u32[]{:S(2)}, u32[]{:S(2)}) collective-permute-start(bf16[32,1536]{1,0:T(8,128)(2,1)} %get-tuple-element.34), channel_id=1, source_target_pairs={{0,4},{1,2},{2,1},{3,7},{4,0},{5,6},{6,5},{7,3},{8,12},{9,10},{10,... | collective-permute-start | bytes 294920 | tf_op jit(solution)/shard_map/ppermute | solution.py:31
  3.6 7.4 %all-to-all-start = ((bf16[32,8,128]{2,1,0:T(8,128)(2,1)}), bf16[32,8,128]{2,1,0:T(8,128)(2,1)S(1)}, u32[]{:S(2)}, u32[]{:S(2)}) async-start(bf16[32,8,128]{2,1,0:T(8,128)(2,1)} %bitcast.8), calls=%async_computation | async-start | bytes 131072 | tf_op jit(solution)/shard_map/all_to_all | solution.py:345
  11.0 1.8 %collective-permute-start.1 = (bf16[32,1536]{1,0:T(8,128)(2,1)}, bf16[32,1536]{1,0:T(8,128)(2,1)S(1)}, u32[]{:S(2)}, u32[]{:S(2)}) collective-permute-start(bf16[32,1536]{1,0:T(8,128)(2,1)} %get-tuple-element.43), channel_id=1, source_target_pairs={{0,2},{1,3},{2,0},{3,1},{4,8},{5,9},{6,10},{7,11},{8,4},{9,5},{10,... | collective-permute-start | bytes 294920 | tf_op jit(solution)/shard_map/ppermute | solution.py:31
  12.8 1.5 %collective-permute-start.2 = (bf16[32,1536]{1,0:T(8,128)(2,1)}, bf16[32,1536]{1,0:T(8,128)(2,1)S(1)}, u32[]{:S(2)}, u32[]{:S(2)}) collective-permute-start(bf16[32,1536]{1,0:T(8,128)(2,1)} %get-tuple-element.44), channel_id=1, source_target_pairs={{0,1},{1,0},{2,3},{3,2},{4,5},{5,4},{6,7},{7,6},{8,9},{9,8},{10,11... | collective-permute-start | bytes 294920 | tf_op jit(solution)/shard_map/ppermute | solution.py:31
  14.3 0.0 collective-permute-start.3
  14.3 0.0 collective-permute-done.refs_0_
  14.3 1.8 %gather_kernel.1 = (bf16[64,1024]{1,0:T(8,128)(2,1)S(1)}, bf16[10,32,128]{2,1,0:T(8,128)(2,1)S(1)}, bf16[2,32,128]{2,1,0:T(8,128)(2,1)S(1)}, bf16[8,7,128,128]{3...) custom-call(bf16[32,1024]{1,0:T(8,128)(2,1)S(1)} %get-tuple-element.30.inverse_ref, ...), custom_call_target="tpu_custom_call" | custom-call | flops 99999997952 | tf_op jit(solution)/shard_map/gather_kernel/pallas_call | solution.py:327
  16.1 0.0 collective-permute-done.1.refs_0_
  16.1 2.1 %collective-permute-done.2.refs_1_ = bf16[32,1536]{1,0:T(8,128)(2,1)S(1)} collective-permute-done((bf16[32,1536]{1,0:T(8,128)(2,1)}, bf16[32,1536]{1,0:T(8,128)(2,1)S(1)}, u32[]{:S(2)}, u32[]{:S(2)}) %collective-permute-start.2) | collective-permute-done | bytes 98336 | tf_op jit(solution)/shard_map/ppermute | solution.py:31
  18.2 0.0 collective-permute-done.3.refs_2_
  18.2 0.3 all-to-all-done
  18.5 2.2 %first_kernel.1 = (bf16[512,128]{1,0:T(8,128)(2,1)}, f32[16,32,128]{2,1,0:T(8,128)S(1)}, f32[8,32,128]{2,1,0:T(8,128)S(1)}, bf16[32,256]{1,0:T(8,128)(2,1)}, bf1...) custom-call(s32[8,6]{1,0:T(8,128)S(1)} %get-tuple-element.35.cols_ref, ...), custom_call_target="tpu_custom_call" | custom-call | tf_op jit(solution)/shard_map/first_kernel/pallas_call | solution.py:327
  20.7 3.7 %all-to-all-start.1 = ((bf16[32,16,128]{2,1,0:T(8,128)(2,1)}), bf16[32,16,128]{2,1,0:T(8,128)(2,1)S(1)}, u32[]{:S(2)}, u32[]{:S(2)}) async-start(bf16[32,16,128]{2,1,0:T(8,128)(2,1)} %bitcast.7), calls=%async_computation.1 | async-start | bytes 262144 | tf_op jit(solution)/shard_map/all_to_all | solution.py:345
  24.4 0.3 collective-permute-start.4
  24.8 3.0 %collective-permute-start.5 = (bf16[32,256]{1,0:T(8,128)(2,1)}, bf16[32,256]{1,0:T(8,128)(2,1)S(1)}, u32[]{:S(2)}, u32[]{:S(2)}) collective-permute-start(bf16[32,256]{1,0:T(8,128)(2,1)} %get-tuple-element.50), channel_id=1, source_target_pairs={{0,2},{1,3},{2,0},{3,1},{4,8},{5,9},{6,10},{7,11},{8,4},{9,5},{10,... | collective-permute-start | bytes 49160 | tf_op jit(solution)/shard_map/ppermute | solution.py:31
  27.7 0.2 collective-permute-start.6
  27.9 1.2 %collective-permute-start.7 = (bf16[32,256]{1,0:T(8,128)(2,1)}, bf16[32,256]{1,0:T(8,128)(2,1)S(1)}, u32[]{:S(2)}, u32[]{:S(2)}) collective-permute-start(bf16[32,256]{1,0:T(8,128)(2,1)} %get-tuple-element.52), channel_id=1, source_target_pairs={{0,4},{1,5},{2,6},{3,7},{4,0},{5,1},{6,2},{7,3},{8,12},{9,13},{10,... | collective-permute-start | bytes 49160 | tf_op jit(solution)/shard_map/ppermute | solution.py:31
  29.0 0.3 local_kernel.1.local_ref
  29.3 0.0 collective-permute-done.4.refs_3_
  29.3 0.4 collective-permute-done.5.refs_4_
  29.7 2.1 %collective-permute-done.6.refs_5_ = bf16[32,256]{1,0:T(8,128)(2,1)S(1)} collective-permute-done((bf16[32,256]{1,0:T(8,128)(2,1)}, bf16[32,256]{1,0:T(8,128)(2,1)S(1)}, u32[]{:S(2)}, u32[]{:S(2)}) %collective-permute-start.6) | collective-permute-done | bytes 16416 | tf_op jit(solution)/shard_map/ppermute | solution.py:31
  31.8 0.0 collective-permute-done.7.refs_6_
  31.8 1.1 %all-to-all-done.1 = bf16[32,16,128]{2,1,0:T(8,128)(2,1)S(1)} async-done(((bf16[32,16,128]{2,1,0:T(8,128)(2,1)}), bf16[32,16,128]{2,1,0:T(8,128)(2,1)S(1)}, u32[]{:S(2)}, u32[]{:S(2)}) %all-to-all-start.1) | async-done | bytes 131104 | tf_op jit(solution)/shard_map/all_to_all | solution.py:345
  32.8 1.2 %second_kernel.1 = (f32[32,1,128]{2,1,0:T(1,128)S(1)}, f32[8,32,128]{2,1,0:T(8,128)S(1)}, f32[8,32,128]{2,1,0:T(8,128)S(1)}, f32[8,32,128]{2,1,0:T(8,128)S(1)}, f32[8,32,128]{2,1,0:T(8,128)S(1)}) custom-call(s32[8,6]{1,0:T(8,128)S(1)} %get-tuple-element.35.cols_ref, bf16[512,128]{1,0:T(8,128)(2,1)S(1)} %bitcast.5, ...), custom_call_target="tpu_custom_call" | custom-call | tf_op jit(solution)/shard_map/second_kernel/pallas_call | solution.py:327
  34.1 9.2 %all_to_all.15.arrived_ref = f32[32,1,128]{2,1,0:T(1,128)S(1)} all-to-all(f32[32,1,128]{2,1,0:T(1,128)S(1)} %get-tuple-element.53), channel_id=1, replica_groups=mesh['sx'=8,'sy'=4] {'sx','sy'}, dimensions={0} | all-to-all | bytes 32768 | tf_op jit(solution)/shard_map/all_to_all | solution.py:345
  43.3 0.8 %last_kernel.1 = (f32[8,32,128]{2,1,0:T(8,128)}, f32[8,32,128]{2,1,0:T(8,128)}) custom-call(f32[32,1,128]{2,1,0:T(1,128)S(1)} %all_to_all.15.arrived_ref, f32[8,32,128]{2,1,0:T(8,128)S(1)} %get-tuple-element.54.scaled_ref, f32[8,32,128]{2,1,0:T(8,128)S(1)} %get-tuple-element.55.second_ref, f32[8,32,128]{2,1,0:T(8,128)S(1)} %get-tuple-element.56.residual_ref, ...), custom_call_target="tpu_custom_call" | custom-call | tf_op jit(solution)/shard_map/last_kernel/pallas_call | solution.py:327
Async XLA Ops:
  3.1 11.2 %collective-permute-start = (bf16[32,1536]{1,0:T(8,128)(2,1)}, bf16[32,1536]{1,0:T(8,128)(2,1)S(1)}, u32[]{:S(2)}, u32[]{:S(2)}) collective-permute-start(bf16[32,1536]{1,0:T(8,128)(2,1)} %get-tuple-element.34), channel_id=1, source_target_pairs={{0,4},{1,2},{2,1},{3,7},{4,0},{5,6},{6,5},{7,3},{8,12},{9,10},{10,... | collective-permute-start | bytes 294920 | tf_op jit(solution)/shard_map/ppermute | solution.py:31
  3.6 14.9 %all-to-all-start = ((bf16[32,8,128]{2,1,0:T(8,128)(2,1)}), bf16[32,8,128]{2,1,0:T(8,128)(2,1)S(1)}, u32[]{:S(2)}, u32[]{:S(2)}) async-start(bf16[32,8,128]{2,1,0:T(8,128)(2,1)} %bitcast.8), calls=%async_computation | async-start | bytes 131072 | tf_op jit(solution)/shard_map/all_to_all | solution.py:345
  11.0 5.1 %collective-permute-start.1 = (bf16[32,1536]{1,0:T(8,128)(2,1)}, bf16[32,1536]{1,0:T(8,128)(2,1)S(1)}, u32[]{:S(2)}, u32[]{:S(2)}) collective-permute-start(bf16[32,1536]{1,0:T(8,128)(2,1)} %get-tuple-element.43), channel_id=1, source_target_pairs={{0,2},{1,3},{2,0},{3,1},{4,8},{5,9},{6,10},{7,11},{8,4},{9,5},{10,... | collective-permute-start | bytes 294920 | tf_op jit(solution)/shard_map/ppermute | solution.py:31
  12.8 5.4 %collective-permute-start.2 = (bf16[32,1536]{1,0:T(8,128)(2,1)}, bf16[32,1536]{1,0:T(8,128)(2,1)S(1)}, u32[]{:S(2)}, u32[]{:S(2)}) collective-permute-start(bf16[32,1536]{1,0:T(8,128)(2,1)} %get-tuple-element.44), channel_id=1, source_target_pairs={{0,1},{1,0},{2,3},{3,2},{4,5},{5,4},{6,7},{7,6},{8,9},{9,8},{10,11... | collective-permute-start | bytes 294920 | tf_op jit(solution)/shard_map/ppermute | solution.py:31
  14.3 3.9 %collective-permute-start.3 = (bf16[32,1536]{1,0:T(8,128)(2,1)}, bf16[32,1536]{1,0:T(8,128)(2,1)S(1)}, u32[]{:S(2)}, u32[]{:S(2)}) collective-permute-start(bf16[32,1536]{1,0:T(8,128)(2,1)} %get-tuple-element.45), channel_id=1, source_target_pairs={{0,4},{1,5},{2,6},{3,7},{4,0},{5,1},{6,2},{7,3},{8,12},{9,13},{10,... | collective-permute-start | bytes 294920 | tf_op jit(solution)/shard_map/ppermute | solution.py:31
  20.7 12.1 %all-to-all-start.1 = ((bf16[32,16,128]{2,1,0:T(8,128)(2,1)}), bf16[32,16,128]{2,1,0:T(8,128)(2,1)S(1)}, u32[]{:S(2)}, u32[]{:S(2)}) async-start(bf16[32,16,128]{2,1,0:T(8,128)(2,1)} %bitcast.7), calls=%async_computation.1 | async-start | bytes 262144 | tf_op jit(solution)/shard_map/all_to_all | solution.py:345
  24.4 4.9 %collective-permute-start.4 = (bf16[32,256]{1,0:T(8,128)(2,1)}, bf16[32,256]{1,0:T(8,128)(2,1)S(1)}, u32[]{:S(2)}, u32[]{:S(2)}) collective-permute-start(bf16[32,256]{1,0:T(8,128)(2,1)} %get-tuple-element.49), channel_id=1, source_target_pairs={{0,4},{1,2},{2,1},{3,7},{4,0},{5,6},{6,5},{7,3},{8,12},{9,10},{10,... | collective-permute-start | bytes 49160 | tf_op jit(solution)/shard_map/ppermute | solution.py:31
  24.8 4.9 %collective-permute-start.5 = (bf16[32,256]{1,0:T(8,128)(2,1)}, bf16[32,256]{1,0:T(8,128)(2,1)S(1)}, u32[]{:S(2)}, u32[]{:S(2)}) collective-permute-start(bf16[32,256]{1,0:T(8,128)(2,1)} %get-tuple-element.50), channel_id=1, source_target_pairs={{0,2},{1,3},{2,0},{3,1},{4,8},{5,9},{6,10},{7,11},{8,4},{9,5},{10,... | collective-permute-start | bytes 49160 | tf_op jit(solution)/shard_map/ppermute | solution.py:31
  27.7 4.0 %collective-permute-start.6 = (bf16[32,256]{1,0:T(8,128)(2,1)}, bf16[32,256]{1,0:T(8,128)(2,1)S(1)}, u32[]{:S(2)}, u32[]{:S(2)}) collective-permute-start(bf16[32,256]{1,0:T(8,128)(2,1)} %get-tuple-element.51), channel_id=1, source_target_pairs={{0,1},{1,0},{2,3},{3,2},{4,5},{5,4},{6,7},{7,6},{8,9},{9,8},{10,11... | collective-permute-start | bytes 49160 | tf_op jit(solution)/shard_map/ppermute | solution.py:31
  27.9 3.9 %collective-permute-start.7 = (bf16[32,256]{1,0:T(8,128)(2,1)}, bf16[32,256]{1,0:T(8,128)(2,1)S(1)}, u32[]{:S(2)}, u32[]{:S(2)}) collective-permute-start(bf16[32,256]{1,0:T(8,128)(2,1)} %get-tuple-element.52), channel_id=1, source_target_pairs={{0,4},{1,5},{2,6},{3,7},{4,0},{5,1},{6,2},{7,3},{8,12},{9,13},{10,... | collective-permute-start | bytes 49160 | tf_op jit(solution)/shard_map/ppermute | solution.py:31

commit v8 on v7

--- a/solution.py
+++ b/solution.py
@@ -46,10 +46,10 @@
     return high, (value - high.astype(F32)).astype(BF)
 
 
-def restrict_slot(vectors, basis_ref):
+def restrict_slot(vectors, basis_ref, parts=2):
     left, right = [], []
     for b, vector in enumerate(vectors):
-        for part in split(vector):
+        for part in split(vector)[:parts]:
             left.append(basis_ref[b])
             right.append(jnp.concatenate([part] * 4, axis=0))
     full = lax.dot_general(
@@ -140,7 +140,7 @@
     for copy in copies[:2]:
         copy.wait()
     vectors = [right_ref[b] for b in range(blocks)]
-    slot_ref[...] = repeated(restrict_slot(vectors, basis_ref), slot_ref.shape)
+    slot_ref[...] = repeated(restrict_slot(vectors, basis_ref, 1), slot_ref.shape)
     leaving = fetch([(slot_ref, slot_hbm)], out_sems)
     copies[3].wait()
     inverse = wide[...].astype(BF)

time: 44.4 us -> 44.2 us (level)
  no operation moved by 1% of the time
where the time goes in v8:
time: 44.2 us; the launch traced here: 43.9 us
  starting transfers between devices  19.5 us (44%)
  blocking collectives  9.2 us (21%)
  Pallas kernels  8.56 us (19%)
  waiting for transfers between devices  5.98 us (14%)
  between operations  0.69 us (2%)
    all_to_all x2, starting transfers between devices, exchange(): return lax.all_to_all(split_up, AXES, 0, 0, tiled=True).reshape(slots.shape)  11.1 us
    all_to_all x1, blocking collectives, exchange(): return lax.all_to_all(split_up, AXES, 0, 0, tiled=True).reshape(slots.shape)  9.2 us
    pallas_call x6, Pallas kernels, call(): pl.pallas_call(kernel, out_shape=[pltpu.HBM(shape, dtype) if p == 'h' els...  8.56 us
    ppermute x8, starting transfers between devices, swap(): return lax.ppermute(value, AXES, pairs)  8.42 us
    ppermute x8, waiting for transfers between devices, swap(): return lax.ppermute(value, AXES, pairs)  4.6 us
    all_to_all x2, waiting for transfers between devices, exchange(): return lax.all_to_all(split_up, AXES, 0, 0, tiled=True).reshape(slots.shape)  1.37 us
  transfers between devices with their start and end apart: 10, of which 5 were waited for; matrix products, arithmetic and copies ran while one was open for 0% of the time, Pallas kernels for 5%

profile of v8, /device:TPU:0, one launch (start us, length us, event | category | flops | bytes accessed | tf_op | source)
XLA Modules:
  0.0 43.9 jit_solution(2192910019099694341)
XLA Ops:
  0.6 2.3 %start_kernel.1 = (bf16[256,128]{1,0:T(8,128)(2,1)}, f32[8,32,128]{2,1,0:T(8,128)S(1)}, bf16[8,128,128]{2,1,0:T(8,128)(2,1)S(1)}, bf16[8,32,128]{2,1,0:T(8,128)(...) custom-call(s32[2,4]{1,0:T(2,128)} %bitcast.9, ...), custom_call_target="tpu_custom_call" | custom-call | tf_op jit(solution)/shard_map/start_kernel/pallas_call | solution.py:327
  2.9 0.5 %collective-permute-start = (bf16[32,1536]{1,0:T(8,128)(2,1)}, bf16[32,1536]{1,0:T(8,128)(2,1)S(1)}, u32[]{:S(2)}, u32[]{:S(2)}) collective-permute-start(bf16[32,1536]{1,0:T(8,128)(2,1)} %get-tuple-element.34), channel_id=1, source_target_pairs={{0,4},{1,2},{2,1},{3,7},{4,0},{5,6},{6,5},{7,3},{8,12},{9,10},{10,... | collective-permute-start | bytes 294920 | tf_op jit(solution)/shard_map/ppermute | solution.py:31
  3.4 7.4 %all-to-all-start = ((bf16[32,8,128]{2,1,0:T(8,128)(2,1)}), bf16[32,8,128]{2,1,0:T(8,128)(2,1)S(1)}, u32[]{:S(2)}, u32[]{:S(2)}) async-start(bf16[32,8,128]{2,1,0:T(8,128)(2,1)} %bitcast.8), calls=%async_computation | async-start | bytes 131072 | tf_op jit(solution)/shard_map/all_to_all | solution.py:345
  10.8 1.8 %collective-permute-start.1 = (bf16[32,1536]{1,0:T(8,128)(2,1)}, bf16[32,1536]{1,0:T(8,128)(2,1)S(1)}, u32[]{:S(2)}, u32[]{:S(2)}) collective-permute-start(bf16[32,1536]{1,0:T(8,128)(2,1)} %get-tuple-element.43), channel_id=1, source_target_pairs={{0,2},{1,3},{2,0},{3,1},{4,8},{5,9},{6,10},{7,11},{8,4},{9,5},{10,... | collective-permute-start | bytes 294920 | tf_op jit(solution)/shard_map/ppermute | solution.py:31
  12.6 1.5 %collective-permute-start.2 = (bf16[32,1536]{1,0:T(8,128)(2,1)}, bf16[32,1536]{1,0:T(8,128)(2,1)S(1)}, u32[]{:S(2)}, u32[]{:S(2)}) collective-permute-start(bf16[32,1536]{1,0:T(8,128)(2,1)} %get-tuple-element.44), channel_id=1, source_target_pairs={{0,1},{1,0},{2,3},{3,2},{4,5},{5,4},{6,7},{7,6},{8,9},{9,8},{10,11... | collective-permute-start | bytes 294920 | tf_op jit(solution)/shard_map/ppermute | solution.py:31
  14.1 0.0 collective-permute-start.3
  14.1 0.0 collective-permute-done.refs_0_
  14.1 1.8 %gather_kernel.1 = (bf16[64,1024]{1,0:T(8,128)(2,1)S(1)}, bf16[10,32,128]{2,1,0:T(8,128)(2,1)S(1)}, bf16[2,32,128]{2,1,0:T(8,128)(2,1)S(1)}, bf16[8,7,128,128]{3...) custom-call(bf16[32,1024]{1,0:T(8,128)(2,1)S(1)} %get-tuple-element.30.inverse_ref, ...), custom_call_target="tpu_custom_call" | custom-call | flops 99999997952 | tf_op jit(solution)/shard_map/gather_kernel/pallas_call | solution.py:327
  15.9 0.0 collective-permute-done.1.refs_0_
  15.9 2.1 %collective-permute-done.2.refs_1_ = bf16[32,1536]{1,0:T(8,128)(2,1)S(1)} collective-permute-done((bf16[32,1536]{1,0:T(8,128)(2,1)}, bf16[32,1536]{1,0:T(8,128)(2,1)S(1)}, u32[]{:S(2)}, u32[]{:S(2)}) %collective-permute-start.2) | collective-permute-done | bytes 98336 | tf_op jit(solution)/shard_map/ppermute | solution.py:31
  18.0 0.0 collective-permute-done.3.refs_2_
  18.0 0.3 all-to-all-done
  18.3 2.2 %first_kernel.1 = (bf16[512,128]{1,0:T(8,128)(2,1)}, f32[16,32,128]{2,1,0:T(8,128)S(1)}, f32[8,32,128]{2,1,0:T(8,128)S(1)}, bf16[32,256]{1,0:T(8,128)(2,1)}, bf1...) custom-call(s32[8,6]{1,0:T(8,128)S(1)} %get-tuple-element.35.cols_ref, ...), custom_call_target="tpu_custom_call" | custom-call | tf_op jit(solution)/shard_map/first_kernel/pallas_call | solution.py:327
  20.5 3.7 %all-to-all-start.1 = ((bf16[32,16,128]{2,1,0:T(8,128)(2,1)}), bf16[32,16,128]{2,1,0:T(8,128)(2,1)S(1)}, u32[]{:S(2)}, u32[]{:S(2)}) async-start(bf16[32,16,128]{2,1,0:T(8,128)(2,1)} %bitcast.7), calls=%async_computation.1 | async-start | bytes 262144 | tf_op jit(solution)/shard_map/all_to_all | solution.py:345
  24.2 0.3 collective-permute-start.4
  24.5 3.0 %collective-permute-start.5 = (bf16[32,256]{1,0:T(8,128)(2,1)}, bf16[32,256]{1,0:T(8,128)(2,1)S(1)}, u32[]{:S(2)}, u32[]{:S(2)}) collective-permute-start(bf16[32,256]{1,0:T(8,128)(2,1)} %get-tuple-element.50), channel_id=1, source_target_pairs={{0,2},{1,3},{2,0},{3,1},{4,8},{5,9},{6,10},{7,11},{8,4},{9,5},{10,... | collective-permute-start | bytes 49160 | tf_op jit(solution)/shard_map/ppermute | solution.py:31
  27.5 0.2 collective-permute-start.6
  27.7 1.2 %collective-permute-start.7 = (bf16[32,256]{1,0:T(8,128)(2,1)}, bf16[32,256]{1,0:T(8,128)(2,1)S(1)}, u32[]{:S(2)}, u32[]{:S(2)}) collective-permute-start(bf16[32,256]{1,0:T(8,128)(2,1)} %get-tuple-element.52), channel_id=1, source_target_pairs={{0,4},{1,5},{2,6},{3,7},{4,0},{5,1},{6,2},{7,3},{8,12},{9,13},{10,... | collective-permute-start | bytes 49160 | tf_op jit(solution)/shard_map/ppermute | solution.py:31
  28.8 0.3 local_kernel.1.local_ref
  29.1 0.0 collective-permute-done.4.refs_3_
  29.1 0.4 collective-permute-done.5.refs_4_
  29.5 2.1 %collective-permute-done.6.refs_5_ = bf16[32,256]{1,0:T(8,128)(2,1)S(1)} collective-permute-done((bf16[32,256]{1,0:T(8,128)(2,1)}, bf16[32,256]{1,0:T(8,128)(2,1)S(1)}, u32[]{:S(2)}, u32[]{:S(2)}) %collective-permute-start.6) | collective-permute-done | bytes 16416 | tf_op jit(solution)/shard_map/ppermute | solution.py:31
  31.6 0.0 collective-permute-done.7.refs_6_
  31.6 1.1 %all-to-all-done.1 = bf16[32,16,128]{2,1,0:T(8,128)(2,1)S(1)} async-done(((bf16[32,16,128]{2,1,0:T(8,128)(2,1)}), bf16[32,16,128]{2,1,0:T(8,128)(2,1)S(1)}, u32[]{:S(2)}, u32[]{:S(2)}) %all-to-all-start.1) | async-done | bytes 131104 | tf_op jit(solution)/shard_map/all_to_all | solution.py:345
  32.6 1.2 %second_kernel.1 = (f32[32,1,128]{2,1,0:T(1,128)S(1)}, f32[8,32,128]{2,1,0:T(8,128)S(1)}, f32[8,32,128]{2,1,0:T(8,128)S(1)}, f32[8,32,128]{2,1,0:T(8,128)S(1)}, f32[8,32,128]{2,1,0:T(8,128)S(1)}) custom-call(s32[8,6]{1,0:T(8,128)S(1)} %get-tuple-element.35.cols_ref, bf16[512,128]{1,0:T(8,128)(2,1)S(1)} %bitcast.5, ...), custom_call_target="tpu_custom_call" | custom-call | tf_op jit(solution)/shard_map/second_kernel/pallas_call | solution.py:327
  33.9 9.2 %all_to_all.15.arrived_ref = f32[32,1,128]{2,1,0:T(1,128)S(1)} all-to-all(f32[32,1,128]{2,1,0:T(1,128)S(1)} %get-tuple-element.53), channel_id=1, replica_groups=mesh['sx'=8,'sy'=4] {'sx','sy'}, dimensions={0} | all-to-all | bytes 32768 | tf_op jit(solution)/shard_map/all_to_all | solution.py:345
  43.1 0.8 %last_kernel.1 = (f32[8,32,128]{2,1,0:T(8,128)}, f32[8,32,128]{2,1,0:T(8,128)}) custom-call(f32[32,1,128]{2,1,0:T(1,128)S(1)} %all_to_all.15.arrived_ref, f32[8,32,128]{2,1,0:T(8,128)S(1)} %get-tuple-element.54.scaled_ref, f32[8,32,128]{2,1,0:T(8,128)S(1)} %get-tuple-element.55.second_ref, f32[8,32,128]{2,1,0:T(8,128)S(1)} %get-tuple-element.56.residual_ref, ...), custom_call_target="tpu_custom_call" | custom-call | tf_op jit(solution)/shard_map/last_kernel/pallas_call | solution.py:327
Async XLA Ops:
  2.9 11.2 %collective-permute-start = (bf16[32,1536]{1,0:T(8,128)(2,1)}, bf16[32,1536]{1,0:T(8,128)(2,1)S(1)}, u32[]{:S(2)}, u32[]{:S(2)}) collective-permute-start(bf16[32,1536]{1,0:T(8,128)(2,1)} %get-tuple-element.34), channel_id=1, source_target_pairs={{0,4},{1,2},{2,1},{3,7},{4,0},{5,6},{6,5},{7,3},{8,12},{9,10},{10,... | collective-permute-start | bytes 294920 | tf_op jit(solution)/shard_map/ppermute | solution.py:31
  3.4 14.9 %all-to-all-start = ((bf16[32,8,128]{2,1,0:T(8,128)(2,1)}), bf16[32,8,128]{2,1,0:T(8,128)(2,1)S(1)}, u32[]{:S(2)}, u32[]{:S(2)}) async-start(bf16[32,8,128]{2,1,0:T(8,128)(2,1)} %bitcast.8), calls=%async_computation | async-start | bytes 131072 | tf_op jit(solution)/shard_map/all_to_all | solution.py:345
  10.8 5.1 %collective-permute-start.1 = (bf16[32,1536]{1,0:T(8,128)(2,1)}, bf16[32,1536]{1,0:T(8,128)(2,1)S(1)}, u32[]{:S(2)}, u32[]{:S(2)}) collective-permute-start(bf16[32,1536]{1,0:T(8,128)(2,1)} %get-tuple-element.43), channel_id=1, source_target_pairs={{0,2},{1,3},{2,0},{3,1},{4,8},{5,9},{6,10},{7,11},{8,4},{9,5},{10,... | collective-permute-start | bytes 294920 | tf_op jit(solution)/shard_map/ppermute | solution.py:31
  12.6 5.4 %collective-permute-start.2 = (bf16[32,1536]{1,0:T(8,128)(2,1)}, bf16[32,1536]{1,0:T(8,128)(2,1)S(1)}, u32[]{:S(2)}, u32[]{:S(2)}) collective-permute-start(bf16[32,1536]{1,0:T(8,128)(2,1)} %get-tuple-element.44), channel_id=1, source_target_pairs={{0,1},{1,0},{2,3},{3,2},{4,5},{5,4},{6,7},{7,6},{8,9},{9,8},{10,11... | collective-permute-start | bytes 294920 | tf_op jit(solution)/shard_map/ppermute | solution.py:31
  14.1 3.9 %collective-permute-start.3 = (bf16[32,1536]{1,0:T(8,128)(2,1)}, bf16[32,1536]{1,0:T(8,128)(2,1)S(1)}, u32[]{:S(2)}, u32[]{:S(2)}) collective-permute-start(bf16[32,1536]{1,0:T(8,128)(2,1)} %get-tuple-element.45), channel_id=1, source_target_pairs={{0,4},{1,5},{2,6},{3,7},{4,0},{5,1},{6,2},{7,3},{8,12},{9,13},{10,... | collective-permute-start | bytes 294920 | tf_op jit(solution)/shard_map/ppermute | solution.py:31
  20.5 12.1 %all-to-all-start.1 = ((bf16[32,16,128]{2,1,0:T(8,128)(2,1)}), bf16[32,16,128]{2,1,0:T(8,128)(2,1)S(1)}, u32[]{:S(2)}, u32[]{:S(2)}) async-start(bf16[32,16,128]{2,1,0:T(8,128)(2,1)} %bitcast.7), calls=%async_computation.1 | async-start | bytes 262144 | tf_op jit(solution)/shard_map/all_to_all | solution.py:345
  24.2 4.9 %collective-permute-start.4 = (bf16[32,256]{1,0:T(8,128)(2,1)}, bf16[32,256]{1,0:T(8,128)(2,1)S(1)}, u32[]{:S(2)}, u32[]{:S(2)}) collective-permute-start(bf16[32,256]{1,0:T(8,128)(2,1)} %get-tuple-element.49), channel_id=1, source_target_pairs={{0,4},{1,2},{2,1},{3,7},{4,0},{5,6},{6,5},{7,3},{8,12},{9,10},{10,... | collective-permute-start | bytes 49160 | tf_op jit(solution)/shard_map/ppermute | solution.py:31
  24.5 4.9 %collective-permute-start.5 = (bf16[32,256]{1,0:T(8,128)(2,1)}, bf16[32,256]{1,0:T(8,128)(2,1)S(1)}, u32[]{:S(2)}, u32[]{:S(2)}) collective-permute-start(bf16[32,256]{1,0:T(8,128)(2,1)} %get-tuple-element.50), channel_id=1, source_target_pairs={{0,2},{1,3},{2,0},{3,1},{4,8},{5,9},{6,10},{7,11},{8,4},{9,5},{10,... | collective-permute-start | bytes 49160 | tf_op jit(solution)/shard_map/ppermute | solution.py:31
  27.5 4.0 %collective-permute-start.6 = (bf16[32,256]{1,0:T(8,128)(2,1)}, bf16[32,256]{1,0:T(8,128)(2,1)S(1)}, u32[]{:S(2)}, u32[]{:S(2)}) collective-permute-start(bf16[32,256]{1,0:T(8,128)(2,1)} %get-tuple-element.51), channel_id=1, source_target_pairs={{0,1},{1,0},{2,3},{3,2},{4,5},{5,4},{6,7},{7,6},{8,9},{9,8},{10,11... | collective-permute-start | bytes 49160 | tf_op jit(solution)/shard_map/ppermute | solution.py:31
  27.7 3.9 %collective-permute-start.7 = (bf16[32,256]{1,0:T(8,128)(2,1)}, bf16[32,256]{1,0:T(8,128)(2,1)S(1)}, u32[]{:S(2)}, u32[]{:S(2)}) collective-permute-start(bf16[32,256]{1,0:T(8,128)(2,1)} %get-tuple-element.52), channel_id=1, source_target_pairs={{0,4},{1,5},{2,6},{3,7},{4,0},{5,1},{6,2},{7,3},{8,12},{9,13},{10,... | collective-permute-start | bytes 49160 | tf_op jit(solution)/shard_map/ppermute | solution.py:31

commit v9 on v8

--- a/solution.py
+++ b/solution.py
@@ -206,6 +206,18 @@
         extended[blocks + halo * slot + m] = jnp.where(valid, value, 0.0).astype(BF)
 
 
+def spreads(coarse, bases, blocks, halo):
+    out, k = [], 0
+    while k < len(bases):
+        s = owner(k, blocks, halo)
+        pair = 2 if k + 1 < len(bases) and owner(k + 1, blocks, halo) == s else 1
+        order = bases[k].shape[1]
+        both = jnp.dot(coarse[s], jnp.concatenate(bases[k : k + pair], axis=1), preferred_element_type=F32)
+        out += [both[:, order * m : order * (m + 1)] for m in range(pair)]
+        k += pair
+    return out
+
+
 def owner(k, blocks, halo):
     return 0 if k < blocks else 1 + (k - blocks) // halo
 
@@ -224,8 +236,9 @@
     arrived = arrived_ref[...].astype(F32).reshape(-1, SLOT, LANES)
     coarse = coarse_parts(arrived, all_inverses(inverses_ref, late))
     early = blocks + halo * EARLY[0]
+    bases = [basis_block(k, bases_ref, late, total, halo) for k in range(update_ref.shape[0])]
+    spread = spreads(coarse, bases, blocks, halo)
     for k in range(update_ref.shape[0]):
-        basis = basis_block(k, bases_ref, late, total, halo)
         if k < blocks:
             local = local_ref[k]
         elif k < early:
@@ -234,7 +247,7 @@
             q, m = divmod(k - early, halo)
             at = total + (halo + m) * order
             local = late[q][:, at : at + order].astype(F32)
-        update = local + jnp.dot(coarse[owner(k, blocks, halo)], basis, preferred_element_type=F32)
+        update = local + spread[k]
         update_ref[k] = update
         pack(extended, k, update, blocks, halo)
     upper = lower = jnp.zeros((rhs, order), F32)
@@ -287,16 +300,16 @@
     sums = jnp.sum(arrived[:, SLOT : SLOT + 1], axis=0)
     turned = jnp.broadcast_to(sums, (LANES, LANES)).T
     weight = (turned[:32] + turned[64:96]) / (turned[32:64] + turned[96:] + 1e-6)
+    bases = [basis_block(k, bases_ref, late, total, halo) for k in range(update_ref.shape[0])]
+    spread = spreads(coarse, bases, blocks, halo)
     for k in range(update_ref.shape[0]):
-        basis = basis_block(k, bases_ref, late, total, halo)
         if k < local_ref.shape[0]:
             local = local_ref[k]
         else:
             q, m = divmod(k - local_ref.shape[0], halo)
             local = nexts[q][:, m * order : (m + 1) * order].astype(F32)
         update = update_ref[k]
-        spread = jnp.dot(coarse[owner(k, blocks, halo)], basis, preferred_element_type=F32)
-        second = update - weight * (local + spread)
+        second = update - weight * (local + spread[k])
         if k < blocks:
             scaled_ref[k] = weight * update
             second_ref[k] = second

time: 44.2 us -> 44.2 us (level)
  no operation moved by 1% of the time
where the time goes in v9:
time: 44.2 us; the launch traced here: 43.9 us
  starting transfers between devices  19.5 us (44%)
  blocking collectives  9.19 us (21%)
  Pallas kernels  8.55 us (19%)
  waiting for transfers between devices  5.98 us (14%)
  between operations  0.69 us (2%)
    all_to_all x2, starting transfers between devices, exchange(): return lax.all_to_all(split_up, AXES, 0, 0, tiled=True).reshape(slots.shape)  11.1 us
    all_to_all x1, blocking collectives, exchange(): return lax.all_to_all(split_up, AXES, 0, 0, tiled=True).reshape(slots.shape)  9.19 us
    pallas_call x6, Pallas kernels, call(): pl.pallas_call(kernel, out_shape=[pltpu.HBM(shape, dtype) if p == 'h' els...  8.55 us
    ppermute x8, starting transfers between devices, swap(): return lax.ppermute(value, AXES, pairs)  8.42 us
    ppermute x8, waiting for transfers between devices, swap(): return lax.ppermute(value, AXES, pairs)  4.6 us
    all_to_all x2, waiting for transfers between devices, exchange(): return lax.all_to_all(split_up, AXES, 0, 0, tiled=True).reshape(slots.shape)  1.37 us
  transfers between devices with their start and end apart: 10, of which 5 were waited for; matrix products, arithmetic and copies ran while one was open for 0% of the time, Pallas kernels for 5%

profile of v9, /device:TPU:0, one launch (start us, length us, event | category | flops | bytes accessed | tf_op | source)
XLA Modules:
  0.0 43.9 jit_solution(8330618164988134439)
XLA Ops:
  0.6 2.3 %start_kernel.1 = (bf16[256,128]{1,0:T(8,128)(2,1)}, f32[8,32,128]{2,1,0:T(8,128)S(1)}, bf16[8,128,128]{2,1,0:T(8,128)(2,1)S(1)}, bf16[8,32,128]{2,1,0:T(8,128)(...) custom-call(s32[2,4]{1,0:T(2,128)} %bitcast.9, ...), custom_call_target="tpu_custom_call" | custom-call | tf_op jit(solution)/shard_map/start_kernel/pallas_call | solution.py:340
  2.9 0.5 %collective-permute-start = (bf16[32,1536]{1,0:T(8,128)(2,1)}, bf16[32,1536]{1,0:T(8,128)(2,1)S(1)}, u32[]{:S(2)}, u32[]{:S(2)}) collective-permute-start(bf16[32,1536]{1,0:T(8,128)(2,1)} %get-tuple-element.34), channel_id=1, source_target_pairs={{0,4},{1,2},{2,1},{3,7},{4,0},{5,6},{6,5},{7,3},{8,12},{9,10},{10,... | collective-permute-start | bytes 294920 | tf_op jit(solution)/shard_map/ppermute | solution.py:31
  3.4 7.4 %all-to-all-start = ((bf16[32,8,128]{2,1,0:T(8,128)(2,1)}), bf16[32,8,128]{2,1,0:T(8,128)(2,1)S(1)}, u32[]{:S(2)}, u32[]{:S(2)}) async-start(bf16[32,8,128]{2,1,0:T(8,128)(2,1)} %bitcast.8), calls=%async_computation | async-start | bytes 131072 | tf_op jit(solution)/shard_map/all_to_all | solution.py:358
  10.8 1.8 %collective-permute-start.1 = (bf16[32,1536]{1,0:T(8,128)(2,1)}, bf16[32,1536]{1,0:T(8,128)(2,1)S(1)}, u32[]{:S(2)}, u32[]{:S(2)}) collective-permute-start(bf16[32,1536]{1,0:T(8,128)(2,1)} %get-tuple-element.43), channel_id=1, source_target_pairs={{0,2},{1,3},{2,0},{3,1},{4,8},{5,9},{6,10},{7,11},{8,4},{9,5},{10,... | collective-permute-start | bytes 294920 | tf_op jit(solution)/shard_map/ppermute | solution.py:31
  12.6 1.5 %collective-permute-start.2 = (bf16[32,1536]{1,0:T(8,128)(2,1)}, bf16[32,1536]{1,0:T(8,128)(2,1)S(1)}, u32[]{:S(2)}, u32[]{:S(2)}) collective-permute-start(bf16[32,1536]{1,0:T(8,128)(2,1)} %get-tuple-element.44), channel_id=1, source_target_pairs={{0,1},{1,0},{2,3},{3,2},{4,5},{5,4},{6,7},{7,6},{8,9},{9,8},{10,11... | collective-permute-start | bytes 294920 | tf_op jit(solution)/shard_map/ppermute | solution.py:31
  14.1 0.0 collective-permute-start.3
  14.1 0.0 collective-permute-done.refs_0_
  14.1 1.8 %gather_kernel.1 = (bf16[64,1024]{1,0:T(8,128)(2,1)S(1)}, bf16[10,32,128]{2,1,0:T(8,128)(2,1)S(1)}, bf16[2,32,128]{2,1,0:T(8,128)(2,1)S(1)}, bf16[8,7,128,128]{3...) custom-call(bf16[32,1024]{1,0:T(8,128)(2,1)S(1)} %get-tuple-element.30.inverse_ref, ...), custom_call_target="tpu_custom_call" | custom-call | flops 99999997952 | tf_op jit(solution)/shard_map/gather_kernel/pallas_call | solution.py:340
  15.9 0.0 collective-permute-done.1.refs_0_
  15.9 2.1 %collective-permute-done.2.refs_1_ = bf16[32,1536]{1,0:T(8,128)(2,1)S(1)} collective-permute-done((bf16[32,1536]{1,0:T(8,128)(2,1)}, bf16[32,1536]{1,0:T(8,128)(2,1)S(1)}, u32[]{:S(2)}, u32[]{:S(2)}) %collective-permute-start.2) | collective-permute-done | bytes 98336 | tf_op jit(solution)/shard_map/ppermute | solution.py:31
  18.0 0.0 collective-permute-done.3.refs_2_
  18.0 0.3 all-to-all-done
  18.3 2.2 %first_kernel.1 = (bf16[512,128]{1,0:T(8,128)(2,1)}, f32[16,32,128]{2,1,0:T(8,128)S(1)}, f32[8,32,128]{2,1,0:T(8,128)S(1)}, bf16[32,256]{1,0:T(8,128)(2,1)}, bf1...) custom-call(s32[8,6]{1,0:T(8,128)S(1)} %get-tuple-element.35.cols_ref, ...), custom_call_target="tpu_custom_call" | custom-call | tf_op jit(solution)/shard_map/first_kernel/pallas_call | solution.py:340
  20.5 3.7 %all-to-all-start.1 = ((bf16[32,16,128]{2,1,0:T(8,128)(2,1)}), bf16[32,16,128]{2,1,0:T(8,128)(2,1)S(1)}, u32[]{:S(2)}, u32[]{:S(2)}) async-start(bf16[32,16,128]{2,1,0:T(8,128)(2,1)} %bitcast.7), calls=%async_computation.1 | async-start | bytes 262144 | tf_op jit(solution)/shard_map/all_to_all | solution.py:358
  24.2 0.3 collective-permute-start.4
  24.5 3.0 %collective-permute-start.5 = (bf16[32,256]{1,0:T(8,128)(2,1)}, bf16[32,256]{1,0:T(8,128)(2,1)S(1)}, u32[]{:S(2)}, u32[]{:S(2)}) collective-permute-start(bf16[32,256]{1,0:T(8,128)(2,1)} %get-tuple-element.50), channel_id=1, source_target_pairs={{0,2},{1,3},{2,0},{3,1},{4,8},{5,9},{6,10},{7,11},{8,4},{9,5},{10,... | collective-permute-start | bytes 49160 | tf_op jit(solution)/shard_map/ppermute | solution.py:31
  27.5 0.2 collective-permute-start.6
  27.7 1.2 %collective-permute-start.7 = (bf16[32,256]{1,0:T(8,128)(2,1)}, bf16[32,256]{1,0:T(8,128)(2,1)S(1)}, u32[]{:S(2)}, u32[]{:S(2)}) collective-permute-start(bf16[32,256]{1,0:T(8,128)(2,1)} %get-tuple-element.52), channel_id=1, source_target_pairs={{0,4},{1,5},{2,6},{3,7},{4,0},{5,1},{6,2},{7,3},{8,12},{9,13},{10,... | collective-permute-start | bytes 49160 | tf_op jit(solution)/shard_map/ppermute | solution.py:31
  28.8 0.3 local_kernel.1.local_ref
  29.1 0.0 collective-permute-done.4.refs_3_
  29.1 0.4 collective-permute-done.5.refs_4_
  29.5 2.1 %collective-permute-done.6.refs_5_ = bf16[32,256]{1,0:T(8,128)(2,1)S(1)} collective-permute-done((bf16[32,256]{1,0:T(8,128)(2,1)}, bf16[32,256]{1,0:T(8,128)(2,1)S(1)}, u32[]{:S(2)}, u32[]{:S(2)}) %collective-permute-start.6) | collective-permute-done | bytes 16416 | tf_op jit(solution)/shard_map/ppermute | solution.py:31
  31.6 0.0 collective-permute-done.7.refs_6_
  31.6 1.1 %all-to-all-done.1 = bf16[32,16,128]{2,1,0:T(8,128)(2,1)S(1)} async-done(((bf16[32,16,128]{2,1,0:T(8,128)(2,1)}), bf16[32,16,128]{2,1,0:T(8,128)(2,1)S(1)}, u32[]{:S(2)}, u32[]{:S(2)}) %all-to-all-start.1) | async-done | bytes 131104 | tf_op jit(solution)/shard_map/all_to_all | solution.py:358
  32.6 1.2 %second_kernel.1 = (f32[32,1,128]{2,1,0:T(1,128)S(1)}, f32[8,32,128]{2,1,0:T(8,128)S(1)}, f32[8,32,128]{2,1,0:T(8,128)S(1)}, f32[8,32,128]{2,1,0:T(8,128)S(1)}, f32[8,32,128]{2,1,0:T(8,128)S(1)}) custom-call(s32[8,6]{1,0:T(8,128)S(1)} %get-tuple-element.35.cols_ref, bf16[512,128]{1,0:T(8,128)(2,1)S(1)} %bitcast.5, ...), custom_call_target="tpu_custom_call" | custom-call | tf_op jit(solution)/shard_map/second_kernel/pallas_call | solution.py:340
  33.9 9.2 %all_to_all.15.arrived_ref = f32[32,1,128]{2,1,0:T(1,128)S(1)} all-to-all(f32[32,1,128]{2,1,0:T(1,128)S(1)} %get-tuple-element.53), channel_id=1, replica_groups=mesh['sx'=8,'sy'=4] {'sx','sy'}, dimensions={0} | all-to-all | bytes 32768 | tf_op jit(solution)/shard_map/all_to_all | solution.py:358
  43.1 0.8 %last_kernel.1 = (f32[8,32,128]{2,1,0:T(8,128)}, f32[8,32,128]{2,1,0:T(8,128)}) custom-call(f32[32,1,128]{2,1,0:T(1,128)S(1)} %all_to_all.15.arrived_ref, f32[8,32,128]{2,1,0:T(8,128)S(1)} %get-tuple-element.54.scaled_ref, f32[8,32,128]{2,1,0:T(8,128)S(1)} %get-tuple-element.55.second_ref, f32[8,32,128]{2,1,0:T(8,128)S(1)} %get-tuple-element.56.residual_ref, ...), custom_call_target="tpu_custom_call" | custom-call | tf_op jit(solution)/shard_map/last_kernel/pallas_call | solution.py:340
Async XLA Ops:
  2.9 11.2 %collective-permute-start = (bf16[32,1536]{1,0:T(8,128)(2,1)}, bf16[32,1536]{1,0:T(8,128)(2,1)S(1)}, u32[]{:S(2)}, u32[]{:S(2)}) collective-permute-start(bf16[32,1536]{1,0:T(8,128)(2,1)} %get-tuple-element.34), channel_id=1, source_target_pairs={{0,4},{1,2},{2,1},{3,7},{4,0},{5,6},{6,5},{7,3},{8,12},{9,10},{10,... | collective-permute-start | bytes 294920 | tf_op jit(solution)/shard_map/ppermute | solution.py:31
  3.4 14.9 %all-to-all-start = ((bf16[32,8,128]{2,1,0:T(8,128)(2,1)}), bf16[32,8,128]{2,1,0:T(8,128)(2,1)S(1)}, u32[]{:S(2)}, u32[]{:S(2)}) async-start(bf16[32,8,128]{2,1,0:T(8,128)(2,1)} %bitcast.8), calls=%async_computation | async-start | bytes 131072 | tf_op jit(solution)/shard_map/all_to_all | solution.py:358
  10.8 5.1 %collective-permute-start.1 = (bf16[32,1536]{1,0:T(8,128)(2,1)}, bf16[32,1536]{1,0:T(8,128)(2,1)S(1)}, u32[]{:S(2)}, u32[]{:S(2)}) collective-permute-start(bf16[32,1536]{1,0:T(8,128)(2,1)} %get-tuple-element.43), channel_id=1, source_target_pairs={{0,2},{1,3},{2,0},{3,1},{4,8},{5,9},{6,10},{7,11},{8,4},{9,5},{10,... | collective-permute-start | bytes 294920 | tf_op jit(solution)/shard_map/ppermute | solution.py:31
  12.6 5.4 %collective-permute-start.2 = (bf16[32,1536]{1,0:T(8,128)(2,1)}, bf16[32,1536]{1,0:T(8,128)(2,1)S(1)}, u32[]{:S(2)}, u32[]{:S(2)}) collective-permute-start(bf16[32,1536]{1,0:T(8,128)(2,1)} %get-tuple-element.44), channel_id=1, source_target_pairs={{0,1},{1,0},{2,3},{3,2},{4,5},{5,4},{6,7},{7,6},{8,9},{9,8},{10,11... | collective-permute-start | bytes 294920 | tf_op jit(solution)/shard_map/ppermute | solution.py:31
  14.1 3.9 %collective-permute-start.3 = (bf16[32,1536]{1,0:T(8,128)(2,1)}, bf16[32,1536]{1,0:T(8,128)(2,1)S(1)}, u32[]{:S(2)}, u32[]{:S(2)}) collective-permute-start(bf16[32,1536]{1,0:T(8,128)(2,1)} %get-tuple-element.45), channel_id=1, source_target_pairs={{0,4},{1,5},{2,6},{3,7},{4,0},{5,1},{6,2},{7,3},{8,12},{9,13},{10,... | collective-permute-start | bytes 294920 | tf_op jit(solution)/shard_map/ppermute | solution.py:31
  20.5 12.1 %all-to-all-start.1 = ((bf16[32,16,128]{2,1,0:T(8,128)(2,1)}), bf16[32,16,128]{2,1,0:T(8,128)(2,1)S(1)}, u32[]{:S(2)}, u32[]{:S(2)}) async-start(bf16[32,16,128]{2,1,0:T(8,128)(2,1)} %bitcast.7), calls=%async_computation.1 | async-start | bytes 262144 | tf_op jit(solution)/shard_map/all_to_all | solution.py:358
  24.2 4.9 %collective-permute-start.4 = (bf16[32,256]{1,0:T(8,128)(2,1)}, bf16[32,256]{1,0:T(8,128)(2,1)S(1)}, u32[]{:S(2)}, u32[]{:S(2)}) collective-permute-start(bf16[32,256]{1,0:T(8,128)(2,1)} %get-tuple-element.49), channel_id=1, source_target_pairs={{0,4},{1,2},{2,1},{3,7},{4,0},{5,6},{6,5},{7,3},{8,12},{9,10},{10,... | collective-permute-start | bytes 49160 | tf_op jit(solution)/shard_map/ppermute | solution.py:31
  24.5 4.9 %collective-permute-start.5 = (bf16[32,256]{1,0:T(8,128)(2,1)}, bf16[32,256]{1,0:T(8,128)(2,1)S(1)}, u32[]{:S(2)}, u32[]{:S(2)}) collective-permute-start(bf16[32,256]{1,0:T(8,128)(2,1)} %get-tuple-element.50), channel_id=1, source_target_pairs={{0,2},{1,3},{2,0},{3,1},{4,8},{5,9},{6,10},{7,11},{8,4},{9,5},{10,... | collective-permute-start | bytes 49160 | tf_op jit(solution)/shard_map/ppermute | solution.py:31
  27.5 4.0 %collective-permute-start.6 = (bf16[32,256]{1,0:T(8,128)(2,1)}, bf16[32,256]{1,0:T(8,128)(2,1)S(1)}, u32[]{:S(2)}, u32[]{:S(2)}) collective-permute-start(bf16[32,256]{1,0:T(8,128)(2,1)} %get-tuple-element.51), channel_id=1, source_target_pairs={{0,1},{1,0},{2,3},{3,2},{4,5},{5,4},{6,7},{7,6},{8,9},{9,8},{10,11... | collective-permute-start | bytes 49160 | tf_op jit(solution)/shard_map/ppermute | solution.py:31
  27.7 3.9 %collective-permute-start.7 = (bf16[32,256]{1,0:T(8,128)(2,1)}, bf16[32,256]{1,0:T(8,128)(2,1)S(1)}, u32[]{:S(2)}, u32[]{:S(2)}) collective-permute-start(bf16[32,256]{1,0:T(8,128)(2,1)} %get-tuple-element.52), channel_id=1, source_target_pairs={{0,4},{1,5},{2,6},{3,7},{4,0},{5,1},{6,2},{7,3},{8,12},{9,13},{10,... | collective-permute-start | bytes 49160 | tf_op jit(solution)/shard_map/ppermute | solution.py:31
